TPU v7x, 32 devices: a whole 2x2x4 slice. The times are simulated.
32 devices in a mesh: dp: 4 (over y, core), ctx: 8 (over z, x).
Axes of the slice: x: 2, y: 2, z: 4, core: 2. Of those that a mesh axis runs over, the one named last changes fastest.
Arguments:
- tokens: bfloat16 [4, 1024, 2048], P('dp', 'ctx'), may hold values from -6 to 6
- document_ids: int32 [4, 1024], P('dp'), may hold values from 0 to 6, as said below
- routes: int32 [4, 1024, 8], P('dp', 'ctx'), may hold values from 0 to 15, all different within a row; in each aligned block of 128 rows (0 to 127, 128 to 255, ..., all dimensions but the last counted through in order) at most 128 rows name the same one
- norm_gains: bfloat16 [2048, 4], P(('dp', 'ctx')), may hold values from 0.5 to 1.5
- project_in: bfloat16 [2048, 6144], P(('dp', 'ctx')), may hold values from -0.125 to 0.125
- project_out: bfloat16 [2048, 2048], P(('dp', 'ctx')), may hold values from -1 to 1
- router_weight: bfloat16 [2048, 16], P(('dp', 'ctx')), may hold values from -0.0625 to 0.0625
- expert_in: bfloat16 [16, 2048, 2048], P('ctx', 'dp'), may hold values from -0.125 to 0.125
- expert_out: bfloat16 [16, 1024, 2048], P('ctx', 'dp'), may hold values from -0.5 to 0.5
- cotangent: bfloat16 [4, 1024, 2048], P('dp', 'ctx'), may hold values from -6 to 6
Outputs:
- layer_output: bfloat16 [4, 1024, 2048], P('dp', 'ctx')
- tokens_gradient: bfloat16 [4, 1024, 2048], P('dp', 'ctx')
- gains_gradient: float32 [2048, 4], P(('dp', 'ctx'))
- project_in_gradient: float32 [2048, 6144], P(('dp', 'ctx'))
- project_out_gradient: float32 [2048, 2048], P(('dp', 'ctx'))
- router_gradient: float32 [2048, 16], P(('dp', 'ctx'))
- expert_in_gradient: float32 [16, 2048, 2048], P('ctx', 'dp')
- expert_out_gradient: float32 [16, 1024, 2048], P('ctx', 'dp')
Inputs may be any that keep to these rules, and one draw needn't show every extreme that they name: `document_ids`: each stream's ids start at 0 and rise by one where a document starts; ids never fall along a stream. Every stream holds exactly 7 documents, and one of them covers at least positions 64 to 511. `routes`: each row names 8 different experts. In the rows of one device no expert is named by more than 128 rows.
All inputs are finite; a program needn't handle non-finite values.
Results may differ from a plain program's by a relative error of at most 0.015.
Values may be sent and summed in bfloat16 or wider, within the bound.
A program may use at most 320 MiB of HBM per device.

v0:
```python
import jax
import jax.numpy as jnp
from jax import lax
from jax.sharding import PartitionSpec as P

HEADS = 16
HEAD_DIM = 128
FF = 1024


EPSILON = 1e-05
ROPE_BASE = 10000.0
MASKED = -1e30


def inverse_rms(values):
    return lax.rsqrt(jnp.mean(values * values, axis=-1, keepdims=True) + EPSILON)


def normalize_back(normed_back, normed, inverse):
    return inverse * (normed_back - normed * jnp.mean(normed_back * normed, axis=-1, keepdims=True))


def rotary_tables(relative, head_dim):
    half_dim = head_dim // 2
    frequency = ROPE_BASE ** (-jnp.arange(half_dim, dtype=jnp.float32) / half_dim)
    angles = relative.astype(jnp.float32)[..., None] * frequency
    return (jnp.cos(angles)[..., None, :], jnp.sin(angles)[..., None, :])


def rotate(values, cosine, sine_table):
    half_dim = values.shape[-1] // 2
    first_half = values[..., :half_dim]
    second_half = values[..., half_dim:]
    return jnp.concatenate(
        [
            first_half * cosine - second_half * sine_table,
            second_half * cosine + first_half * sine_table,
        ],
        axis=-1,
    )


def dealt_positions(indices, tok_rows, context_size):
    half_block = tok_rows // 2
    device = indices // tok_rows
    within = indices % tok_rows
    block_index = jnp.where(within < half_block, device, 2 * context_size - 1 - device)
    return block_index * half_block + within % half_block


def document_starts(document_row):
    places = jnp.arange(document_row.shape[-1], dtype=jnp.int32)
    head_flag = jnp.ones(document_row.shape[:-1] + (1,), jnp.bool_)
    fresh_start = jnp.concatenate(
        [head_flag, document_row[..., 1:] != document_row[..., :-1]], axis=-1
    )
    return lax.cummax(jnp.where(fresh_start, places, 0), axis=document_row.ndim - 1)


def block_scores(
    query_rows, key_block, query_place, query_document, key_place, key_document, score_scale
):
    scores = (
        jnp.einsum("thd,khd->htk", query_rows, key_block, preferred_element_type=jnp.float32)
        * score_scale
    )
    visible = (
        (key_document[None, :] == query_document[:, None])
        & (key_place[None, :] <= query_place[:, None])
    )[None]
    return (jnp.where(visible, scores, MASKED), visible)


def block_backward(
    query_rows,
    output_back,
    row_logsum,
    row_delta,
    key_block,
    value_block,
    query_place,
    query_document,
    key_place,
    key_document,
    score_scale,
):
    scores, visible = block_scores(
        query_rows, key_block, query_place, query_document, key_place, key_document, score_scale
    )
    prob_rows = jnp.where(visible, jnp.exp(scores - row_logsum[..., None]), 0.0)
    prob_back = jnp.einsum(
        "thd,khd->htk", output_back, value_block, preferred_element_type=jnp.float32
    )
    score_back = (prob_rows * (prob_back - row_delta[..., None])).astype(jnp.bfloat16)
    query_part = (
        jnp.einsum("htk,khd->thd", score_back, key_block, preferred_element_type=jnp.float32)
        * score_scale
    )
    key_part = (
        jnp.einsum("htk,thd->khd", score_back, query_rows, preferred_element_type=jnp.float32)
        * score_scale
    )
    value_part = jnp.einsum(
        "htk,thd->khd",
        prob_rows.astype(jnp.bfloat16),
        output_back,
        preferred_element_type=jnp.float32,
    )
    return (query_part, key_part, value_part)


def dispatch_plan(route_rows, expert_count, capacity):
    flat_routes = route_rows.reshape(-1)
    pair_count = flat_routes.shape[0]
    member = (flat_routes[:, None] == jnp.arange(expert_count, dtype=jnp.int32)[None, :]).astype(
        jnp.int32
    )
    earlier = jnp.cumsum(member, axis=0) - member
    target_slot = flat_routes * capacity + jnp.sum(earlier * member, axis=1)
    slot_owner = (
        jnp.full((expert_count * capacity,), pair_count, jnp.int32)
        .at[target_slot]
        .set(jnp.arange(pair_count, dtype=jnp.int32))
    )
    return (target_slot, slot_owner)


def local(
    tokens,
    document_ids,
    routes,
    norm_gains,
    project_in,
    project_out,
    router_weight,
    expert_in,
    expert_out,
    cotangent,
):
    inputs = tokens[0].astype(jnp.float32)
    tok_rows, model_width = inputs.shape
    context_size = lax.axis_size("ctx")
    sequence_rows = tok_rows * context_size
    local_experts = expert_in.shape[0]
    expert_count = local_experts * context_size
    route_rows = routes[0]
    top_count = route_rows.shape[1]
    capacity = 2 * tok_rows * top_count // expert_count
    score_scale = HEAD_DIM ** (-0.5)
    key_span = min(512, sequence_rows)
    key_blocks = sequence_rows // key_span
    heads_shape = (tok_rows, HEADS, HEAD_DIM)
    block_shape = (key_blocks, key_span, HEADS, HEAD_DIM)
    slot_shape = (context_size, local_experts * capacity, model_width)
    expert_shape = (context_size, local_experts, capacity, model_width)
    gathered_gains, gathered_in, gathered_out, gathered_router = (
        lax.all_gather(norm_gains, ("dp", "ctx"), axis=0, tiled=True),
        lax.all_gather(project_in, ("dp", "ctx"), axis=0, tiled=True),
        lax.all_gather(project_out, ("dp", "ctx"), axis=0, tiled=True),
        lax.all_gather(router_weight, ("dp", "ctx"), axis=0, tiled=True),
    )
    gathered_first, gathered_second = (
        lax.all_gather(expert_in, "dp", axis=1, tiled=True),
        lax.all_gather(expert_out, "dp", axis=1, tiled=True),
    )
    gain_rows = gathered_gains.astype(jnp.float32)
    own_rows = lax.axis_index("ctx") * tok_rows + jnp.arange(tok_rows, dtype=jnp.int32)
    own_place = dealt_positions(own_rows, tok_rows, context_size)
    all_place = dealt_positions(jnp.arange(sequence_rows, dtype=jnp.int32), tok_rows, context_size)
    document_row = document_ids[0]
    own_document = jnp.take(document_row, own_place)
    all_document = jnp.take(document_row, all_place)
    relative = own_place - jnp.take(document_starts(document_row), own_place)
    cosine, sine_table = rotary_tables(relative, HEAD_DIM)
    attend_inverse = inverse_rms(inputs)
    attend_normed = inputs * attend_inverse
    attend_in = (attend_normed * gain_rows[:, 0]).astype(jnp.bfloat16)
    projected = jnp.dot(attend_in, gathered_in, preferred_element_type=jnp.float32)
    raw_query = projected[:, :model_width]
    raw_key = projected[:, model_width : 2 * model_width]
    query_inverse = inverse_rms(raw_query)
    query_normed = raw_query * query_inverse
    key_inverse = inverse_rms(raw_key)
    key_normed = raw_key * key_inverse
    query_low = rotate(
        (query_normed * gain_rows[:, 1]).reshape(heads_shape), cosine, sine_table
    ).astype(jnp.bfloat16)
    key_low = rotate(
        (key_normed * gain_rows[:, 2]).reshape(heads_shape), cosine, sine_table
    ).astype(jnp.bfloat16)
    value_low = projected[:, 2 * model_width :].astype(jnp.bfloat16)
    key_all, value_all = (
        lax.all_gather(key_low.reshape(tok_rows, model_width), "ctx", axis=0, tiled=True),
        lax.all_gather(value_low, "ctx", axis=0, tiled=True),
    )
    key_split = key_all.reshape(block_shape)
    value_split = value_all.reshape(block_shape)
    place_split = all_place.reshape(key_blocks, key_span)
    document_split = all_document.reshape(key_blocks, key_span)

    def total_step(state_pair, block_args):
        row_peak, row_total = state_pair
        key_block, key_place, key_document = block_args
        scores, visible = block_scores(
            query_low, key_block, own_place, own_document, key_place, key_document, score_scale
        )
        new_peak = jnp.maximum(row_peak, jnp.max(scores, axis=-1))
        fresh_total = jnp.sum(
            jnp.where(visible, jnp.exp(scores - new_peak[..., None]), 0.0), axis=-1
        )
        return ((new_peak, row_total * jnp.exp(row_peak - new_peak) + fresh_total), None)

    start_pair = (
        jnp.full((HEADS, tok_rows), MASKED, jnp.float32),
        jnp.zeros((HEADS, tok_rows), jnp.float32),
    )
    (row_peak, row_total), unused = lax.scan(
        total_step, start_pair, (key_split, place_split, document_split)
    )
    row_logsum = row_peak + jnp.log(row_total)

    def value_step(running, block_args):
        key_block, value_block, key_place, key_document = block_args
        scores, visible = block_scores(
            query_low, key_block, own_place, own_document, key_place, key_document, score_scale
        )
        prob_low = jnp.where(visible, jnp.exp(scores - row_logsum[..., None]), 0.0).astype(
            jnp.bfloat16
        )
        return (
            running
            + jnp.einsum("htk,khd->thd", prob_low, value_block, preferred_element_type=jnp.float32),
            None,
        )

    attend_out, unused = lax.scan(
        value_step,
        jnp.zeros(heads_shape, jnp.float32),
        (key_split, value_split, place_split, document_split),
    )
    attend_low = attend_out.reshape(tok_rows, model_width).astype(jnp.bfloat16)
    residual = inputs + jnp.dot(attend_low, gathered_out, preferred_element_type=jnp.float32)
    mixed_inverse = inverse_rms(residual)
    mixed_normed = residual * mixed_inverse
    mixed_low = (mixed_normed * gain_rows[:, 3]).astype(jnp.bfloat16)
    logits = jnp.dot(mixed_low, gathered_router, preferred_element_type=jnp.float32)
    route_onehot = (route_rows[..., None] == jnp.arange(expert_count, dtype=jnp.int32)).astype(
        jnp.float32
    )
    gate_weights = jax.nn.softmax(jnp.sum(route_onehot * logits[:, None, :], axis=-1), axis=-1)
    target_slot, slot_owner = dispatch_plan(route_rows, expert_count, capacity)
    padded_rows = jnp.concatenate([mixed_low, jnp.zeros((1, model_width), jnp.bfloat16)], axis=0)
    send_rows = jnp.take(padded_rows, slot_owner // top_count, axis=0).reshape(slot_shape)
    received = lax.all_to_all(send_rows, "ctx", split_axis=0, concat_axis=0, tiled=True).reshape(
        expert_shape
    )
    expert_up = jnp.einsum(
        "sxcd,xdf->sxcf", received, gathered_first, preferred_element_type=jnp.float32
    )
    gate_part = expert_up[..., :FF]
    up_part = expert_up[..., FF:]
    sigmoid_gate = jax.nn.sigmoid(gate_part)
    swish_gate = gate_part * sigmoid_gate
    hidden_low = (swish_gate * up_part).astype(jnp.bfloat16)
    expert_result = jnp.einsum(
        "sxcf,xfd->sxcd", hidden_low, gathered_second, preferred_element_type=jnp.float32
    ).astype(jnp.bfloat16)
    returned = lax.all_to_all(
        expert_result.reshape(slot_shape), "ctx", split_axis=0, concat_axis=0, tiled=True
    ).reshape(expert_count * capacity, model_width)
    pair_result = jnp.take(returned, target_slot, axis=0).reshape(tok_rows, top_count, model_width)
    mixture = jnp.sum(gate_weights[..., None] * pair_result, axis=1)
    layer_output = (residual + mixture).astype(jnp.bfloat16)
    upstream = cotangent[0].astype(jnp.float32)
    pair_back = (gate_weights[..., None] * upstream[:, None, :]).astype(jnp.bfloat16)
    gate_back = jnp.sum(pair_result * upstream[:, None, :], axis=-1)
    padded_back = jnp.concatenate(
        [
            pair_back.reshape(tok_rows * top_count, model_width),
            jnp.zeros((1, model_width), jnp.bfloat16),
        ],
        axis=0,
    )
    send_back = jnp.take(padded_back, slot_owner, axis=0).reshape(slot_shape)
    received_back = lax.all_to_all(
        send_back, "ctx", split_axis=0, concat_axis=0, tiled=True
    ).reshape(expert_shape)
    first_back, second_back = (gathered_first, gathered_second)
    hidden_back = jnp.einsum(
        "sxcd,xfd->sxcf", received_back, second_back, preferred_element_type=jnp.float32
    )
    second_weight_back = jnp.einsum(
        "sxcf,sxcd->xfd", hidden_low, received_back, preferred_element_type=jnp.float32
    )
    swish_slope = sigmoid_gate * (1.0 + gate_part * (1.0 - sigmoid_gate))
    up_back = jnp.concatenate(
        [hidden_back * up_part * swish_slope, hidden_back * swish_gate], axis=-1
    ).astype(jnp.bfloat16)
    first_weight_back = jnp.einsum(
        "sxcd,sxcf->xdf", received, up_back, preferred_element_type=jnp.float32
    )
    input_back = jnp.einsum(
        "sxcf,xdf->sxcd", up_back, first_back, preferred_element_type=jnp.float32
    ).astype(jnp.bfloat16)
    expert_in_gradient, expert_out_gradient = (
        lax.psum_scatter(
            first_weight_back.astype(jnp.bfloat16), "dp", scatter_dimension=1, tiled=True
        ).astype(jnp.float32),
        lax.psum_scatter(
            second_weight_back.astype(jnp.bfloat16), "dp", scatter_dimension=1, tiled=True
        ).astype(jnp.float32),
    )
    rows_back = lax.all_to_all(
        input_back.reshape(slot_shape), "ctx", split_axis=0, concat_axis=0, tiled=True
    ).reshape(expert_count * capacity, model_width)
    mixed_back = jnp.sum(
        jnp.take(rows_back, target_slot, axis=0)
        .reshape(tok_rows, top_count, model_width)
        .astype(jnp.float32),
        axis=1,
    )
    gains_back, in_back, out_back, router_back = (
        gathered_gains,
        gathered_in,
        gathered_out,
        gathered_router,
    )
    gain_values = gains_back.astype(jnp.float32)
    chosen_back = gate_weights * (
        gate_back - jnp.sum(gate_weights * gate_back, axis=-1, keepdims=True)
    )
    logit_back = jnp.sum(chosen_back[..., None] * route_onehot, axis=1).astype(jnp.bfloat16)
    router_weight_back = jnp.einsum(
        "td,te->de", mixed_low, logit_back, preferred_element_type=jnp.float32
    )
    mixed_back = mixed_back + jnp.einsum(
        "te,de->td", logit_back, router_back, preferred_element_type=jnp.float32
    )
    mixed_gain_back = jnp.sum(mixed_back * mixed_normed, axis=0)
    residual_back = upstream + normalize_back(
        mixed_back * gain_values[:, 3], mixed_normed, mixed_inverse
    )
    residual_low = residual_back.astype(jnp.bfloat16)
    out_weight_back = jnp.einsum(
        "td,te->de", attend_low, residual_low, preferred_element_type=jnp.float32
    )
    attend_back = (
        jnp.einsum("te,de->td", residual_low, out_back, preferred_element_type=jnp.float32)
        .astype(jnp.bfloat16)
        .reshape(heads_shape)
    )
    row_delta = jnp.einsum("thd,thd->ht", attend_back.astype(jnp.float32), attend_out)

    def back_step(query_acc, block_args):
        key_block, value_block, key_place, key_document = block_args
        query_part, key_part, value_part = block_backward(
            query_low,
            attend_back,
            row_logsum,
            row_delta,
            key_block,
            value_block,
            own_place,
            own_document,
            key_place,
            key_document,
            score_scale,
        )
        return (query_acc + query_part, (key_part, value_part))

    query_back, (key_parts, value_parts) = lax.scan(
        back_step,
        jnp.zeros(heads_shape, jnp.float32),
        (key_split, value_split, place_split, document_split),
    )
    key_back, value_back = (
        lax.psum_scatter(
            key_parts.reshape(sequence_rows, model_width).astype(jnp.bfloat16),
            "ctx",
            scatter_dimension=0,
            tiled=True,
        ).astype(jnp.float32),
        lax.psum_scatter(
            value_parts.reshape(sequence_rows, model_width).astype(jnp.bfloat16),
            "ctx",
            scatter_dimension=0,
            tiled=True,
        ).astype(jnp.float32),
    )
    query_flat = rotate(query_back, cosine, -sine_table).reshape(tok_rows, model_width)
    key_flat = rotate(key_back.reshape(heads_shape), cosine, -sine_table).reshape(
        tok_rows, model_width
    )
    query_gain_back = jnp.sum(query_flat * query_normed, axis=0)
    key_gain_back = jnp.sum(key_flat * key_normed, axis=0)
    raw_query_back = normalize_back(query_flat * gain_values[:, 1], query_normed, query_inverse)
    raw_key_back = normalize_back(key_flat * gain_values[:, 2], key_normed, key_inverse)
    raw_back = jnp.concatenate([raw_query_back, raw_key_back, value_back], axis=-1).astype(
        jnp.bfloat16
    )
    in_weight_back = jnp.einsum(
        "td,tf->df", attend_in, raw_back, preferred_element_type=jnp.float32
    )
    attend_in_back = jnp.einsum("tf,df->td", raw_back, in_back, preferred_element_type=jnp.float32)
    attend_gain_back = jnp.sum(attend_in_back * attend_normed, axis=0)
    tokens_back = residual_back + normalize_back(
        attend_in_back * gain_values[:, 0], attend_normed, attend_inverse
    )
    gain_columns = jnp.stack(
        [attend_gain_back, query_gain_back, key_gain_back, mixed_gain_back], axis=1
    )
    gains_gradient, project_in_gradient, project_out_gradient, router_gradient = (
        lax.psum_scatter(gain_columns, ("dp", "ctx"), scatter_dimension=0, tiled=True),
        lax.psum_scatter(in_weight_back, ("dp", "ctx"), scatter_dimension=0, tiled=True),
        lax.psum_scatter(out_weight_back, ("dp", "ctx"), scatter_dimension=0, tiled=True),
        lax.psum_scatter(router_weight_back, ("dp", "ctx"), scatter_dimension=0, tiled=True),
    )
    return (
        layer_output[None],
        tokens_back.astype(jnp.bfloat16)[None],
        gains_gradient,
        project_in_gradient,
        project_out_gradient,
        router_gradient,
        expert_in_gradient,
        expert_out_gradient,
    )


def solution(mesh):
    placed = (
        P("dp", "ctx", None),
        P("dp", None),
        P("dp", "ctx", None),
        P(("dp", "ctx"), None),
        P(("dp", "ctx"), None),
        P(("dp", "ctx"), None),
        P(("dp", "ctx"), None),
        P("ctx", "dp", None),
        P("ctx", "dp", None),
        P("dp", "ctx", None),
    )
    return jax.shard_map(
        local,
        mesh=mesh,
        in_specs=placed,
        out_specs=(
            P("dp", "ctx", None),
            P("dp", "ctx", None),
            P(("dp", "ctx"), None),
            P(("dp", "ctx"), None),
            P(("dp", "ctx"), None),
            P(("dp", "ctx"), None),
            P("ctx", "dp", None),
            P("ctx", "dp", None),
        ),
        check_vma=False,
    )
```

profile of v0, /device:TPU:1, one launch (start us, length us, event | category | flops | bytes accessed | tf_op | source)
XLA Modules:
  0.0 2926.0 jit_solution(12027754991494369237)
XLA Ops:
  8.0 62.9 %all-gather = bf16[32,64,4]{1,2,0:T(4,128)(2,1)S(1)} all-gather(bf16[1,64,4]{1,2,0:T(4,128)(2,1)} %bitcast.392), channel_id=1, replica_groups=mesh['dp'=4,'ctx'=8] {'dp','ctx'}, dimensions={0}, use_global_device_ids=true | all-gather | bytes 16896 | tf_op jit(solution)/shard_map/all_gather | solution.py:158
  77.2 91.3 %all-gather.9.cloned.1.call-done = bf16[2048,6144]{1,0:T(8,128)(2,1)} async-done(((bf16[64,6144]{1,0:T(8,128)(2,1)}), bf16[2048,6144]{1,0:T(8,128)(2,1)}) %all-gather.9.cloned.1.call-update) | async-done | bytes 25165840 | tf_op jit(solution)/shard_map/all_gather | solution.py:159
  209.2 52.4 %all-gather.13.cloned.1.call-done = bf16[1024,2048]{1,0:T(8,128)(2,1)} async-done(((bf16[128,2048]{1,0:T(8,128)(2,1)}), bf16[1024,2048]{1,0:T(8,128)(2,1)}) %all-gather.13.cloned.1.call-update) | async-done | bytes 4194320 | tf_op jit(solution)/shard_map/all_gather | solution.py:194
  268.2 67.8 %all-gather.11.cloned.1.call-done = bf16[1024,2048]{1,0:T(8,128)(2,1)} async-done(((bf16[128,2048]{1,0:T(8,128)(2,1)}), bf16[1024,2048]{1,0:T(8,128)(2,1)}) %all-gather.11.cloned.1.call-update) | async-done | bytes 4194320 | tf_op jit(solution)/shard_map/all_gather | solution.py:195
  341.6 15.9 while.39
  357.5 19.9 while.40
  379.0 37.2 %all-gather.15.cloned.1.call-done = bf16[2048,2048]{1,0:T(8,128)(2,1)} async-done(((bf16[64,2048]{1,0:T(8,128)(2,1)}), bf16[2048,2048]{1,0:T(8,128)(2,1)}) %all-gather.15.cloned.1.call-update) | async-done | bytes 8388624 | tf_op jit(solution)/shard_map/all_gather | solution.py:160
  446.7 75.4 %all-gather.17.cloned.1.call-done = bf16[2,2048,2048]{2,1,0:T(8,128)(2,1)} async-done(((bf16[2,512,2048]{2,1,0:T(8,128)(2,1)}), bf16[2,2048,2048]{2,1,0:T(8,128)(2,1)}) %all-gather.17.cloned.1.call-update) | async-done | bytes 16777232 | tf_op jit(solution)/shard_map/all_gather | solution.py:164
  522.2 107.0 %all-to-all-done = bf16[8,256,2048]{2,1,0:T(8,128)(2,1)} async-done(((bf16[8,256,2048]{2,1,0:T(8,128)(2,1)}), bf16[8,256,2048]{2,1,0:T(8,128)(2,1)}, u32[]{:S(2)}, u32[]{:S(2)}) %all-to-all-start) | async-done | bytes 8388640 | tf_op jit(solution)/shard_map/all_to_all | solution.py:255
  629.1 24.7 fusion.91
  662.4 15.1 convert_bitcast_fusion.2
  690.9 233.6 %all-gather.1 = bf16[32,64,16]{1,2,0:T(8,128)(2,1)S(1)} all-gather(bf16[1,64,16]{1,2,0:T(8,128)(2,1)S(1)} %bitcast.390), channel_id=1, replica_groups=mesh['dp'=4,'ctx'=8] {'dp','ctx'}, dimensions={0}, use_global_device_ids=true | all-gather | bytes 67584 | tf_op jit(solution)/shard_map/all_gather | solution.py:161
  925.3 13.3 gather_fusion.5
  945.4 19.1 gather_fusion.2
  972.0 187.4 %all_to_all.20 = bf16[8,256,2048]{2,1,0:T(8,128)(2,1)} all-to-all(bf16[8,256,2048]{2,1,0:T(8,128)(2,1)} %broadcast_select_fusion), channel_id=1, replica_groups=mesh['dp'=4,'ctx'=8] {'ctx'}, dimensions={0} | all-to-all | bytes 16777216 | tf_op jit(solution)/shard_map/all_to_all | solution.py:286
  1159.5 19.7 fusion.79
  1179.2 24.2 convert_bitcast_fusion.1
  1217.0 179.3 %all-to-all-done.3 = bf16[8,256,2048]{2,1,0:T(8,128)(2,1)} async-done(((bf16[8,256,2048]{2,1,0:T(8,128)(2,1)}), bf16[8,256,2048]{2,1,0:T(8,128)(2,1)}, u32[]{:S(2)}, u32[]{:S(2)}) %all-to-all-start.3) | async-done | bytes 8388640 | tf_op jit(solution)/shard_map/all_to_all | solution.py:314
  1396.2 13.3 gather_fusion.6
  1430.9 26.8 while.41
  1478.6 15.2 bitcast_convert_fusion.1
  1494.1 63.2 %reduce-scatter.13.cloned.1.call-done = bf16[128,2048]{1,0:T(8,128)(2,1)} async-done(((bf16[1024,2048]{1,0:T(8,128)(2,1)}), bf16[128,2048]{1,0:T(8,128)(2,1)}) %reduce-scatter.13.cloned.1.call-update) | async-done | bytes 524304 | tf_op jit(solution)/shard_map/reduce_scatter | solution.py:378
  1572.6 77.2 %reduce-scatter.15.cloned.1.call-done = bf16[128,2048]{1,0:T(8,128)(2,1)} async-done(((bf16[1024,2048]{1,0:T(8,128)(2,1)}), bf16[128,2048]{1,0:T(8,128)(2,1)}) %reduce-scatter.15.cloned.1.call-update) | async-done | bytes 524304 | tf_op jit(solution)/shard_map/reduce_scatter | solution.py:384
  1649.8 14.5 fusion.112
  1665.8 24.4 bitcast_convert_fusion
  1701.2 19.6 fusion.116
  1720.9 58.0 %reduce-scatter.27.cloned.1.call-done = f32[64,16]{1,0:T(8,128)} async-done(((f32[2048,16]{1,0:T(8,128)}), f32[64,16]{1,0:T(8,128)}) %reduce-scatter.27.cloned.1.call-update) | async-done | bytes 4112
  1780.3 77.7 %reduce-scatter.23.cloned.1.call-done = bf16[2,256,2048]{2,1,0:T(8,128)(2,1)} async-done(((bf16[2,1024,2048]{2,1,0:T(8,128)(2,1)}), bf16[2,256,2048]{2,1,0:T(8,128)(2,1)}) %reduce-scatter.23.cloned.1.call-update) | async-done | bytes 2097168 | tf_op jit(solution)/shard_map/reduce_scatter | solution.py:310
  1863.3 124.0 %reduce-scatter.25.cloned.1.call-done = f32[64,4]{1,0:T(8,128)} async-done(((f32[2048,4]{1,0:T(8,128)}), f32[64,4]{1,0:T(8,128)}) %reduce-scatter.25.cloned.1.call-update) | async-done | bytes 1040
  1988.7 131.7 %reduce-scatter.21.cloned.1.call-done = bf16[2,512,2048]{2,1,0:T(8,128)(2,1)} async-done(((bf16[2,2048,2048]{2,1,0:T(8,128)(2,1)}), bf16[2,512,2048]{2,1,0:T(8,128)(2,1)}) %reduce-scatter.21.cloned.1.call-update) | async-done | bytes 4194320 | tf_op jit(solution)/shard_map/reduce_scatter | solution.py:307
  2127.1 353.7 %reduce-scatter.19.cloned.1.call-done = f32[64,2048]{1,0:T(8,128)} async-done(((f32[2048,2048]{1,0:T(8,128)}), f32[64,2048]{1,0:T(8,128)}) %reduce-scatter.19.cloned.1.call-update) | async-done | bytes 524304 | tf_op jit(solution)/shard_map/reduce_scatter | solution.py:416
  2480.7 438.5 %reduce-scatter.17.cloned.1.call-done = f32[64,6144]{1,0:T(8,128)} async-done(((f32[2048,6144]{1,0:T(8,128)}), f32[64,6144]{1,0:T(8,128)}) %reduce-scatter.17.cloned.1.call-update) | async-done | bytes 1572880 | tf_op jit(solution)/shard_map/reduce_scatter | solution.py:415
  (333 shorter events, 289.1 us)
Async XLA Ops:
  7.2 161.4 %all-gather.9.cloned.1.call-start = ((), (), s32[]{:S(2)}) async-start(), calls=%async_computation.12 | async-start | bytes 25952256 | tf_op jit(solution)/shard_map/all_gather | solution.py:159
  7.9 253.7 %all-gather.13.cloned.1.call-start = ((), (), s32[]{:S(2)}) async-start(), calls=%async_computation.14 | async-start | bytes 4718592 | tf_op jit(solution)/shard_map/all_gather | solution.py:194
  76.3 102.4 %copy-start.47 = (f32[128]{0:T(128)}, f32[128]{0:T(128)S(1)}, u32[]{:S(2)}) copy-start(f32[128]{0:T(128)S(1)} %add_rsqrt_fusion.3) | copy-start | bytes 1540
  77.2 108.9 %copy-start.34 = (f32[128,64]{0,1:T(8,128)}, f32[128,64]{0,1:T(8,128)S(1)}, u32[]{:S(2)}) copy-start(f32[128,64]{0,1:T(8,128)S(1)} %get-tuple-element.592) | copy-start | bytes 98308
  77.2 101.6 %copy-start.28 = (f32[2048,1]{0,1:T(1,128)}, f32[2048,1]{0,1:T(1,128)S(1)}, u32[]{:S(2)}) copy-start(f32[2048,1]{0,1:T(1,128)S(1)} %get-tuple-element.585) | copy-start | bytes 24580
  77.2 101.8 %copy-start.38 = (f32[2048,1]{0,1:T(1,128)}, f32[2048,1]{0,1:T(1,128)S(1)}, u32[]{:S(2)}) copy-start(f32[2048,1]{0,1:T(1,128)S(1)} %get-tuple-element.583) | copy-start | bytes 24580
  77.2 101.8 %copy-start.40 = (f32[2048,1]{0,1:T(1,128)}, f32[2048,1]{0,1:T(1,128)S(1)}, u32[]{:S(2)}) copy-start(f32[2048,1]{0,1:T(1,128)S(1)} %get-tuple-element.584) | copy-start | bytes 24580
  77.2 343.8 %copy-start.42 = (f32[2048,1]{0,1:T(1,128)}, f32[2048,1]{0,1:T(1,128)S(1)}, u32[]{:S(2)}) copy-start(f32[2048,1]{0,1:T(1,128)S(1)} %get-tuple-element.582) | copy-start | bytes 24580
  191.5 144.5 %all-gather.11.cloned.1.call-start = ((), (), s32[]{:S(2)}) async-start(), calls=%async_computation.13 | async-start | bytes 4718592 | tf_op jit(solution)/shard_map/all_gather | solution.py:195
  192.4 223.8 %all-gather.15.cloned.1.call-start = ((), (), s32[]{:S(2)}) async-start(), calls=%async_computation.15 | async-start | bytes 8650752 | tf_op jit(solution)/shard_map/all_gather | solution.py:160
  193.0 329.2 %all-gather.17.cloned.1.call-start = ((), (), s32[]{:S(2)}) async-start(), calls=%async_computation.16 | async-start | bytes 20971520 | tf_op jit(solution)/shard_map/all_gather | solution.py:164
  357.5 58.7 %copy-start.13 = (bf16[1,128,2048]{2,1,0:T(8,128)(2,1)S(1)}, bf16[1,128,2048]{2,1,0:T(8,128)(2,1)}, u32[]{:S(2)}) copy-start(bf16[1,128,2048]{2,1,0:T(8,128)(2,1)} %param.20) | copy-start | bytes 1572868
  422.1 502.8 %copy-start.17 = (bf16[128,2048]{1,0:T(8,128)(2,1)}, bf16[128,2048]{1,0:T(8,128)(2,1)S(1)}, u32[]{:S(2)}) copy-start(bf16[128,2048]{1,0:T(8,128)(2,1)S(1)} %multiply_convert_fusion.3) | copy-start | bytes 1572868
  441.2 187.9 %all-to-all-start = ((bf16[8,256,2048]{2,1,0:T(8,128)(2,1)}), bf16[8,256,2048]{2,1,0:T(8,128)(2,1)}, u32[]{:S(2)}, u32[]{:S(2)}) async-start(bf16[8,256,2048]{2,1,0:T(8,128)(2,1)} %broadcast_select_fusion.1), calls=%async_computation | async-start | bytes 16777216 | tf_op jit(solution)/shard_map/all_to_all | solution.py:255
  446.1 216.2 %all-gather.19.cloned.1.call-start = ((), (), s32[]{:S(2)}) async-start(), calls=%async_computation.17 | async-start | bytes 10485760 | tf_op jit(solution)/shard_map/all_gather | solution.py:165
  685.8 239.0 %copy-start.24 = (bf16[1,128,2048]{2,1,0:T(8,128)(2,1)S(1)}, bf16[1,128,2048]{2,1,0:T(8,128)(2,1)}, u32[]{:S(2)}) copy-start(bf16[1,128,2048]{2,1,0:T(8,128)(2,1)} %param.29) | copy-start | bytes 1572868
  685.8 239.4 %all-to-all-start.1 = ((bf16[8,256,2048]{2,1,0:T(8,128)(2,1)}), bf16[8,256,2048]{2,1,0:T(8,128)(2,1)}, u32[]{:S(2)}, u32[]{:S(2)}) async-start(bf16[8,256,2048]{2,1,0:T(8,128)(2,1)} %bitcast.341), calls=%async_computation.1 | async-start | bytes 16777216 | tf_op jit(solution)/shard_map/all_to_all | solution.py:269
  1211.6 184.6 %all-to-all-start.3 = ((bf16[8,256,2048]{2,1,0:T(8,128)(2,1)}), bf16[8,256,2048]{2,1,0:T(8,128)(2,1)}, u32[]{:S(2)}, u32[]{:S(2)}) async-start(bf16[8,256,2048]{2,1,0:T(8,128)(2,1)} %bitcast.342), calls=%async_computation.3 | async-start | bytes 16777216 | tf_op jit(solution)/shard_map/all_to_all | solution.py:314
  1216.6 340.7 %reduce-scatter.13.cloned.1.call-start = ((), (), s32[]{:S(2)}) async-start(), calls=%async_computation.18 | async-start | bytes 4718592 | tf_op jit(solution)/shard_map/reduce_scatter | solution.py:378
  1466.8 183.0 %reduce-scatter.15.cloned.1.call-start = ((), (), s32[]{:S(2)}) async-start(), calls=%async_computation.19 | async-start | bytes 4718592 | tf_op jit(solution)/shard_map/reduce_scatter | solution.py:384
  1476.0 302.8 %reduce-scatter.27.cloned.1.call-start = ((), (), s32[]{:S(2)}) async-start(), calls=%async_computation.25 | async-start | bytes 1081344
  1478.5 379.5 %reduce-scatter.23.cloned.1.call-start = ((), (), s32[]{:S(2)}) async-start(), calls=%async_computation.23 | async-start | bytes 10485760 | tf_op jit(solution)/shard_map/reduce_scatter | solution.py:310
  1493.8 64.8 %copy-start.8 = (f32[128,16,128]{0,2,1:T(8,128)S(1)}, f32[128,16,128]{0,2,1:T(8,128)}, u32[]{:S(2)}) copy-start(f32[128,16,128]{0,2,1:T(8,128)} %get-tuple-element.187) | copy-start | bytes 3145732
  1493.8 64.8 %copy-start.35 = (f32[128,64]{0,1:T(8,128)S(1)}, f32[128,64]{0,1:T(8,128)}, u32[]{:S(2)}) copy-start(f32[128,64]{0,1:T(8,128)} %copy-done.34) | copy-start | bytes 98308
  1493.8 64.8 %copy-start.44 = (f32[128,64]{0,1:T(8,128)S(1)}, f32[128,64]{0,1:T(8,128)}, u32[]{:S(2)}) copy-start(f32[128,64]{0,1:T(8,128)} %get-tuple-element.590) | copy-start | bytes 98308
  1493.9 493.5 %reduce-scatter.25.cloned.1.call-start = ((), (), s32[]{:S(2)}) async-start(), calls=%async_computation.24 | async-start | bytes 1081344
  1568.7 81.2 %copy-start.29 = (f32[2048,1]{0,1:T(1,128)S(1)}, f32[2048,1]{0,1:T(1,128)}, u32[]{:S(2)}) copy-start(f32[2048,1]{0,1:T(1,128)} %copy-done.28) | copy-start | bytes 24580
  1568.7 81.1 %copy-start.48 = (f32[128]{0:T(128)S(1)}, f32[128]{0:T(128)}, u32[]{:S(2)}) copy-start(f32[128]{0:T(128)} %copy-done.47) | copy-start | bytes 1540
  1665.7 454.7 %reduce-scatter.21.cloned.1.call-start = ((), (), s32[]{:S(2)}) async-start(), calls=%async_computation.22 | async-start | bytes 20971520 | tf_op jit(solution)/shard_map/reduce_scatter | solution.py:307
  1690.2 790.5 %reduce-scatter.19.cloned.1.call-start = ((), (), s32[]{:S(2)}) async-start(), calls=%async_computation.21 | async-start | bytes 17301504 | tf_op jit(solution)/shard_map/reduce_scatter | solution.py:416
  1699.7 1219.5 %reduce-scatter.17.cloned.1.call-start = ((), (), s32[]{:S(2)}) async-start(), calls=%async_computation.20 | async-start | bytes 51904512 | tf_op jit(solution)/shard_map/reduce_scatter | solution.py:415
  1720.9 141.3 %copy-start.25 = (f32[128,2048]{1,0:T(8,128)S(1)}, f32[128,2048]{1,0:T(8,128)}, u32[]{:S(2)}) copy-start(f32[128,2048]{1,0:T(8,128)} %get-tuple-element.596) | copy-start | bytes 3145732
  (46 other events, 463.2 us)
Sparse Core Ops, SparseCore 0:
  11.0 157.5 all-gather.8
  191.6 69.9 all-gather.12
  264.3 71.6 all-gather.10
  338.8 77.2 all-gather.14
  417.6 104.5 all-gather.16
  523.6 58.2 all-gather.18
  1466.9 90.3 reduce-scatter.12
  1562.0 87.7 reduce-scatter.14
  1652.1 126.7 reduce-scatter.26
  1782.1 75.9 reduce-scatter.22
  1860.3 126.9 reduce-scatter.24
  1989.9 130.4 reduce-scatter.20
  2123.3 357.3 reduce-scatter.18
  2487.6 431.5 reduce-scatter.16
where the time goes:
time: 2930 us
  waiting for transfers between devices  1940 us (66%)
  blocking collectives  484 us (17%)
  matrix products  233 us (8%)
  local copies, waits for them, and re-layouts  155 us (5%)
  other arithmetic  85.2 us (3%)
    reduce_scatter x1, waiting for transfers between devices, local(): lax.psum_scatter(in_weight_back, ('dp', 'ctx'), scatter_dimension=0, tile...  438 us
    reduce_scatter x1, waiting for transfers between devices, local(): lax.psum_scatter(out_weight_back, ('dp', 'ctx'), scatter_dimension=0, til...  354 us
    all_gather x1, blocking collectives, local(): lax.all_gather(router_weight, ('dp', 'ctx'), axis=0, tiled=True)  234 us
    all_to_all x1, blocking collectives, local(): lax.all_to_all(send_back, 'ctx', split_axis=0, concat_axis=0, tiled=True)  187 us
    unnamed x16, waiting for transfers between devices  184 us
    all_to_all x1, waiting for transfers between devices, local(): lax.all_to_all(input_back.reshape(slot_shape), 'ctx', split_axis=0, conca...  179 us
    reduce_scatter x1, waiting for transfers between devices, local(): lax.psum_scatter(first_weight_back.astype(jnp.bfloat16), 'dp', scatter_di...  132 us
    all_to_all x1, waiting for transfers between devices, local(): lax.all_to_all(send_rows, 'ctx', split_axis=0, concat_axis=0, tiled=True)  107 us
  transfers between devices with their start and end apart: 17, of which 15 were waited for; matrix products, arithmetic and copies ran while one was open for 9% of the time, Pallas kernels for 0%

commit v1 on v0

--- a/solution.py
+++ b/solution.py
@@ -126,7 +126,7 @@
     return (target_slot, slot_owner)
 
 
-def local(
+def gathered_local(
     tokens,
     document_ids,
     routes,
@@ -428,7 +428,217 @@
     )
 
 
+def gather_ctx(block):
+    return lax.all_gather(block, "ctx", axis=0, tiled=True)
+
+
+def scatter_ctx(partial):
+    return lax.psum_scatter(
+        partial.astype(jnp.bfloat16), "ctx", scatter_dimension=0, tiled=True
+    ).astype(jnp.float32)
+
+
+def heads_local(
+    tokens,
+    document_ids,
+    routes,
+    norm_gains,
+    project_in,
+    project_out,
+    router_weight,
+    expert_in,
+    expert_out,
+    cotangent,
+):
+    bf16, f32 = jnp.bfloat16, jnp.float32
+    n = lax.axis_size("ctx")
+    n_dp = lax.axis_size("dp")
+    me = lax.axis_index("ctx")
+    tok_rows, width = tokens.shape[1:]
+    rows = tok_rows * n
+    weight_rows = project_in.shape[0]
+    own_heads = HEADS // n
+    cols = own_heads * HEAD_DIM
+    local_experts = expert_in.shape[0]
+    expert_count = local_experts * n
+    score_scale = HEAD_DIM ** (-0.5)
+
+    def own(array, size, axis=0):
+        return lax.dynamic_slice_in_dim(array, me * size, size, axis)
+
+    token_all = gather_ctx(tokens[0])
+    upstream_all = gather_ctx(cotangent[0])
+    route_all = gather_ctx(routes[0])
+    in_blocks = project_in.reshape(weight_rows, 3, n, cols).transpose(2, 0, 1, 3)
+    in_blocks = in_blocks.reshape(n, weight_rows, 3 * cols)
+    in_blocks = lax.all_to_all(in_blocks, "ctx", split_axis=0, concat_axis=0, tiled=True)
+    in_own = lax.all_gather(in_blocks, "dp", axis=0, tiled=True).reshape(width, 3 * cols)
+    small = jnp.concatenate([norm_gains, router_weight], axis=1)
+    small_all = lax.all_gather(small, ("dp", "ctx"), axis=0, tiled=True)
+    gains = small_all[:, :4].astype(f32)
+    router_all = small_all[:, 4:]
+    out_all = lax.all_gather(project_out, ("dp", "ctx"), axis=0, tiled=True)
+    first = lax.all_gather(expert_in, "dp", axis=1, tiled=True)
+    second = lax.all_gather(expert_out, "dp", axis=1, tiled=True)
+
+    places = dealt_positions(jnp.arange(rows, dtype=jnp.int32), tok_rows, n)
+    document_row = document_ids[0]
+    documents = jnp.take(document_row, places)
+    relative = places - jnp.take(document_starts(document_row), places)
+    cosine, sine = rotary_tables(relative, HEAD_DIM)
+    visible = (documents[None, :] == documents[:, None]) & (places[None, :] <= places[:, None])
+
+    inputs = token_all.astype(f32)
+    attend_inverse = inverse_rms(inputs)
+    attend_in = (inputs * attend_inverse * gains[:, 0]).astype(bf16)
+    projected = jnp.dot(attend_in, in_own, preferred_element_type=f32)
+    raw = projected[:, : 2 * cols].reshape(rows, 2, cols)
+    squares = lax.psum(jnp.sum(raw * raw, axis=-1), "ctx")
+    inverse = lax.rsqrt(squares / width + EPSILON)[..., None]
+    normed = raw * inverse
+    pair_gains = own(gains, cols)[:, 1:3].T
+    rotated = rotate((normed * pair_gains).reshape(rows, 2 * own_heads, HEAD_DIM), cosine, sine)
+    rotated = rotated.reshape(rows, 2, own_heads, HEAD_DIM).astype(bf16)
+    query, key = rotated[:, 0], rotated[:, 1]
+    value = projected[:, 2 * cols :].astype(bf16).reshape(rows, own_heads, HEAD_DIM)
+
+    scores = jnp.einsum("thd,khd->htk", query, key, preferred_element_type=f32) * score_scale
+    scores = jnp.where(visible[None], scores, MASKED)
+    peak = jnp.max(scores, axis=-1, keepdims=True)
+    powers = jnp.where(visible[None], jnp.exp(scores - peak), 0.0)
+    total = jnp.sum(powers, axis=-1, keepdims=True)
+    probs = (powers / total).astype(bf16)
+    attend_out = jnp.einsum("htk,khd->thd", probs, value, preferred_element_type=f32)
+    attend_low = attend_out.reshape(rows, cols).astype(bf16)
+    attend_all = lax.all_gather(attend_low, "ctx", axis=1, tiled=True)
+
+    residual = inputs + jnp.dot(attend_all, out_all, preferred_element_type=f32)
+    mixed_inverse = inverse_rms(residual)
+    mixed_low = (residual * mixed_inverse * gains[:, 3]).astype(bf16)
+    logits = jnp.dot(mixed_low, router_all, preferred_element_type=f32)
+    named = jnp.any(
+        route_all[..., None] == jnp.arange(expert_count, dtype=jnp.int32), axis=1
+    )
+    chosen = jnp.where(named, logits, MASKED)
+    chosen = jnp.where(named, jnp.exp(chosen - jnp.max(chosen, axis=-1, keepdims=True)), 0.0)
+    gates = chosen / jnp.sum(chosen, axis=-1, keepdims=True)
+    gate_own = own(gates, local_experts, 1).T[..., None]
+
+    expert_up = jnp.einsum("td,xdf->xtf", mixed_low, first, preferred_element_type=f32)
+    gate_part, up_part = expert_up[..., :FF], expert_up[..., FF:]
+    sigmoid = jax.nn.sigmoid(gate_part)
+    swish = gate_part * sigmoid
+    hidden = swish * up_part
+    hidden_gated = (hidden * gate_own).astype(bf16)
+    mixture = jnp.einsum("xtf,xfd->td", hidden_gated, second, preferred_element_type=f32)
+    mixture = scatter_ctx(mixture)
+    own_residual = own(residual, tok_rows)
+    layer_output = (own_residual + mixture).astype(bf16)
+
+    hidden_back = jnp.einsum("td,xfd->xtf", upstream_all, second, preferred_element_type=f32)
+    gate_back = jnp.sum(hidden.astype(bf16).astype(f32) * hidden_back, axis=-1)
+    hidden_back = hidden_back * gate_own
+    slope = sigmoid * (1.0 + gate_part * (1.0 - sigmoid))
+    up_back = jnp.concatenate(
+        [hidden_back * up_part * slope, hidden_back * swish], axis=-1
+    ).astype(bf16)
+    second_back = jnp.einsum("xtf,td->xfd", hidden_gated, upstream_all, preferred_element_type=f32)
+    first_back = jnp.einsum("td,xtf->xdf", mixed_low, up_back, preferred_element_type=f32)
+    expert_in_gradient, expert_out_gradient = (
+        lax.psum_scatter(part.astype(bf16), "dp", scatter_dimension=1, tiled=True).astype(f32)
+        for part in (first_back, second_back)
+    )
+    mixed_back = scatter_ctx(
+        jnp.einsum("xtf,xdf->td", up_back, first, preferred_element_type=f32)
+    )
+    gate_back = lax.all_to_all(
+        gate_back.reshape(local_experts, n, tok_rows), "ctx", split_axis=1, concat_axis=0, tiled=True
+    ).reshape(expert_count, tok_rows).T
+
+    own_gates = own(gates, tok_rows)
+    own_mixed = own(mixed_low, tok_rows)
+    own_mixed_inverse = own(mixed_inverse, tok_rows)
+    own_mixed_normed = own_residual * own_mixed_inverse
+    chosen_back = own_gates * (
+        gate_back - jnp.sum(own_gates * gate_back, axis=-1, keepdims=True)
+    )
+    logit_back = chosen_back.astype(bf16)
+    router_part = jnp.einsum("td,te->de", own_mixed, logit_back, preferred_element_type=f32)
+    mixed_back = mixed_back + jnp.einsum(
+        "te,de->td", logit_back, router_all, preferred_element_type=f32
+    )
+    mixed_gain_back = jnp.sum(mixed_back * own_mixed_normed, axis=0)
+    residual_back = cotangent[0].astype(f32) + normalize_back(
+        mixed_back * gains[:, 3], own_mixed_normed, own_mixed_inverse
+    )
+    back_all = gather_ctx(residual_back.astype(bf16))
+
+    out_part = jnp.einsum("td,te->de", attend_low, back_all, preferred_element_type=f32)
+    out_part = lax.psum_scatter(
+        out_part.astype(bf16), "dp", scatter_dimension=0, tiled=True
+    )
+    pairs = []
+    for d in range(n_dp):
+        for c in range(n):
+            pairs.append((d * n + c, c * n_dp + d))
+    project_out_gradient = lax.ppermute(out_part, ("dp", "ctx"), pairs).astype(f32)
+    attend_back = jnp.einsum(
+        "td,ed->te", back_all, own(out_all, cols), preferred_element_type=f32
+    ).astype(bf16).reshape(rows, own_heads, HEAD_DIM)
+    delta = jnp.einsum("thd,thd->ht", attend_back.astype(f32), attend_out)[..., None]
+    prob_back = jnp.einsum("thd,khd->htk", attend_back, value, preferred_element_type=f32)
+    score_back = (probs.astype(f32) * (prob_back - delta)).astype(bf16)
+    query_back = jnp.einsum("htk,khd->thd", score_back, key, preferred_element_type=f32)
+    key_back = jnp.einsum("htk,thd->khd", score_back, query, preferred_element_type=f32)
+    value_back = jnp.einsum("htk,thd->khd", probs, attend_back, preferred_element_type=f32)
+    pair_back = jnp.concatenate([query_back, key_back], axis=1) * score_scale
+    pair_back = rotate(pair_back, cosine, -sine).reshape(rows, 2, cols)
+    pair_gain_back = jnp.sum(pair_back * normed, axis=0)
+    pair_back = pair_back * pair_gains
+    means = lax.psum(jnp.sum(pair_back * normed, axis=-1), "ctx")[..., None] / width
+    pair_back = inverse * (pair_back - normed * means)
+    raw_back = jnp.concatenate(
+        [pair_back.reshape(rows, 2 * cols), value_back.reshape(rows, cols)], axis=-1
+    ).astype(bf16)
+    attend_in_back = scatter_ctx(
+        jnp.einsum("tf,df->td", raw_back, in_own, preferred_element_type=f32)
+    )
+    in_part = jnp.einsum("td,tf->df", attend_in, raw_back, preferred_element_type=f32)
+    in_part = lax.psum_scatter(in_part.astype(bf16), "dp", scatter_dimension=0, tiled=True)
+    in_part = lax.all_to_all(
+        in_part.reshape(n, weight_rows, 3 * cols), "ctx", split_axis=0, concat_axis=0, tiled=True
+    ).reshape(n, weight_rows, 3, cols)
+    project_in_gradient = in_part.transpose(1, 2, 0, 3).reshape(weight_rows, 3 * width).astype(f32)
+
+    own_inverse = own(attend_inverse, tok_rows)
+    own_normed = tokens[0].astype(f32) * own_inverse
+    attend_gain_back = jnp.sum(attend_in_back * own_normed, axis=0)
+    tokens_back = residual_back + normalize_back(
+        attend_in_back * gains[:, 0], own_normed, own_inverse
+    )
+    pair_columns = lax.dynamic_update_slice_in_dim(
+        jnp.zeros((width, 2), f32), pair_gain_back.T, me * cols, 0
+    )
+    small_part = jnp.concatenate(
+        [attend_gain_back[:, None], pair_columns, mixed_gain_back[:, None], router_part], axis=1
+    )
+    small_gradient = lax.psum_scatter(
+        small_part, ("dp", "ctx"), scatter_dimension=0, tiled=True
+    )
+    return (
+        layer_output[None],
+        tokens_back.astype(bf16)[None],
+        small_gradient[:, :4],
+        project_in_gradient,
+        project_out_gradient,
+        small_gradient[:, 4:],
+        expert_in_gradient,
+        expert_out_gradient,
+    )
+
+
 def solution(mesh):
+    split_heads = HEADS % mesh.shape["ctx"] == 0
     placed = (
         P("dp", "ctx", None),
         P("dp", None),
@@ -442,7 +652,7 @@
         P("dp", "ctx", None),
     )
     return jax.shard_map(
-        local,
+        heads_local if split_heads else gathered_local,
         mesh=mesh,
         in_specs=placed,
         out_specs=(

time: 2930 us -> 1430 us (0.49)
  waiting for transfers between devices: 1940 us -> 967 us
  blocking collectives: 484 us -> 166 us
  local copies, waits for them, and re-layouts: 155 us -> 44.3 us
  other arithmetic: 85.2 us -> 30.9 us
  matrix products: 233 us -> 184 us
    reduce_scatter x6 -> x7, waiting for transfers between devices: 1140 us -> 440 us  [the longest x3 204 us: scatter_ctx(): lax.psum_scatter(partial.astype(jnp.bfloat16), 'ctx', scatter_dimension=0...]
    all_to_all x3 -> x2, waiting for transfers between devices: 286 us -> 5.35 us  [the longest x1 5.34 us: heads_local(): lax.all_to_all(gate_back.reshape(local_experts, n, tok_rows), 'ctx', spli...]
    all_gather x2, blocking collectives: 296 us -> 91.8 us  [the longest x1 67.2 us: heads_local(): small_all = lax.all_gather(small, ('dp', 'ctx'), axis=0, tiled=True)]
    all_to_all x1, blocking collectives: 187 us -> 37.3 us  [heads_local(): lax.all_to_all(in_blocks, 'ctx', split_axis=0, concat_axis=0, tiled=True)]
    all_gather x6 -> x8, waiting for transfers between devices: 324 us -> 393 us  [the longest x3 122 us: gather_ctx(): return lax.all_gather(block, 'ctx', axis=0, tiled=True)]
    unnamed x16 -> x17, waiting for transfers between devices: 184 us -> 129 us
    dot_general x28 -> x20, matrix products: 232 us -> 177 us  [the longest x1 24.6 us: heads_local(): jnp.einsum('td,xtf->xdf', mixed_low, up_back, preferred_element_type=f32)]
    gather x8 -> x2, local copies, waits for them, and re-layouts: 63.6 us -> 9.05 us  [the longest x1 4.53 us: heads_local(): documents = jnp.take(document_row, places)]
  transfers between devices with their start and end apart: 17 -> 19, of which waited for: 15 -> 15; matrix products, arithmetic and copies ran while one was open for 9% -> 10% of each run, Pallas kernels for 0% -> 0%
where the time goes in v1:
time: 1430 us; the launch traced here: 1420 us
  waiting for transfers between devices  967 us (68%)
  matrix products  184 us (13%)
  blocking collectives  166 us (12%)
  local copies, waits for them, and re-layouts  44.3 us (3%)
  other arithmetic  30.9 us (2%)
  starting transfers between devices  15.8 us (1%)
  between operations  15.2 us (1%)
    reduce_scatter x3, waiting for transfers between devices, scatter_ctx(): lax.psum_scatter(partial.astype(jnp.bfloat16), 'ctx', scatter_dimension=0...  204 us
    reduce_scatter x2, waiting for transfers between devices, heads_local(): lax.psum_scatter(part.astype(bf16), 'dp', scatter_dimension=1, tiled=True)  200 us
    unnamed x17, waiting for transfers between devices  129 us
    all_gather x3, waiting for transfers between devices, gather_ctx(): return lax.all_gather(block, 'ctx', axis=0, tiled=True)  122 us
    all_gather x1, waiting for transfers between devices, heads_local(): first = lax.all_gather(expert_in, 'dp', axis=1, tiled=True)  83.9 us
    all_gather x1, waiting for transfers between devices, heads_local(): out_all = lax.all_gather(project_out, ('dp', 'ctx'), axis=0, tiled=True)  80.2 us
    all_gather x1, blocking collectives, heads_local(): small_all = lax.all_gather(small, ('dp', 'ctx'), axis=0, tiled=True)  67.2 us
    all_gather x1, waiting for transfers between devices, heads_local(): second = lax.all_gather(expert_out, 'dp', axis=1, tiled=True)  59.8 us
  transfers between devices with their start and end apart: 19, of which 15 were waited for; matrix products, arithmetic and copies ran while one was open for 10% of the time, Pallas kernels for 0%

profile of v1, /device:TPU:1, one launch (start us, length us, event | category | flops | bytes accessed | tf_op | source)
XLA Modules:
  0.0 1423.5 jit_solution(3590202633654882789)
XLA Ops:
  10.6 37.3 %all_to_all.25 = bf16[8,64,768]{2,1,0:T(8,128)(2,1)} all-to-all(bf16[8,64,768]{2,1,0:T(8,128)(2,1)S(1)} %reshape.376), channel_id=1, replica_groups=mesh['dp'=4,'ctx'=8] {'ctx'}, dimensions={0} | all-to-all | bytes 1572864 | tf_op jit(solution)/shard_map/all_to_all | solution.py:474
  48.0 67.2 %all-gather.3 = bf16[32,64,20]{1,2,0:T(8,128)(2,1)S(1)} all-gather(bf16[1,64,20]{1,2,0:T(8,128)(2,1)S(1)} %maximum_bitcast_fusion), channel_id=1, replica_groups=mesh['dp'=4,'ctx'=8] {'dp','ctx'}, dimensions={0}, use_global_device_ids=true | all-gather | bytes 84480 | tf_op jit(solution)/shard_map/all_gather | solution.py:477
  132.9 6.7 fusion.24
  141.6 20.2 %psum.14 = f32[1024,2]{0,1:T(2,128)S(1)} all-reduce(f32[1024,2]{0,1:T(2,128)S(1)} %bitcast_reduce_fusion), channel_id=1, replica_groups=mesh['dp'=4,'ctx'=8] {'ctx'}, use_global_device_ids=true, to_apply=%region_2.4 | all-reduce | flops 2048 | bytes 16384 | tf_op jit(solution)/shard_map/psum | solution.py:496
  163.9 7.4 fusion.70
  182.3 24.6 %all-gather.1 = s32[1,1024,8]{1,2,0:T(8,128)S(1)} all-gather(s32[1,128,8]{1,2,0:T(8,128)S(1)} %copy-done.28), channel_id=3, replica_groups=mesh['dp'=4,'ctx'=8] {'ctx'}, dimensions={1}, use_global_device_ids=true | all-gather | bytes 36864 | tf_op jit(solution)/shard_map/all_gather | solution.py:432
  207.0 47.1 %all-gather.15.cloned.1.call-done = bf16[1024,2048]{0,1:T(8,128)(2,1)} async-done(((bf16[1024,256]{0,1:T(8,128)(2,1)}), bf16[1024,2048]{0,1:T(8,128)(2,1)}) %all-gather.15.cloned.1.call-update) | async-done | bytes 4194320 | tf_op jit(solution)/shard_map/all_gather | solution.py:513
  254.1 80.2 %all-gather.17.cloned.1.call-done = bf16[2048,2048]{1,0:T(8,128)(2,1)} async-done(((bf16[64,2048]{1,0:T(8,128)(2,1)}), bf16[2048,2048]{1,0:T(8,128)(2,1)}) %all-gather.17.cloned.1.call-update) | async-done | bytes 8388624 | tf_op jit(solution)/shard_map/all_gather | solution.py:480
  334.3 14.3 %multiply_reduce_fusion = (f32[1024]{0:T(1024)S(1)}, f32[1024,2048]{1,0:T(8,128)S(1)}) fusion(bf16[1024,2048]{0,1:T(8,128)(2,1)} %all-gather.15.cloned.1.call-done, bf16[2048,2048]{1,0:T(8,128)(2,1)} %all-gather.17.cloned.1.call-done, bf16[1,1024,2048]{2,1,0:T(8,128)(2,1)} %all-gather.25.cloned.1.call-done), kind=kOutput, calls=%fused_computation.23 | convolution fusion | flops 8598322176 | bytes 25169920 | tf_op jit(solution)/shard_map/dot_general | solution.py:515
  356.4 83.9 %all-gather.19.cloned.1.call-done = bf16[2,2048,2048]{2,1,0:T(8,128)(2,1)} async-done(((bf16[2,512,2048]{2,1,0:T(8,128)(2,1)}), bf16[2,2048,2048]{2,1,0:T(8,128)(2,1)}) %all-gather.19.cloned.1.call-update) | async-done | bytes 16777232 | tf_op jit(solution)/shard_map/all_gather | solution.py:481
  440.3 23.5 %convolution_bitcast_fusion = f32[2,1024,2048]{2,1,0:T(8,128)} fusion(bf16[2,2048,2048]{2,1,0:T(8,128)(2,1)} %all-gather.19.cloned.1.call-done, bf16[1024,2048]{1,0:T(8,128)(2,1)} %copy-done.5), kind=kOutput, calls=%fused_computation.28 | convolution fusion | flops 17179869184 | bytes 37748736 | tf_op jit(solution)/shard_map/td,xdf->xtf/dot_general | solution.py:527
  463.8 50.3 %all-gather.27.cloned.1.call-done = bf16[1,1024,2048]{2,1,0:T(8,128)(2,1)} async-done(((bf16[1,128,2048]{2,1,0:T(8,128)(2,1)}), bf16[1,1024,2048]{2,1,0:T(8,128)(2,1)}) %all-gather.27.cloned.1.call-update) | async-done | bytes 4194320 | tf_op jit(solution)/shard_map/all_gather | solution.py:432
  514.1 59.8 %all-gather.21.cloned.1.call-done = bf16[2,1024,2048]{2,1,0:T(8,128)(2,1)} async-done(((bf16[2,256,2048]{2,1,0:T(8,128)(2,1)}), bf16[2,1024,2048]{2,1,0:T(8,128)(2,1)}) %all-gather.21.cloned.1.call-update) | async-done | bytes 8388624 | tf_op jit(solution)/shard_map/all_gather | solution.py:482
  573.8 22.1 %multiply_convert_fusion.2 = (bf16[2,1024,1024]{2,1,0:T(8,128)(2,1)}, bf16[2,1024,1024]{2,1,0:T(8,128)(2,1)}, f32[2,1024]{1,0:T(2,128)}, bf16[2,1024,1024]{2,1,0:T(8,128)(2,1)}) fusion(f32[2,1024,2048]{2,1,0:T(8,128)} %convolution_bitcast_fusion, f32[2,1024]{1,0:T(2,128)S(1)} %dynamic-slice_bitcast_fusion, ...), kind=kOutput, calls=%fused_computation.18 | convolution fusion | flops 8633972736 | bytes 41959424 | tf_op jit(solution)/shard_map/td,xfd->xtf/dot_general | solution.py:538
  595.9 23.9 %bitcast_convert_fusion = bf16[1024,2048]{1,0:T(8,128)(2,1)} fusion(bf16[2,2048,2048]{2,1,0:T(8,128)(2,1)} %all-gather.19.cloned.1.call-done, bf16[2,1024,1024]{2,1,0:T(8,128)(2,1)} %get-tuple-element.54, bf16[2,1024,1024]{2,1,0:T(8,128)(2,1)} %get-tuple-element.53), kind=kOutput, calls=%fused_computation.11 | convolution fusion | flops 17198743552 | bytes 29360128 | tf_op jit(solution)/shard_map/xtf,xdf->td/dot_general | solution.py:552
  619.8 5.4 all-to-all-start.1
  625.3 5.3 all-to-all-done.1
  630.7 77.0 %reduce-scatter.13.cloned.1.call-done = bf16[128,2048]{1,0:T(8,128)(2,1)} async-done(((bf16[1024,2048]{1,0:T(8,128)(2,1)}), bf16[128,2048]{1,0:T(8,128)(2,1)}) %reduce-scatter.13.cloned.1.call-update) | async-done | bytes 524304 | tf_op jit(solution)/shard_map/reduce_scatter | solution.py:436
  713.2 71.8 %all-gather.23.cloned.1.call-done = bf16[1024,2048]{1,0:T(8,128)(2,1)} async-done(((bf16[128,2048]{1,0:T(8,128)(2,1)}), bf16[1024,2048]{1,0:T(8,128)(2,1)}) %all-gather.23.cloned.1.call-update) | async-done | bytes 4194320 | tf_op jit(solution)/shard_map/all_gather | solution.py:432
  799.1 16.5 %psum.15 = f32[1024,2]{0,1:T(2,128)S(1)} all-reduce(f32[1024,2]{0,1:T(2,128)S(1)} %reduce_sum.136), channel_id=1, replica_groups=mesh['dp'=4,'ctx'=8] {'ctx'}, use_global_device_ids=true, to_apply=%region_18.20 | all-reduce | flops 2048 | bytes 16384 | tf_op jit(solution)/shard_map/psum | solution.py:598
  825.5 7.6 convolution_convert_fusion.2
  837.7 14.1 convolution_convert_fusion
  852.1 14.0 bitcast_convert_fusion.1
  867.6 45.6 %reduce-scatter.15.cloned.1.call-done = bf16[128,2048]{1,0:T(8,128)(2,1)} async-done(((bf16[1024,2048]{1,0:T(8,128)(2,1)}), bf16[128,2048]{1,0:T(8,128)(2,1)}) %reduce-scatter.15.cloned.1.call-update) | async-done | bytes 524304 | tf_op jit(solution)/shard_map/reduce_scatter | solution.py:436
  916.1 24.6 %convert_bitcast_fusion = bf16[2,2048,2048]{1,2,0:T(8,128)(2,1)} fusion(bf16[2,1024,1024]{2,1,0:T(8,128)(2,1)} %get-tuple-element.54, bf16[2,1024,1024]{2,1,0:T(8,128)(2,1)} %get-tuple-element.53, bf16[1024,2048]{1,0:T(8,128)(2,1)} %copy-done.5), kind=kOutput, calls=%fused_computation.3 | convolution fusion | flops 17205035008 | bytes 29360128 | tf_op jit(solution)/shard_map/td,xtf->xdf/dot_general | solution.py:546
  940.8 12.6 reduce-scatter.17.cloned.1.call-done
  958.6 22.8 %reduce-scatter.19.cloned.1.call-done = bf16[64,2048]{1,0:T(8,128)(2,1)} async-done(((bf16[256,2048]{1,0:T(8,128)(2,1)}), bf16[64,2048]{1,0:T(8,128)(2,1)}) %reduce-scatter.19.cloned.1.call-update) | async-done | bytes 262160 | tf_op jit(solution)/shard_map/reduce_scatter | solution.py:577
  985.4 70.4 %reduce-scatter.23.cloned.1.call-done = bf16[2,256,2048]{2,1,0:T(8,128)(2,1)} async-done(((bf16[2,1024,2048]{2,1,0:T(8,128)(2,1)}), bf16[2,256,2048]{2,1,0:T(8,128)(2,1)}) %reduce-scatter.23.cloned.1.call-update) | async-done | bytes 2097168 | tf_op jit(solution)/shard_map/reduce_scatter | solution.py:548
  1065.9 81.9 %reduce-scatter.11.cloned.1.call-done = bf16[128,2048]{1,0:T(8,128)(2,1)} async-done(((bf16[1024,2048]{1,0:T(8,128)(2,1)}), bf16[128,2048]{1,0:T(8,128)(2,1)}) %reduce-scatter.11.cloned.1.call-update) | async-done | bytes 524304 | tf_op jit(solution)/shard_map/reduce_scatter | solution.py:436
  1151.2 125.5 %reduce-scatter.25.cloned.1.call-done = f32[64,20]{1,0:T(8,128)} async-done(((f32[2048,20]{1,0:T(8,128)}), f32[64,20]{1,0:T(8,128)}) %reduce-scatter.25.cloned.1.call-update) | async-done | bytes 5136
  1279.6 130.0 %reduce-scatter.21.cloned.1.call-done = bf16[2,512,2048]{1,2,0:T(8,128)(2,1)} async-done(((bf16[2,2048,2048]{1,2,0:T(8,128)(2,1)}), bf16[2,512,2048]{1,2,0:T(8,128)(2,1)}) %reduce-scatter.21.cloned.1.call-update) | async-done | bytes 4194320 | tf_op jit(solution)/shard_map/reduce_scatter | solution.py:548
  1409.7 6.8 copy.103
  (191 shorter events, 108.0 us)
Async XLA Ops:
  7.2 40.8 %copy-start.31 = (bf16[64,16]{0,1:T(8,128)(2,1)S(1)}, bf16[64,16]{0,1:T(8,128)(2,1)}, u32[]{:S(2)}) copy-start(bf16[64,16]{0,1:T(8,128)(2,1)} %param.18) | copy-start | bytes 6148
  7.2 40.8 %copy-start.32 = (bf16[64,4]{0,1:T(4,128)(2,1)S(1)}, bf16[64,4]{0,1:T(4,128)(2,1)}, u32[]{:S(2)}) copy-start(bf16[64,4]{0,1:T(4,128)(2,1)} %param.15) | copy-start | bytes 1540
  7.2 122.6 %all-gather.25.cloned.1.call-start = ((), (), s32[]{:S(2)}) async-start(), calls=%async_computation.24 | async-start | bytes 4718592 | tf_op jit(solution)/shard_map/all_gather | solution.py:432
  7.9 125.0 %all-gather.13.cloned.1.call-start = ((), (), s32[]{:S(2)}) async-start(), calls=%async_computation.11 | async-start | bytes 3932160 | tf_op jit(solution)/shard_map/all_gather | solution.py:475
  8.0 108.2 %copy-start = (s32[1,1024]{1,0:T(1,128)S(1)}, s32[1,1024]{1,0:T(1,128)}, u32[]{:S(2)}) copy-start(s32[1,1024]{1,0:T(1,128)} %param.13) | copy-start | bytes 12292
  47.9 206.2 %all-gather.15.cloned.1.call-start = ((), (), s32[]{:S(2)}) async-start(), calls=%async_computation.12 | async-start | bytes 4718592 | tf_op jit(solution)/shard_map/all_gather | solution.py:513
  116.1 46.3 %copy-start.25 = (f32[4,128]{1,0:T(4,128)}, f32[4,128]{1,0:T(4,128)S(1)}, u32[]{:S(2)}) copy-start(f32[4,128]{1,0:T(4,128)S(1)} %mul.381) | copy-start | bytes 6148
  127.8 34.9 %copy-start.11 = (f32[1024,64]{0,1:T(8,128)}, f32[1024,64]{0,1:T(8,128)S(1)}, u32[]{:S(2)}) copy-start(f32[1024,64]{0,1:T(8,128)S(1)} %get-tuple-element.73) | copy-start | bytes 786436
  129.8 9.8 copy-start.21
  132.9 6.7 copy-start.29
  179.8 154.5 %all-gather.17.cloned.1.call-start = ((), (), s32[]{:S(2)}) async-start(), calls=%async_computation.13 | async-start | bytes 8650752 | tf_op jit(solution)/shard_map/all_gather | solution.py:480
  180.4 259.9 %all-gather.19.cloned.1.call-start = ((), (), s32[]{:S(2)}) async-start(), calls=%async_computation.14 | async-start | bytes 20971520 | tf_op jit(solution)/shard_map/all_gather | solution.py:481
  181.0 333.1 %all-gather.27.cloned.1.call-start = ((), (), s32[]{:S(2)}) async-start(), calls=%async_computation.25 | async-start | bytes 4718592 | tf_op jit(solution)/shard_map/all_gather | solution.py:432
  181.5 392.3 %all-gather.21.cloned.1.call-start = ((), (), s32[]{:S(2)}) async-start(), calls=%async_computation.15 | async-start | bytes 10485760 | tf_op jit(solution)/shard_map/all_gather | solution.py:482
  182.3 525.3 %reduce-scatter.13.cloned.1.call-start = ((), (), s32[]{:S(2)}) async-start(), calls=%async_computation.17 | async-start | bytes 4718592 | tf_op jit(solution)/shard_map/reduce_scatter | solution.py:436
  619.8 90.8 %copy-start.9 = (bf16[1,128,2048]{2,1,0:T(8,128)(2,1)S(1)}, bf16[1,128,2048]{2,1,0:T(8,128)(2,1)}, u32[]{:S(2)}) copy-start(bf16[1,128,2048]{2,1,0:T(8,128)(2,1)} %param.21) | copy-start | bytes 1572868
  619.8 93.4 %copy-start.27 = (f32[1,2,2,128]{3,2,1,0:T(2,128)S(1)}, f32[1,2,2,128]{3,2,1,0:T(2,128)}, u32[]{:S(2)}) copy-start(f32[1,2,2,128]{3,2,1,0:T(2,128)} %get-tuple-element.67) | copy-start | bytes 6148
  619.8 10.8 all-to-all-start.1
  625.2 159.8 %all-gather.23.cloned.1.call-start = ((), (), s32[]{:S(2)}) async-start(), calls=%async_computation.18 | async-start | bytes 4718592 | tf_op jit(solution)/shard_map/all_gather | solution.py:432
  712.9 200.2 %reduce-scatter.15.cloned.1.call-start = ((), (), s32[]{:S(2)}) async-start(), calls=%async_computation.19 | async-start | bytes 4718592 | tf_op jit(solution)/shard_map/reduce_scatter | solution.py:436
  796.0 19.7 %copy-start.24 = (f32[1024,2]{0,1:T(2,128)S(1)}, f32[1024,2]{0,1:T(2,128)}, u32[]{:S(2)}) copy-start(f32[1024,2]{0,1:T(2,128)} %copy-done.23) | copy-start | bytes 24580
  824.2 9.0 copy-start.13
  824.2 129.2 %reduce-scatter.17.cloned.1.call-start = ((), (), s32[]{:S(2)}) async-start(), calls=%async_computation.20 | async-start | bytes 3932160 | tf_op jit(solution)/shard_map/reduce_scatter | solution.py:607
  833.2 148.3 %reduce-scatter.19.cloned.1.call-start = ((), (), s32[]{:S(2)}) async-start(), calls=%async_computation.21 | async-start | bytes 1310720 | tf_op jit(solution)/shard_map/reduce_scatter | solution.py:577
  837.7 218.1 %reduce-scatter.23.cloned.1.call-start = ((), (), s32[]{:S(2)}) async-start(), calls=%async_computation.23 | async-start | bytes 10485760 | tf_op jit(solution)/shard_map/reduce_scatter | solution.py:548
  851.8 296.0 %reduce-scatter.11.cloned.1.call-start = ((), (), s32[]{:S(2)}) async-start(), calls=%async_computation.16 | async-start | bytes 4718592 | tf_op jit(solution)/shard_map/reduce_scatter | solution.py:436
  866.1 47.1 %copy-start.10 = (bf16[1,128,2048]{2,1,0:T(8,128)(2,1)S(1)}, bf16[1,128,2048]{2,1,0:T(8,128)(2,1)}, u32[]{:S(2)}) copy-start(bf16[1,128,2048]{2,1,0:T(8,128)(2,1)} %param.12) | copy-start | bytes 1572868
  866.1 410.6 %reduce-scatter.25.cloned.1.call-start = ((), (), s32[]{:S(2)}) async-start(), calls=%async_computation.26 | async-start | bytes 1081344
  916.1 493.6 %reduce-scatter.21.cloned.1.call-start = ((), (), s32[]{:S(2)}) async-start(), calls=%async_computation.22 | async-start | bytes 20971520 | tf_op jit(solution)/shard_map/reduce_scatter | solution.py:548
  953.4 107.4 %all-to-all-start.2 = ((bf16[8,64,768]{2,1,0:T(8,128)(2,1)}), bf16[8,64,768]{2,1,0:T(8,128)(2,1)}, u32[]{:S(2)}, u32[]{:S(2)}) async-start(bf16[8,64,768]{2,1,0:T(8,128)(2,1)} %bitcast.218), calls=%async_computation.6 | async-start | bytes 1572864 | tf_op jit(solution)/shard_map/all_to_all | solution.py:608
  981.4 78.5 %collective-permute-start = (bf16[64,2048]{1,0:T(8,128)(2,1)}, bf16[64,2048]{1,0:T(8,128)(2,1)S(1)}, u32[]{:S(2)}, u32[]{:S(2)}) collective-permute-start(bf16[64,2048]{1,0:T(8,128)(2,1)} %reduce-scatter.19.cloned.1.call-done), channel_id=1, source_target_pairs={{0,0},{1,4},{2,8},{3,12},{4,16},{5,20},{6,24},{7,28},{8,1},{9,5},{... | collective-permute-start | bytes 786440 | tf_op jit(solution)/shard_map/ppermute | solution.py:584
  1060.7 87.1 %copy-start.8 = (f32[128,2048]{1,0:T(8,128)S(1)}, f32[128,2048]{1,0:T(8,128)}, u32[]{:S(2)}) copy-start(f32[128,2048]{1,0:T(8,128)} %copy-done.7) | copy-start | bytes 3145732
  (21 other events, 40.6 us)
Sparse Core Ops, SparseCore 0:
  10.1 88.8 all-gather.24
  100.6 28.9 all-gather.12
  179.9 74.1 all-gather.14
  257.0 77.2 all-gather.16
  335.7 104.5 all-gather.18
  442.2 71.7 all-gather.26
  515.6 58.1 all-gather.20
  619.9 87.6 reduce-scatter.12
  713.0 71.9 all-gather.22
  824.3 88.8 reduce-scatter.14
  915.7 37.6 reduce-scatter.16
  956.5 24.8 reduce-scatter.18
  984.0 71.7 reduce-scatter.22
  1059.7 88.1 reduce-scatter.10
  1149.9 126.7 reduce-scatter.24
  1279.3 130.3 reduce-scatter.20

commit v2 on v1

--- a/solution.py
+++ b/solution.py
@@ -1,6 +1,8 @@
 import jax
 import jax.numpy as jnp
 from jax import lax
+from jax.experimental import pallas as pl
+from jax.experimental.pallas import tpu as pltpu
 from jax.sharding import PartitionSpec as P
 
 HEADS = 16
@@ -11,6 +13,7 @@
 EPSILON = 1e-05
 ROPE_BASE = 10000.0
 MASKED = -1e30
+LANES = 128
 
 
 def inverse_rms(values):
@@ -428,6 +431,672 @@
     )
 
 
+MESH = pl.DeviceIdType.MESH
+VMEM_LIMIT = 48 * 1024 * 1024
+
+
+def ring_place(device, n):
+    odd = device % 2
+    return (1 - odd) * (device // 2) + odd * (n - 1 - device // 2)
+
+
+def ring_device(place, n):
+    far = place // (n // 2)
+    return (1 - far) * (2 * place) + far * (2 * (n - 1 - place) + 1)
+
+
+class Ring:
+    def __init__(self, n):
+        self.n = n
+        self.me = lax.axis_index("ctx")
+        self.place = ring_place(self.me, n)
+
+    def at(self, offset):
+        return ring_device((self.place + offset + self.n) % self.n, self.n)
+
+    def hops(self, way, half):
+        return self.n // 2 if way == half else self.n // 2 - 1
+
+    def barrier(self, others):
+        semaphore = pltpu.get_barrier_semaphore()
+        for other in others:
+            pl.semaphore_signal(semaphore, inc=1, device_id=other, device_id_type=MESH)
+        pl.semaphore_wait(semaphore, len(others))
+
+    def neighbours(self):
+        return [{"ctx": self.at(1)}, {"ctx": self.at(-1)}]
+
+
+def remote(source, target, send, receive, device):
+    return pltpu.make_async_remote_copy(
+        src_ref=source,
+        dst_ref=target,
+        send_sem=send,
+        recv_sem=receive,
+        device_id=device,
+        device_id_type=MESH,
+    )
+
+
+def gather_steps(ring, source, place, send, receive, arrived=None, ready=None):
+    signs = (1, -1)
+
+    def copy(way, half, hop):
+        origin = ring.at(-signs[way] * hop)
+        spot = place(origin, half)
+        return remote(
+            source(half) if hop == 0 else spot,
+            spot,
+            send.at[way, half, hop],
+            receive.at[way, half, hop],
+            {"ctx": ring.at(signs[way])},
+        )
+
+    def landed(way, half, hop):
+        spot = place(ring.at(-signs[way] * (hop + 1)), half)
+        return remote(
+            spot,
+            spot,
+            send.at[way, half, hop],
+            receive.at[way, half, hop],
+            {"ctx": ring.at(signs[way])},
+        )
+
+    started = []
+    for half in (0, 1):
+        if ready is not None:
+            ready(half)
+        for way in (0, 1):
+            started.append(copy(way, half, 0))
+            started[-1].start()
+        yield
+    for hop in range(ring.n // 2):
+        for half in (0, 1):
+            for way in (0, 1):
+                if hop < ring.hops(way, half):
+                    landed(way, half, hop).wait_recv()
+                    if hop + 1 < ring.hops(way, half):
+                        started.append(copy(way, half, hop + 1))
+                        started[-1].start()
+                    if arrived is not None:
+                        arrived(way, half, hop, ring.at(-signs[way] * (hop + 1)))
+                    yield
+    for one in started:
+        one.wait_send()
+
+
+def scatter_steps(ring, part, slots, store, send, receive):
+    signs = (1, -1)
+
+    def copy(way, half, hop, source):
+        return remote(
+            source,
+            slots.at[way, half, hop],
+            send.at[way, half, hop],
+            receive.at[way, half, hop],
+            {"ctx": ring.at(signs[way])},
+        )
+
+    started = []
+    for half in (0, 1):
+        for way in (0, 1):
+            goal = ring.at(signs[way] * ring.hops(way, half))
+            started.append(copy(way, half, 0, part(goal, half)))
+            started[-1].start()
+        yield
+    for hop in range(ring.n // 2):
+        for half in (0, 1):
+            for way in (0, 1):
+                last = ring.hops(way, half) - 1
+                if hop <= last:
+                    slot = slots.at[way, half, hop]
+                    copy(way, half, hop, slot).wait_recv()
+                    if hop < last:
+                        goal = ring.at(signs[way] * (last - hop))
+                        slot[...] = (
+                            slot[...].astype(jnp.float32)
+                            + part(goal, half)[...].astype(jnp.float32)
+                        ).astype(slot.dtype)
+                        started.append(copy(way, half, hop + 1, slot))
+                        started[-1].start()
+                    yield
+    for half in (0, 1):
+        total = part(ring.me, half)[...].astype(jnp.float32)
+        for way in (0, 1):
+            total = total + slots[way, half, ring.hops(way, half) - 1].astype(jnp.float32)
+        store(half, total)
+    for one in started:
+        one.wait_send()
+
+
+def run_steps(*tasks):
+    tasks = list(tasks)
+    while tasks:
+        left = []
+        for task in tasks:
+            try:
+                next(task)
+                left.append(task)
+            except StopIteration:
+                pass
+        tasks = left
+
+
+def sems(*shape):
+    return pltpu.SemaphoreType.DMA(shape)
+
+
+def kernel_call(body, outs, in_specs, out_specs, scratch, identity, name, sent):
+    return pl.pallas_call(
+        body,
+        out_shape=outs,
+        in_specs=in_specs,
+        out_specs=out_specs,
+        scratch_shapes=scratch,
+        name=name,
+        cost_estimate=pl.CostEstimate(flops=0, bytes_accessed=sent, transcendentals=0),
+        compiler_params=pltpu.CompilerParams(
+            collective_id=identity, has_side_effects=True, vmem_limit_bytes=VMEM_LIMIT
+        ),
+    )
+
+
+ANY = pl.BlockSpec(memory_space=pl.ANY)
+VMEM = pl.BlockSpec(memory_space=pltpu.VMEM)
+
+
+def ring_gather(block, n, identity, name, axis=0):
+    rows, width = block.shape
+    half_rows = rows // 2
+    shape = (rows * n, width) if axis == 0 else (rows, width * n)
+
+    def body(block_ref, all_ref, send, receive, local):
+        ring = Ring(n)
+
+        def place(device, half):
+            if axis == 0:
+                return all_ref.at[pl.ds(pl.multiple_of(device * rows + half * half_rows, 16), half_rows)]
+            return all_ref.at[
+                pl.ds(half * half_rows, half_rows), pl.ds(pl.multiple_of(device * width, 128), width)
+            ]
+
+        whole = (
+            all_ref.at[pl.ds(pl.multiple_of(ring.me * rows, 16), rows)]
+            if axis == 0
+            else all_ref.at[:, pl.ds(pl.multiple_of(ring.me * width, 128), width)]
+        )
+        own = pltpu.make_async_copy(block_ref, whole, local)
+        own.start()
+        ring.barrier(ring.neighbours())
+        run_steps(
+            gather_steps(
+                ring,
+                lambda half: block_ref.at[pl.ds(half * half_rows, half_rows)],
+                place,
+                send,
+                receive,
+            )
+        )
+        own.wait()
+
+    return kernel_call(
+        body,
+        jax.ShapeDtypeStruct(shape, block.dtype),
+        [ANY],
+        ANY,
+        [sems(2, 2, n // 2), sems(2, 2, n // 2), pltpu.SemaphoreType.DMA],
+        identity,
+        name,
+        block.size * 2 * n * 32,
+    )(block)
+
+
+def ring_scatter(partial, n, identity, name):
+    rows, width = partial.shape[0] // n, partial.shape[1]
+    half_rows = rows // 2
+
+    def body(part_ref, sum_ref, slots, send, receive):
+        ring = Ring(n)
+        ring.barrier(ring.neighbours())
+
+        def part(device, half):
+            return part_ref.at[pl.ds(pl.multiple_of(device * rows + half * half_rows, 16), half_rows)]
+
+        def store(half, total):
+            sum_ref[pl.ds(half * half_rows, half_rows)] = total
+
+        run_steps(scatter_steps(ring, part, slots, store, send, receive))
+
+    return kernel_call(
+        body,
+        jax.ShapeDtypeStruct((rows, width), jnp.float32),
+        [VMEM],
+        VMEM,
+        [
+            pltpu.VMEM((2, 2, n // 2, half_rows, width), partial.dtype),
+            sems(2, 2, n // 2),
+            sems(2, 2, n // 2),
+        ],
+        identity,
+        name,
+        partial.size * 2 * 32,
+    )(partial)
+
+
+def direct_exchange(blocks, n, identity, name):
+    def body(block_ref, got_ref, send, receive):
+        me = lax.axis_index("ctx")
+        ring = Ring(n)
+        ring.barrier([{"ctx": (me + k) % n} for k in range(1, n)])
+        got_ref[me] = block_ref[me]
+        copies = []
+        for k in range(1, n):
+            other = (me + k) % n
+            copies.append(
+                remote(
+                    block_ref.at[other],
+                    got_ref.at[me],
+                    send.at[k - 1],
+                    receive.at[k - 1],
+                    {"ctx": other},
+                )
+            )
+            copies[-1].start()
+        for k in range(1, n):
+            spot = got_ref.at[(me - k + n) % n]
+            remote(
+                spot, spot, send.at[k - 1], receive.at[k - 1], {"ctx": (me + k) % n}
+            ).wait_recv()
+        for copy in copies:
+            copy.wait_send()
+
+    return kernel_call(
+        body,
+        jax.ShapeDtypeStruct(blocks.shape, blocks.dtype),
+        [VMEM],
+        VMEM,
+        [sems(n - 1), sems(n - 1)],
+        identity,
+        name,
+        blocks.size * 64,
+    )(blocks)
+
+
+def partners():
+    dp = lax.axis_index("dp")
+    core = dp + 1 - 2 * (dp % 2)
+    chip = (dp + 2) % 4
+    return dp, core, chip, (core + 2) % 4
+
+
+def gather_inputs(tokens, named, in_blocks, out_rows, n, n_dp, identity):
+    tok_rows, width = tokens.shape
+    weight_rows, in_width = in_blocks.shape[1:]
+
+    def body(
+        token_ref,
+        named_ref,
+        in_ref,
+        out_ref,
+        token_all,
+        named_all,
+        in_all,
+        out_all,
+        token_send,
+        token_receive,
+        out_send,
+        out_receive,
+        core_send,
+        core_receive,
+        own_send,
+        own_receive,
+        named_send,
+        named_receive,
+        in_send,
+        in_receive,
+        pass_send,
+        pass_receive,
+        local,
+    ):
+        ring = Ring(n)
+        me = ring.me
+        dp, core, chip, core_chip = partners()
+        half_rows = tok_rows // 2
+
+        def token_place(device, half):
+            return token_all.at[
+                pl.ds(pl.multiple_of(device * tok_rows + half * half_rows, 16), half_rows)
+            ]
+
+        def out_place(group, device):
+            return out_all.at[
+                pl.ds(pl.multiple_of((group * n + device) * weight_rows, 16), weight_rows)
+            ]
+
+        locals_ = [
+            pltpu.make_async_copy(in_ref.at[me], in_all.at[dp, me], local.at[0]),
+            pltpu.make_async_copy(
+                token_ref,
+                token_all.at[pl.ds(pl.multiple_of(me * tok_rows, 16), tok_rows)],
+                local.at[1],
+            ),
+            pltpu.make_async_copy(named_ref, named_all.at[me], local.at[2]),
+            pltpu.make_async_copy(out_ref, out_place(dp, me), local.at[3]),
+        ]
+        for copy in locals_:
+            copy.start()
+        others = [(me + k) % n for k in range(1, n)]
+        ring.barrier([{"ctx": other} for other in others] + [{"dp": core}, {"dp": chip}])
+
+        out_copies = [
+            remote(out_ref, out_place(dp, me), own_send.at[0], own_receive.at[0], {"dp": chip}),
+            remote(out_ref, out_place(dp, me), own_send.at[1], own_receive.at[1], {"dp": core}),
+        ]
+        for copy in out_copies:
+            copy.start()
+        direct = []
+        for k, other in enumerate(others):
+            direct.append(
+                remote(in_ref.at[other], in_all.at[dp, me], in_send.at[k], in_receive.at[k], {"ctx": other})
+            )
+            direct.append(
+                remote(named_ref, named_all.at[me], named_send.at[k], named_receive.at[k], {"ctx": other})
+            )
+        for copy in direct:
+            copy.start()
+
+        def out_ready(half):
+            if half == 1:
+                spot = out_place(chip, me)
+                remote(spot, spot, own_send.at[0], own_receive.at[0], {"dp": chip}).wait_recv()
+                out_copies.append(
+                    remote(spot, spot, own_send.at[2], own_receive.at[2], {"dp": core})
+                )
+                out_copies[-1].start()
+
+        def out_arrived(way, half, hop, origin):
+            spot = out_place(chip if half else dp, origin)
+            out_copies.append(
+                remote(
+                    spot,
+                    spot,
+                    core_send.at[way, half, hop],
+                    core_receive.at[way, half, hop],
+                    {"dp": core},
+                )
+            )
+            out_copies[-1].start()
+
+        def in_steps():
+            for _ in range(2):
+                yield
+            for k in range(1, n):
+                spot = in_all.at[dp, (me - k + n) % n]
+                remote(
+                    spot, spot, in_send.at[k - 1], in_receive.at[k - 1], {"ctx": others[k - 1]}
+                ).wait_recv()
+            locals_[0].wait()
+            passed = []
+            for at, to in ((0, chip), (1, core)):
+                passed.append(
+                    remote(
+                        in_all.at[dp], in_all.at[dp], pass_send.at[at], pass_receive.at[at], {"dp": to}
+                    )
+                )
+                passed[-1].start()
+            for _ in range(6):
+                yield
+            spot = in_all.at[chip]
+            remote(spot, spot, pass_send.at[0], pass_receive.at[0], {"dp": chip}).wait_recv()
+            passed.append(
+                remote(spot, spot, pass_send.at[2], pass_receive.at[2], {"dp": core})
+            )
+            passed[-1].start()
+            for _ in range(6):
+                yield
+            for at, source in ((1, core), (2, core_chip)):
+                spot = in_all.at[source]
+                remote(
+                    spot, spot, pass_send.at[at], pass_receive.at[at], {"dp": core}
+                ).wait_recv()
+            for copy in passed:
+                copy.wait_send()
+
+        run_steps(
+            gather_steps(
+                ring,
+                lambda half: token_ref.at[pl.ds(half * half_rows, half_rows)],
+                token_place,
+                token_send,
+                token_receive,
+            ),
+            gather_steps(
+                ring,
+                lambda half: out_place(chip, me) if half else out_ref,
+                lambda device, half: out_place(chip if half else dp, device),
+                out_send,
+                out_receive,
+                out_arrived,
+                out_ready,
+            ),
+            in_steps(),
+        )
+        for k in range(1, n):
+            spot = named_all.at[(me - k + n) % n]
+            remote(
+                spot, spot, named_send.at[k - 1], named_receive.at[k - 1], {"ctx": others[k - 1]}
+            ).wait_recv()
+        for at, group in ((1, core), (2, core_chip)):
+            spot = out_place(group, me)
+            remote(spot, spot, own_send.at[at], own_receive.at[at], {"dp": core}).wait_recv()
+        for way, sign in ((0, 1), (1, -1)):
+            for half in (0, 1):
+                for hop in range(ring.hops(way, half)):
+                    spot = out_place(core_chip if half else core, ring.at(-sign * (hop + 1)))
+                    remote(
+                        spot,
+                        spot,
+                        core_send.at[way, half, hop],
+                        core_receive.at[way, half, hop],
+                        {"dp": core},
+                    ).wait_recv()
+        for copy in direct + out_copies:
+            copy.wait_send()
+        for copy in locals_[1:]:
+            copy.wait()
+
+    return kernel_call(
+        body,
+        (
+            jax.ShapeDtypeStruct((tok_rows * n, width), tokens.dtype),
+            jax.ShapeDtypeStruct((n,) + named.shape, named.dtype),
+            jax.ShapeDtypeStruct((n_dp,) + in_blocks.shape, in_blocks.dtype),
+            jax.ShapeDtypeStruct((weight_rows * n * n_dp, out_rows.shape[1]), out_rows.dtype),
+        ),
+        [ANY] * 4,
+        (ANY,) * 4,
+        [sems(2, 2, n // 2)] * 6
+        + [sems(3)] * 2
+        + [sems(n - 1)] * 4
+        + [sems(3)] * 2
+        + [sems(4)],
+        identity,
+        "gather_inputs",
+        300_000_000,
+    )(tokens, named, in_blocks, out_rows)
+
+
+def scatter_end(row_part, in_part, out_part, n, identity):
+    rows, width = row_part.shape[0] // n, row_part.shape[1]
+    half_rows = rows // 2
+    f32 = jnp.float32
+
+    def body(
+        row_ref,
+        in_ref,
+        out_ref,
+        row_sum,
+        in_got,
+        out_sum,
+        slots,
+        in_core,
+        in_chip,
+        out_core,
+        out_chip,
+        row_send,
+        row_receive,
+        pass_send,
+        pass_receive,
+        in_send,
+        in_receive,
+    ):
+        ring = Ring(n)
+        me = ring.me
+        dp, core, chip, core_chip = partners()
+        others = [(me + k) % n for k in range(1, n)]
+        ring.barrier([{"ctx": other} for other in others] + [{"dp": core}, {"dp": chip}])
+
+        def part(device, half):
+            return row_ref.at[pl.ds(pl.multiple_of(device * rows + half * half_rows, 16), half_rows)]
+
+        def store(half, total):
+            row_sum[pl.ds(half * half_rows, half_rows)] = total
+
+        def passing(at, source, target, to):
+            return remote(source, target, pass_send.at[at], pass_receive.at[at], {"dp": to})
+
+        def weight_steps():
+            passed = [
+                passing(0, in_ref.at[core_chip], in_core.at[1], core),
+                passing(1, out_ref.at[core_chip], out_core.at[1], core),
+                passing(2, in_ref.at[core], in_core.at[0], core),
+                passing(3, out_ref.at[core], out_core.at[0], core),
+            ]
+            for copy in passed:
+                copy.start()
+            yield
+            passed[0].wait_recv()
+
+            def add_far(k, carry):
+                in_core[1, k] = (in_core[1, k].astype(f32) + in_ref[chip, k].astype(f32)).astype(in_ref.dtype)
+                return carry
+
+            lax.fori_loop(0, n, add_far, 0)
+            passed.append(passing(4, in_core.at[1], in_chip, chip))
+            passed[-1].start()
+            passed[1].wait_recv()
+            out_core[1] = (out_core[1].astype(f32) + out_ref[chip].astype(f32)).astype(out_ref.dtype)
+            passed.append(passing(5, out_core.at[1], out_chip, chip))
+            passed[-1].start()
+            for _ in range(4):
+                yield
+            passed[2].wait_recv()
+            passed[3].wait_recv()
+            passed[4].wait_recv()
+
+            def add_near(k, carry):
+                in_core[0, k] = (
+                    in_core[0, k].astype(f32) + in_ref[dp, k].astype(f32) + in_chip[k].astype(f32)
+                ).astype(in_ref.dtype)
+                return carry
+
+            lax.fori_loop(0, n, add_near, 0)
+            direct = []
+            for k, other in enumerate(others):
+                direct.append(
+                    remote(in_core.at[0, other], in_got.at[me], in_send.at[k], in_receive.at[k], {"ctx": other})
+                )
+                direct[-1].start()
+            in_got[me] = in_core[0, me]
+            passed[5].wait_recv()
+            out_sum[...] = (
+                out_core[0].astype(f32) + out_ref[dp].astype(f32) + out_chip[...].astype(f32)
+            ).astype(out_ref.dtype)
+            for _ in range(8):
+                yield
+            for k in range(1, n):
+                spot = in_got.at[(me - k + n) % n]
+                remote(
+                    spot, spot, in_send.at[k - 1], in_receive.at[k - 1], {"ctx": others[k - 1]}
+                ).wait_recv()
+            for copy in passed + direct:
+                copy.wait_send()
+
+        run_steps(scatter_steps(ring, part, slots, store, row_send, row_receive), weight_steps())
+
+    return kernel_call(
+        body,
+        (
+            jax.ShapeDtypeStruct((rows, width), f32),
+            jax.ShapeDtypeStruct(in_part.shape[1:], in_part.dtype),
+            jax.ShapeDtypeStruct(out_part.shape[1:], out_part.dtype),
+        ),
+        [VMEM] * 3,
+        (VMEM,) * 3,
+        [
+            pltpu.VMEM((2, 2, n // 2, half_rows, width), row_part.dtype),
+            pltpu.VMEM((2,) + in_part.shape[1:], in_part.dtype),
+            pltpu.VMEM(in_part.shape[1:], in_part.dtype),
+            pltpu.VMEM((2,) + out_part.shape[1:], out_part.dtype),
+            pltpu.VMEM(out_part.shape[1:], out_part.dtype),
+            sems(2, 2, n // 2),
+            sems(2, 2, n // 2),
+            sems(6),
+            sems(6),
+            sems(n - 1),
+            sems(n - 1),
+        ],
+        identity,
+        "scatter_end",
+        200_000_000,
+    )(row_part, in_part, out_part)
+
+
+def small_scatter(parts, n, n_dp, identity):
+    def body(part_ref, sum_ref, got, send, receive):
+        me, dp = lax.axis_index("ctx"), lax.axis_index("dp")
+        flat = dp * n + me
+        count = n * n_dp
+        semaphore = pltpu.get_barrier_semaphore()
+
+        def spot(at):
+            return (at // n, at % n)
+
+        for k in range(1, count):
+            pl.semaphore_signal(
+                semaphore, inc=1, device_id=spot((flat + k) % count), device_id_type=MESH
+            )
+        pl.semaphore_wait(semaphore, count - 1)
+        copies = []
+        for k in range(1, count):
+            to = (flat + k) % count
+            copies.append(
+                remote(
+                    part_ref.at[to // n, to % n], got.at[k], send.at[k], receive.at[k], spot(to)
+                )
+            )
+            copies[-1].start()
+        total = part_ref[dp, me]
+        for k in range(1, count):
+            copies[k - 1].wait_recv()
+            total = total + got[k]
+        sum_ref[...] = total
+        for copy in copies:
+            copy.wait_send()
+
+    shape = parts.shape[2:]
+    return kernel_call(
+        body,
+        jax.ShapeDtypeStruct(shape, parts.dtype),
+        [VMEM],
+        VMEM,
+        [pltpu.VMEM((n * n_dp,) + shape, parts.dtype), sems(n * n_dp), sems(n * n_dp)],
+        identity,
+        "small_scatter",
+        40_000_000,
+    )(parts)
+
+
 def gather_ctx(block):
     return lax.all_gather(block, "ctx", axis=0, tiled=True)
 
@@ -466,20 +1135,37 @@
     def own(array, size, axis=0):
         return lax.dynamic_slice_in_dim(array, me * size, size, axis)
 
-    token_all = gather_ctx(tokens[0])
-    upstream_all = gather_ctx(cotangent[0])
-    route_all = gather_ctx(routes[0])
+    named = jnp.any(routes[0][..., None] == jnp.arange(LANES, dtype=jnp.int32), axis=1).astype(bf16)
+    small = jnp.concatenate(
+        [norm_gains, router_weight, jnp.zeros((weight_rows, LANES - 4 - expert_count), bf16)], axis=1
+    )
     in_blocks = project_in.reshape(weight_rows, 3, n, cols).transpose(2, 0, 1, 3)
-    in_blocks = in_blocks.reshape(n, weight_rows, 3 * cols)
-    in_blocks = lax.all_to_all(in_blocks, "ctx", split_axis=0, concat_axis=0, tiled=True)
-    in_own = lax.all_gather(in_blocks, "dp", axis=0, tiled=True).reshape(width, 3 * cols)
-    small = jnp.concatenate([norm_gains, router_weight], axis=1)
-    small_all = lax.all_gather(small, ("dp", "ctx"), axis=0, tiled=True)
+    in_blocks = jnp.concatenate(
+        [
+            in_blocks.reshape(n, weight_rows, 3 * cols),
+            jnp.broadcast_to(small[None], (n, weight_rows, LANES)),
+        ],
+        axis=2,
+    )
+    token_all, named_all, in_all, out_all = gather_inputs(
+        tokens[0], named, in_blocks, project_out, n, n_dp, 1
+    )
+    named_all = named_all.reshape(rows, LANES)[:, :expert_count] > 0
+    in_all = in_all.reshape(width, 3 * cols + LANES)
+    in_own, small_all = in_all[:, : 3 * cols], in_all[:, 3 * cols :]
     gains = small_all[:, :4].astype(f32)
-    router_all = small_all[:, 4:]
-    out_all = lax.all_gather(project_out, ("dp", "ctx"), axis=0, tiled=True)
+    router_all = small_all[:, 4 : 4 + expert_count]
     first = lax.all_gather(expert_in, "dp", axis=1, tiled=True)
     second = lax.all_gather(expert_out, "dp", axis=1, tiled=True)
+    upstream_all = gather_ctx(cotangent[0])
+
+    def sum_ctx(values):
+        shape = values.shape
+        block = values.reshape(-1, LANES)
+        got = direct_exchange(
+            jnp.broadcast_to(block[None], (n,) + block.shape), n, 2, "exchange"
+        )
+        return jnp.sum(got, axis=0).reshape(shape)
 
     places = dealt_positions(jnp.arange(rows, dtype=jnp.int32), tok_rows, n)
     document_row = document_ids[0]
@@ -493,7 +1179,7 @@
     attend_in = (inputs * attend_inverse * gains[:, 0]).astype(bf16)
     projected = jnp.dot(attend_in, in_own, preferred_element_type=f32)
     raw = projected[:, : 2 * cols].reshape(rows, 2, cols)
-    squares = lax.psum(jnp.sum(raw * raw, axis=-1), "ctx")
+    squares = sum_ctx(jnp.sum(raw * raw, axis=-1))
     inverse = lax.rsqrt(squares / width + EPSILON)[..., None]
     normed = raw * inverse
     pair_gains = own(gains, cols)[:, 1:3].T
@@ -510,17 +1196,14 @@
     probs = (powers / total).astype(bf16)
     attend_out = jnp.einsum("htk,khd->thd", probs, value, preferred_element_type=f32)
     attend_low = attend_out.reshape(rows, cols).astype(bf16)
-    attend_all = lax.all_gather(attend_low, "ctx", axis=1, tiled=True)
+    attend_all = ring_gather(attend_low, n, 3, "gather_attention", axis=1)
 
     residual = inputs + jnp.dot(attend_all, out_all, preferred_element_type=f32)
     mixed_inverse = inverse_rms(residual)
     mixed_low = (residual * mixed_inverse * gains[:, 3]).astype(bf16)
     logits = jnp.dot(mixed_low, router_all, preferred_element_type=f32)
-    named = jnp.any(
-        route_all[..., None] == jnp.arange(expert_count, dtype=jnp.int32), axis=1
-    )
-    chosen = jnp.where(named, logits, MASKED)
-    chosen = jnp.where(named, jnp.exp(chosen - jnp.max(chosen, axis=-1, keepdims=True)), 0.0)
+    chosen = jnp.where(named_all, logits, MASKED)
+    chosen = jnp.where(named_all, jnp.exp(chosen - jnp.max(chosen, axis=-1, keepdims=True)), 0.0)
     gates = chosen / jnp.sum(chosen, axis=-1, keepdims=True)
     gate_own = own(gates, local_experts, 1).T[..., None]
 
@@ -544,16 +1227,23 @@
     ).astype(bf16)
     second_back = jnp.einsum("xtf,td->xfd", hidden_gated, upstream_all, preferred_element_type=f32)
     first_back = jnp.einsum("td,xtf->xdf", mixed_low, up_back, preferred_element_type=f32)
+    first_back, second_back, up_back = lax.optimization_barrier(
+        (first_back.astype(bf16), second_back.astype(bf16), up_back)
+    )
     expert_in_gradient, expert_out_gradient = (
-        lax.psum_scatter(part.astype(bf16), "dp", scatter_dimension=1, tiled=True).astype(f32)
+        lax.psum_scatter(part, "dp", scatter_dimension=1, tiled=True).astype(f32)
         for part in (first_back, second_back)
     )
-    mixed_back = scatter_ctx(
-        jnp.einsum("xtf,xdf->td", up_back, first, preferred_element_type=f32)
-    )
-    gate_back = lax.all_to_all(
-        gate_back.reshape(local_experts, n, tok_rows), "ctx", split_axis=1, concat_axis=0, tiled=True
-    ).reshape(expert_count, tok_rows).T
+    mixed_back = ring_scatter(
+        jnp.einsum("xtf,xdf->td", up_back, first, preferred_element_type=f32).astype(bf16),
+        n,
+        4,
+        "scatter_rows",
+    )
+    gate_blocks = gate_back.reshape(local_experts, n, tok_rows).transpose(1, 0, 2)
+    gate_blocks = jnp.pad(gate_blocks, ((0, 0), (0, 2 * rows // LANES - local_experts), (0, 0)))
+    gate_back = direct_exchange(gate_blocks, n, 2, "exchange")[:, :local_experts]
+    gate_back = gate_back.reshape(expert_count, tok_rows).T
 
     own_gates = own(gates, tok_rows)
     own_mixed = own(mixed_low, tok_rows)
@@ -571,17 +1261,9 @@
     residual_back = cotangent[0].astype(f32) + normalize_back(
         mixed_back * gains[:, 3], own_mixed_normed, own_mixed_inverse
     )
-    back_all = gather_ctx(residual_back.astype(bf16))
+    back_all = ring_gather(residual_back.astype(bf16), n, 5, "gather_back")
 
     out_part = jnp.einsum("td,te->de", attend_low, back_all, preferred_element_type=f32)
-    out_part = lax.psum_scatter(
-        out_part.astype(bf16), "dp", scatter_dimension=0, tiled=True
-    )
-    pairs = []
-    for d in range(n_dp):
-        for c in range(n):
-            pairs.append((d * n + c, c * n_dp + d))
-    project_out_gradient = lax.ppermute(out_part, ("dp", "ctx"), pairs).astype(f32)
     attend_back = jnp.einsum(
         "td,ed->te", back_all, own(out_all, cols), preferred_element_type=f32
     ).astype(bf16).reshape(rows, own_heads, HEAD_DIM)
@@ -595,19 +1277,23 @@
     pair_back = rotate(pair_back, cosine, -sine).reshape(rows, 2, cols)
     pair_gain_back = jnp.sum(pair_back * normed, axis=0)
     pair_back = pair_back * pair_gains
-    means = lax.psum(jnp.sum(pair_back * normed, axis=-1), "ctx")[..., None] / width
+    means = sum_ctx(jnp.sum(pair_back * normed, axis=-1))[..., None] / width
     pair_back = inverse * (pair_back - normed * means)
     raw_back = jnp.concatenate(
         [pair_back.reshape(rows, 2 * cols), value_back.reshape(rows, cols)], axis=-1
     ).astype(bf16)
-    attend_in_back = scatter_ctx(
-        jnp.einsum("tf,df->td", raw_back, in_own, preferred_element_type=f32)
-    )
-    in_part = jnp.einsum("td,tf->df", attend_in, raw_back, preferred_element_type=f32)
-    in_part = lax.psum_scatter(in_part.astype(bf16), "dp", scatter_dimension=0, tiled=True)
-    in_part = lax.all_to_all(
-        in_part.reshape(n, weight_rows, 3 * cols), "ctx", split_axis=0, concat_axis=0, tiled=True
-    ).reshape(n, weight_rows, 3, cols)
+    row_part = jnp.einsum("tf,df->td", raw_back, in_own, preferred_element_type=f32).astype(bf16)
+    in_part = jnp.einsum("td,tf->df", attend_in, raw_back, preferred_element_type=f32).astype(bf16)
+    attend_in_back, in_part, out_part = scatter_end(
+        row_part,
+        in_part.reshape(n_dp, n, weight_rows, 3 * cols),
+        out_part.astype(bf16).reshape(n_dp, weight_rows, width),
+        n,
+        6,
+    )
+    pairs = [(d * n + c, c * n_dp + d) for d in range(n_dp) for c in range(n)]
+    project_out_gradient = lax.ppermute(out_part, ("dp", "ctx"), pairs).astype(f32)
+    in_part = in_part.reshape(n, weight_rows, 3, cols)
     project_in_gradient = in_part.transpose(1, 2, 0, 3).reshape(weight_rows, 3 * width).astype(f32)
 
     own_inverse = own(attend_inverse, tok_rows)
@@ -622,9 +1308,15 @@
     small_part = jnp.concatenate(
         [attend_gain_back[:, None], pair_columns, mixed_gain_back[:, None], router_part], axis=1
     )
-    small_gradient = lax.psum_scatter(
-        small_part, ("dp", "ctx"), scatter_dimension=0, tiled=True
-    )
+    small_width = small_part.shape[1]
+    small_rows = -(-weight_rows * small_width // (8 * LANES)) * 8
+    small_part = jnp.pad(
+        small_part.reshape(n_dp * n, weight_rows * small_width),
+        ((0, 0), (0, small_rows * LANES - weight_rows * small_width)),
+    )
+    small_gradient = small_scatter(small_part.reshape(n_dp, n, small_rows, LANES), n, n_dp, 7)
+    small_gradient = small_gradient.reshape(-1)[: weight_rows * small_width]
+    small_gradient = small_gradient.reshape(weight_rows, small_width)
     return (
         layer_output[None],
         tokens_back.astype(bf16)[None],
@@ -638,7 +1330,8 @@
 
 
 def solution(mesh):
-    split_heads = HEADS % mesh.shape["ctx"] == 0
+    n = mesh.shape["ctx"]
+    split_heads = HEADS % n == 0 and n % 4 == 0 and mesh.shape["dp"] == 4
     placed = (
         P("dp", "ctx", None),
         P("dp", None),

time: 1430 us -> 706 us (0.49)
  waiting for transfers between devices: 967 us -> 2.64 us
  Pallas kernels: 0 us -> 395 us
  blocking collectives: 166 us -> 0 us
  local copies, waits for them, and re-layouts: 44.3 us -> 59.7 us
    pallas_call x0 -> x9, Pallas kernels: none -> 395 us  [the longest x2 110 us: ring_gather(): kernel_call(body, jax.ShapeDtypeStruct(shape, block.dtype), [ANY], ANY, [...]
    reduce_scatter x4 -> x2, waiting for transfers between devices: 236 us -> 0.01 us  [heads_local(): lax.psum_scatter(part, 'dp', scatter_dimension=1, tiled=True).astype(f32)]
    reduce_scatter x3 -> x1, waiting for transfers between devices: 204 us -> 0.01 us  [scatter_ctx(): lax.psum_scatter(partial.astype(jnp.bfloat16), 'ctx', scatter_dimension=0...]
    all_gather x3 -> x0, waiting for transfers between devices: 127 us -> none  [the longest x1 80.2 us: heads_local(): out_all = lax.all_gather(project_out, ('dp', 'ctx'), axis=0, tiled=True)]
    unnamed x17 -> x6, waiting for transfers between devices: 129 us -> 2.61 us
    all_gather x3 -> x1, waiting for transfers between devices: 122 us -> 0.01 us  [gather_ctx(): return lax.all_gather(block, 'ctx', axis=0, tiled=True)]
    all_gather x2 -> x0, blocking collectives: 91.8 us -> none  [the longest x1 67.2 us: heads_local(): small_all = lax.all_gather(small, ('dp', 'ctx'), axis=0, tiled=True)]
    all_gather x1, waiting for transfers between devices: 83.9 us -> 0.01 us  [heads_local(): first = lax.all_gather(expert_in, 'dp', axis=1, tiled=True)]
  transfers between devices with their start and end apart: 19 -> 7, of which waited for: 15 -> 0; matrix products, arithmetic and copies ran while one was open for 10% -> 32% of each run, Pallas kernels for 0% -> 57%
where the time goes in v2:
time: 706 us; the launch traced here: 695 us
  Pallas kernels  395 us (56%)
  matrix products  178 us (25%)
  local copies, waits for them, and re-layouts  59.7 us (8%)
  other arithmetic  41.8 us (6%)
  between operations  15.5 us (2%)
    pallas_call x2, Pallas kernels, ring_gather(): kernel_call(body, jax.ShapeDtypeStruct(shape, block.dtype), [ANY], ANY, [...  110 us
    pallas_call x1, Pallas kernels, gather_inputs(): kernel_call(body, (jax.ShapeDtypeStruct((tok_rows * n, width), tokens.dty...  109 us
    pallas_call x1, Pallas kernels, scatter_end(): kernel_call(body, (jax.ShapeDtypeStruct((rows, width), f32), jax.ShapeDty...  85.9 us
    pallas_call x1, Pallas kernels, ring_scatter(): kernel_call(body, jax.ShapeDtypeStruct((rows, width), jnp.float32), [VMEM...  51 us
    unnamed x111, local copies, waits for them, and re-layouts  28.6 us
    dot_general x1, matrix products, heads_local(): jnp.einsum('td,xtf->xdf', mixed_low, up_back, preferred_element_type=f32)  24.8 us
    dot_general x1, matrix products, heads_local(): jnp.einsum('td,xdf->xtf', mixed_low, first, preferred_element_type=f32)  23.5 us
    dot_general x1, matrix products, heads_local(): jnp.einsum('xtf,xdf->td', up_back, first, preferred_element_type=f32)  23 us
  transfers between devices with their start and end apart: 7, of which 0 were waited for; matrix products, arithmetic and copies ran while one was open for 32% of the time, Pallas kernels for 57%

profile of v2, /device:TPU:1, one launch (start us, length us, event | category | flops | bytes accessed | tf_op | source)
XLA Modules:
  0.0 694.7 jit_solution(5939678023012830226)
XLA Ops:
  12.0 109.5 %gather_inputs.1 = (bf16[1024,2048]{1,0:T(8,128)(2,1)}, bf16[8,128,128]{2,1,0:T(8,128)(2,1)S(1)}, bf16[4,8,64,896]{3,2,1,0:T(8,128)(2,1)S(1)}, bf16[2048,2048]{1,0:T(8,128)(2,1)}) custom-call(bf16[128,2048]{1,0:T(8,128)(2,1)S(1)} %bitcast.195, bf16[128,128]{1,0:T(8,128)(2,1)S(1)} %convert_element_type.122.named_ref, ...), custom_call_target="tpu_custom_call" | custom-call | bytes 300000000 | tf_op jit(solution)/shard_map/gather_inputs/pallas_call | solution.py:908
  121.5 4.4 fusion.1
  126.8 6.6 fusion.16
  135.7 4.5 gather_fusion
  140.4 4.5 gather_fusion.1
  150.1 10.7 %exchange.3 = f32[8,16,128]{2,1,0:T(8,128)S(1)} custom-call(f32[8,16,128]{2,1,0:T(8,128)S(1)} %broadcast_in_dim.100.block_ref), custom_call_target="tpu_custom_call" | custom-call | bytes 1048576 | tf_op jit(solution)/shard_map/exchange/pallas_call | solution.py:713
  168.4 6.4 fusion.61
  174.8 4.9 divide_convert_fusion
  182.2 69.7 %gather_attention.1 = bf16[1024,2048]{1,0:T(8,128)(2,1)S(1)} custom-call(bf16[1024,256]{1,0:T(8,128)(2,1)S(1)} %copy.174.block_ref), custom_call_target="tpu_custom_call" | custom-call | bytes 134217728 | tf_op jit(solution)/shard_map/gather_attention/pallas_call | solution.py:642
  253.9 13.4 %multiply_reduce_fusion = (f32[1024]{0:T(1024)S(1)}, f32[1024,2048]{1,0:T(8,128)S(1)}) fusion(bf16[1024,2048]{1,0:T(8,128)(2,1)} %copy-done.3, bf16[2048,2048]{1,0:T(8,128)(2,1)} %get-tuple-element.21, bf16[1024,2048]{1,0:T(8,128)(2,1)} %get-tuple-element.19), kind=kOutput, calls=%fused_computation.23 | convolution fusion | flops 8598322176 | bytes 25169920 | tf_op jit(solution)/shard_map/dot_general | solution.py:1201
  275.8 23.5 %convolution_bitcast_fusion = f32[2,1024,2048]{2,1,0:T(8,128)} fusion(bf16[2,2048,2048]{2,1,0:T(8,128)(2,1)} %all-gather.5.cloned.1.call-done, bf16[1024,2048]{1,0:T(8,128)(2,1)} %copy-done.12), kind=kOutput, calls=%fused_computation.28 | convolution fusion | flops 17179869184 | bytes 37748736 | tf_op jit(solution)/shard_map/td,xdf->xtf/dot_general | solution.py:1210
  299.3 21.4 %multiply_convert_fusion.2 = (bf16[2,1024,1024]{2,1,0:T(8,128)(2,1)}, bf16[2,1024,1024]{2,1,0:T(8,128)(2,1)}, f32[2,1024]{1,0:T(2,128)S(1)}, bf16[2,1024,1024]{2,1,0:T(8,128)(2,1)}) fusion(f32[2,1024,2048]{2,1,0:T(8,128)} %convolution_bitcast_fusion, f32[2,1024]{1,0:T(2,128)S(1)} %dynamic-slice_bitcast_fusion, ...), kind=kOutput, calls=%fused_computation.18 | convolution fusion | flops 8633972736 | bytes 41959424 | tf_op jit(solution)/shard_map/td,xfd->xtf/dot_general | solution.py:1221
  320.7 13.8 %bitcast_convert_fusion.1 = bf16[1024,2048]{1,0:T(8,128)(2,1)} fusion(bf16[2,1024,1024]{2,1,0:T(8,128)(2,1)} %get-tuple-element.76, bf16[2,1024,2048]{2,1,0:T(8,128)(2,1)} %all-gather.7.cloned.1.call-done), kind=kOutput, calls=%fused_computation.15 | convolution fusion | flops 8592031744 | bytes 16777216 | tf_op jit(solution)/shard_map/xtf,xfd->td/dot_general | solution.py:1216
  334.6 8.1 %pad_maximum_fusion = bf16[2,1024,2048]{2,1,0:T(8,128)(2,1)} fusion(bf16[2,1024,1024]{2,1,0:T(8,128)(2,1)} %get-tuple-element.74, bf16[2,1024,1024]{2,1,0:T(8,128)(2,1)} %get-tuple-element.73), kind=kLoop, calls=%fused_computation.10 | loop fusion | flops 16777216 | bytes 16777216 | tf_op jit(solution)/shard_map/concatenate | solution.py:1225
  342.8 14.4 %convolution_convert_fusion = bf16[2,1024,2048]{2,1,0:T(8,128)(2,1)} fusion(bf16[2,1024,1024]{2,1,0:T(8,128)(2,1)} %get-tuple-element.76, bf16[1,1024,2048]{2,1,0:T(8,128)(2,1)} %all-gather.9.cloned.1.call-done), kind=kOutput, calls=%fused_computation.30 | convolution fusion | flops 8594128896 | bytes 16777216 | tf_op jit(solution)/shard_map/xtf,td->xfd/dot_general | solution.py:1228
  357.2 24.8 %convert_bitcast_fusion = bf16[2,2048,2048]{1,2,0:T(8,128)(2,1)} fusion(bf16[1024,2048]{1,0:T(8,128)(2,1)} %copy-done.12, bf16[2,1024,1024]{2,1,0:T(8,128)(2,1)} %get-tuple-element.74, bf16[2,1024,1024]{2,1,0:T(8,128)(2,1)} %get-tuple-element.73), kind=kOutput, calls=%fused_computation.3 | convolution fusion | flops 17205035008 | bytes 29360128 | tf_op jit(solution)/shard_map/td,xtf->xdf/dot_general | solution.py:1229
  383.6 5.5 exchange.4
  389.1 23.0 %bitcast_convert_fusion.part_ref = bf16[1024,2048]{1,0:T(8,128)(2,1)S(1)} fusion(bf16[2,1024,2048]{2,1,0:T(8,128)(2,1)} %pad_maximum_fusion, bf16[2,2048,2048]{2,1,0:T(8,128)(2,1)} %all-gather.5.cloned.1.call-done), kind=kOutput, calls=%fused_computation.11 | convolution fusion | flops 17181966336 | bytes 29360128 | tf_op jit(solution)/shard_map/xtf,xdf->td/dot_general | solution.py:1238
  412.2 51.0 %scatter_rows.1 = f32[128,2048]{1,0:T(8,128)S(1)} custom-call(bf16[1024,2048]{1,0:T(8,128)(2,1)S(1)} %bitcast_convert_fusion.part_ref), custom_call_target="tpu_custom_call" | custom-call | bytes 134217728 | tf_op jit(solution)/shard_map/scatter_rows/pallas_call | solution.py:670
  469.3 40.7 %gather_back.1 = bf16[1024,2048]{1,0:T(8,128)(2,1)S(1)} custom-call(bf16[128,2048]{1,0:T(8,128)(2,1)S(1)} %fusion.59.block_ref), custom_call_target="tpu_custom_call" | custom-call | bytes 134217728 | tf_op jit(solution)/shard_map/gather_back/pallas_call | solution.py:642
  510.1 3.5 fusion.25
  524.7 5.4 exchange.5
  532.7 3.5 fusion.22
  536.3 4.0 convolution_convert_fusion.4
  543.1 5.1 convolution_convert_fusion.1.row_ref
  548.2 5.7 convolution_convert_fusion.2
  553.8 85.9 %scatter_end.1 = (f32[128,2048]{1,0:T(8,128)S(1)}, bf16[8,64,768]{2,1,0:T(8,128)(2,1)S(1)}, bf16[64,2048]{1,0:T(8,128)(2,1)S(1)}) custom-call(bf16[1024,2048]{1,0:T(8,128)(2,1)} %convolution_convert_fusion.1.row_ref, bf16[4,8,64,768]{3,2,1,0:T(8,128)(2,1)} %bitcast.215, bf16[4,64,2048]{2,1,0:T(8,128)(2,1)S(1)} %bitcast.196), custom_call_target="tpu_custom_call" | custom-call | bytes 200000000 | tf_op jit(solution)/shard_map/scatter_end/pallas_call | solution.py:1027
  648.2 16.1 %small_scatter.1 = f32[16,128]{1,0:T(8,128)S(1)} custom-call(f32[4,8,16,128]{3,2,1,0:T(8,128)S(1)} %copy.185), custom_call_target="tpu_custom_call" | custom-call | bytes 40000000 | tf_op jit(solution)/shard_map/small_scatter/pallas_call | solution.py:1088
  667.7 2.6 copy.152
  673.7 2.8 fusion.30
  676.5 4.1 convert_element_type.159
  680.6 6.8 copy.155
  (221 shorter events, 72.6 us)
Async XLA Ops:
  7.2 2.9 copy-start.30
  7.2 268.6 %all-gather.5.cloned.1.call-start = ((), (), s32[]{:S(2)}) async-start(), calls=%async_computation.3 | async-start | bytes 20971520 | tf_op jit(solution)/shard_map/all_gather | solution.py:1158
  7.9 291.4 %all-gather.9.cloned.1.call-start = ((), (), s32[]{:S(2)}) async-start(), calls=%async_computation.8 | async-start | bytes 4718592 | tf_op jit(solution)/shard_map/all_gather | solution.py:1101
  8.7 290.6 %all-gather.7.cloned.1.call-start = ((), (), s32[]{:S(2)}) async-start(), calls=%async_computation.4 | async-start | bytes 10485760 | tf_op jit(solution)/shard_map/all_gather | solution.py:1159
  9.4 664.2 %reduce-scatter.4.cloned.1.call-start = ((), (), s32[]{:S(2)}) async-start(), calls=%async_computation.5 | async-start | bytes 4718592 | tf_op jit(solution)/shard_map/reduce_scatter | solution.py:1105
  121.5 4.4 copy-start.4
  125.9 7.6 %copy-start.46 = (f32[1024]{0:T(1024)}, f32[1024]{0:T(1024)S(1)}, u32[]{:S(2)}) copy-start(f32[1024]{0:T(1024)S(1)} %add_rsqrt_fusion.2) | copy-start | bytes 12292
  126.2 141.1 %copy-start.33 = (f32[2048,1]{0,1:T(1,128)}, f32[2048,1]{0,1:T(1,128)S(1)}, u32[]{:S(2)}) copy-start(f32[2048,1]{0,1:T(1,128)S(1)} %get-tuple-element.89) | copy-start | bytes 24580
  135.1 44.5 %copy-start.18 = (bf16[1024,256]{0,1:T(8,128)(2,1)}, bf16[1024,256]{0,1:T(8,128)(2,1)S(1)}, u32[]{:S(2)}) copy-start(bf16[1024,256]{0,1:T(8,128)(2,1)S(1)} %slice.185) | copy-start | bytes 1572868
  140.4 25.3 %slice-start = ((f32[1024,768]{0,1:T(8,128)}), f32[1024,512]{0,1:T(8,128)S(1)}, s32[]{:S(2)}) async-start(f32[1024,768]{0,1:T(8,128)} %copy-done.10), calls=%async_computation.9 | async-start | bytes 4194304 | tf_op jit(solution)/shard_map/slice | solution.py:1181
  145.8 20.2 %copy-start.40 = (f32[4,128]{1,0:T(4,128)}, f32[4,128]{1,0:T(4,128)S(1)}, u32[]{:S(2)}) copy-start(f32[4,128]{1,0:T(4,128)S(1)} %mul.381) | copy-start | bytes 6148
  167.2 7.6 %copy-start.16 = (bf16[1024,4,128]{2,0,1:T(8,128)(2,1)}, bf16[1024,4,128]{2,0,1:T(8,128)(2,1)S(1)}, u32[]{:S(2)}) copy-start(bf16[1024,4,128]{2,0,1:T(8,128)(2,1)S(1)} %copy.133) | copy-start | bytes 3145732
  181.8 85.5 %copy-start.25 = (bf16[1024,2,128]{0,2,1:T(8,128)(2,1)}, bf16[1024,2,128]{0,2,1:T(8,128)(2,1)S(1)}, u32[]{:S(2)}) copy-start(bf16[1024,2,128]{0,2,1:T(8,128)(2,1)S(1)} %get-tuple-element.96) | copy-start | bytes 1572868
  267.3 3.4 copy-start.13
  334.6 341.9 %reduce-scatter.8.cloned.1.call-start = ((), (), s32[]{:S(2)}) async-start(), calls=%async_computation.7 | async-start | bytes 10485760 | tf_op jit(solution)/shard_map/reduce_scatter | solution.py:1234
  382.1 298.5 %reduce-scatter.6.cloned.1.call-start = ((), (), s32[]{:S(2)}) async-start(), calls=%async_computation.6 | async-start | bytes 20971520 | tf_op jit(solution)/shard_map/reduce_scatter | solution.py:1234
  412.2 52.4 %copy-start.34 = (f32[2048,1]{0,1:T(1,128)S(1)}, f32[2048,1]{0,1:T(1,128)}, u32[]{:S(2)}) copy-start(f32[2048,1]{0,1:T(1,128)} %copy-done.33) | copy-start | bytes 24580
  412.2 55.6 %copy-start.20 = (bf16[1,128,2048]{2,1,0:T(8,128)(2,1)S(1)}, bf16[1,128,2048]{2,1,0:T(8,128)(2,1)}, u32[]{:S(2)}) copy-start(bf16[1,128,2048]{2,1,0:T(8,128)(2,1)} %param.21) | copy-start | bytes 1572868
  466.8 43.3 %copy-start.28 = (f32[2,128,1024]{2,1,0:T(8,128)S(1)}, f32[2,128,1024]{2,1,0:T(8,128)}, u32[]{:S(2)}) copy-start(f32[2,128,1024]{2,1,0:T(8,128)} %get-tuple-element.97) | copy-start | bytes 3145732
  510.0 6.3 copy-start.1
  510.0 4.9 copy-start.9
  510.0 5.0 copy-start.19
  513.5 2.8 copy-start.24
  518.8 2.7 copy-start.11
  521.5 11.2 %copy-start.37 = (f32[1024,2]{0,1:T(2,128)S(1)}, f32[1024,2]{0,1:T(2,128)}, u32[]{:S(2)}) copy-start(f32[1024,2]{0,1:T(2,128)} %copy-done.36) | copy-start | bytes 24580
  536.3 4.0 copy-start.26
  536.3 4.0 copy-start.2
  540.3 2.7 copy-start.29
  543.1 5.1 copy-start.21
  543.1 5.1 copy-start.39
  639.7 32.2 %collective-permute-start = (bf16[64,2048]{1,0:T(8,128)(2,1)S(1)}, bf16[64,2048]{1,0:T(8,128)(2,1)}, u32[]{:S(2)}, u32[]{:S(2)}) collective-permute-start(bf16[64,2048]{1,0:T(8,128)(2,1)S(1)} %get-tuple-element.26), channel_id=1, source_target_pairs={{0,0},{1,4},{2,8},{3,12},{4,16},{5,20},{6,24},{7,28},{8,1},{9,5},{... | collective-permute-start | bytes 786440 | tf_op jit(solution)/shard_map/ppermute | solution.py:1295
  667.7 6.0 copy-start.15
  (25 other events, 42.5 us)
Sparse Core Ops, SparseCore 0:
  9.6 128.0 all-gather.4
  139.9 95.0 all-gather.8
  236.6 60.8 all-gather.6
  334.7 91.6 reduce-scatter.3
  429.0 75.9 reduce-scatter.7
  507.4 153.3 reduce-scatter.5

commit v3 on v2

--- a/solution.py
+++ b/solution.py
@@ -1097,6 +1097,612 @@
     )(parts)
 
 
+def slot_offsets(n):
+    offsets = [0]
+    for k in range(1, n // 2):
+        offsets += [k, -k]
+    return offsets + [n // 2]
+
+
+def slot_of(offset, n):
+    if abs(offset) == n // 2:
+        return n - 1
+    return 2 * offset - 1 if offset > 0 else -2 * offset
+
+
+def slot_gather_steps(ring, first, slots, send, receive):
+    signs = (1, -1)
+    half_rows = slots.shape[1] // 2
+
+    def copy(way, half, hop):
+        rows = pl.ds(half * half_rows, half_rows)
+        held = slot_of(-signs[way] * hop, ring.n)
+        return remote(
+            first.at[rows] if hop == 0 else slots.at[held, rows],
+            slots.at[slot_of(-signs[way] * (hop + 1), ring.n), rows],
+            send.at[way, half, hop],
+            receive.at[way, half, hop],
+            {"ctx": ring.at(signs[way])},
+        )
+
+    started = []
+    for half in (0, 1):
+        for way in (0, 1):
+            started.append(copy(way, half, 0))
+            started[-1].start()
+    yield
+    for hop in range(ring.n // 2):
+        for half in (0, 1):
+            for way in (0, 1):
+                if hop < ring.hops(way, half):
+                    copy(way, half, hop).wait_recv()
+                    if hop + 1 < ring.hops(way, half):
+                        started.append(copy(way, half, hop + 1))
+                        started[-1].start()
+                    yield
+    for one in started:
+        one.wait_send()
+
+
+def advance(steps, count):
+    for _ in range(count):
+        next(steps, None)
+
+
+def dot(a, b):
+    return jnp.dot(a, b, preferred_element_type=jnp.float32)
+
+
+def dot_across(a, b):
+    return lax.dot_general(a, b, (((1,), (1,)), ((), ())), preferred_element_type=jnp.float32)
+
+
+def experts_in(
+    attend_all, token_all, cotangent, out_all, first, second, gain, router, named, n, identity
+):
+    tok_rows, width = cotangent.shape
+    local_experts, ff = first.shape[0], second.shape[0] // first.shape[0]
+    rows = tok_rows * n
+    pair = 2 * tok_rows
+    part = 4 * tok_rows
+    tile, wide = 256, 512
+    bf16, f32 = jnp.bfloat16, jnp.float32
+    offsets = slot_offsets(n)
+
+    def body(
+        attend_ref,
+        token_ref,
+        back_ref,
+        out_ref,
+        first_ref,
+        second_ref,
+        gain_ref,
+        router_ref,
+        named_ref,
+        back_all,
+        mixed_all,
+        gated_all,
+        up_all,
+        own_gates,
+        gate_back,
+        own_residual,
+        out_s,
+        first_s,
+        second_s,
+        mixed_s,
+        back_s,
+        attend_s,
+        token_s,
+        residual_s,
+        gate_s,
+        sum_s,
+        send,
+        receive,
+        load,
+        weight_load,
+        save,
+        local,
+    ):
+        ring = Ring(n)
+        lanes = lax.broadcasted_iota(jnp.int32, (pair, LANES), 1)
+        part_lanes = lax.broadcasted_iota(jnp.int32, (part, LANES), 1)
+        loads = [pltpu.make_async_copy(out_ref, out_s, weight_load.at[0])]
+        for x in range(local_experts):
+            loads.append(pltpu.make_async_copy(first_ref.at[x], first_s.at[x], weight_load.at[1 + x]))
+        loads.append(pltpu.make_async_copy(second_ref, second_s, weight_load.at[1 + local_experts]))
+
+        def row_loads(j):
+            copies = []
+            for k in range(2):
+                device = ring.at(offsets[2 * j + k])
+                source = pl.ds(pl.multiple_of(device * tok_rows, 16), tok_rows)
+                target = pl.ds(k * tok_rows, tok_rows)
+                for at, (array, held) in enumerate(((attend_ref, attend_s), (token_ref, token_s))):
+                    copies.append(
+                        pltpu.make_async_copy(
+                            array.at[source], held.at[j % 2, target], load.at[j % 2, k, at]
+                        )
+                    )
+            return copies
+
+        pending = row_loads(0)
+        for copy in pending:
+            copy.start()
+        loads[0].start()
+        own = pltpu.make_async_copy(back_ref, back_s.at[0], local)
+        own.start()
+        ring.barrier(ring.neighbours())
+        steps = slot_gather_steps(ring, back_ref, back_s, send, receive)
+        advance(steps, 1)
+        loads[0].wait()
+        for copy in loads[1:]:
+            copy.start()
+
+        saves = []
+        for j in range(n // 2):
+            for copy in pending:
+                copy.wait()
+            if j + 1 < n // 2:
+                pending = row_loads(j + 1)
+                for copy in pending:
+                    copy.start()
+
+            def project(t, carry, j=j):
+                columns = pl.ds(pl.multiple_of(t * wide, wide), wide)
+                residual_s[:, columns] = token_s[j % 2, :, columns].astype(f32) + dot(
+                    attend_s[j % 2], out_s[:, columns]
+                )
+                return carry
+
+            lax.fori_loop(0, width // wide, project, 0)
+            residual = residual_s[...]
+            if j == 0:
+                own_residual[...] = residual[:tok_rows]
+            inverse = lax.rsqrt(jnp.mean(residual * residual, axis=-1, keepdims=True) + EPSILON)
+            mixed = (residual * inverse * gain_ref[0:1, :]).astype(bf16)
+            for k in range(2):
+                mixed_s[2 * j + k] = mixed[k * tok_rows : (k + 1) * tok_rows]
+            logits = dot(mixed, router_ref[...])
+            marks = jnp.concatenate(
+                [
+                    named_ref[pl.ds(pl.multiple_of(ring.at(offsets[2 * j + k]) * tok_rows, 16), tok_rows)]
+                    for k in range(2)
+                ],
+                axis=0,
+            ).astype(f32)
+            logits = jnp.where(marks > 0, logits, MASKED)
+            powers = jnp.where(
+                marks > 0, jnp.exp(logits - jnp.max(logits, axis=-1, keepdims=True)), 0.0
+            )
+            gates = powers / jnp.sum(powers, axis=-1, keepdims=True)
+            if j == 0:
+                own_gates[...] = gates[:tok_rows]
+            held = jnp.zeros((pair, LANES), f32)
+            for x in range(local_experts):
+                mine = jnp.sum(
+                    jnp.where(lanes == ring.me * local_experts + x, gates, 0.0), axis=-1, keepdims=True
+                )
+                held = jnp.where(lanes == x, mine, held)
+            gate_s[pl.ds(j * pair, pair)] = held
+            saves.append(
+                pltpu.make_async_copy(
+                    mixed_s.at[pl.ds(2 * j, 2)], mixed_all.at[pl.ds(2 * j, 2)], save.at[j]
+                )
+            )
+            saves[-1].start()
+            advance(steps, 2)
+
+        counts = rows // part
+        outgoing = []
+        base = n // 2
+        for s in range(counts):
+            slots = pl.ds(s * 4, 4)
+            part_rows = pl.ds(s * part, part)
+            advance(steps, 8 if s < counts - 1 else 64)
+            if s == 0:
+                own.wait()
+            sum_s[part_rows] = jnp.zeros((part, LANES), f32)
+            for copy in outgoing:
+                copy.wait()
+            outgoing = []
+            for x in range(local_experts):
+                if s == 0:
+                    loads[1 + x].wait()
+                    if x == 0:
+                        loads[1 + local_experts].wait()
+
+                def hidden(t, carry, s=s, x=x, slots=slots, part_rows=part_rows):
+                    at = pl.multiple_of(t * tile, tile)
+                    mixed = mixed_s[slots].reshape(part, width)
+                    back = back_s[slots].reshape(part, width)
+                    gate_part = dot(mixed, first_s[x, :, pl.ds(at, tile)])
+                    up_part = dot(mixed, first_s[x, :, pl.ds(pl.multiple_of(ff + at, tile), tile)])
+                    hidden_back = dot_across(
+                        back, second_s[pl.ds(pl.multiple_of(x * ff + at, tile), tile), :]
+                    )
+                    gate = gate_s[part_rows, x : x + 1]
+                    sigmoid = jax.nn.sigmoid(gate_part)
+                    swish = gate_part * sigmoid
+                    value = swish * up_part
+                    out_s[pl.ds(0, part), pl.ds(pl.multiple_of(x * ff + at, tile), tile)] = (
+                        value * gate
+                    ).astype(bf16)
+                    sums = jnp.sum(value * hidden_back, axis=-1, keepdims=True)
+                    sum_s[part_rows] = sum_s[part_rows] + jnp.where(part_lanes == x, sums, 0.0)
+                    hidden_back = hidden_back * gate
+                    slope = sigmoid * (1.0 + gate_part * (1.0 - sigmoid))
+                    up_rows = pl.ds((1 + x) * part, part)
+                    out_s[up_rows, pl.ds(at, tile)] = (hidden_back * up_part * slope).astype(bf16)
+                    out_s[up_rows, pl.ds(pl.multiple_of(ff + at, tile), tile)] = (
+                        hidden_back * swish
+                    ).astype(bf16)
+                    return carry
+
+                quarters = ff // tile
+                lax.fori_loop(0, quarters // 2, hidden, 0)
+                advance(steps, 2)
+                lax.fori_loop(quarters // 2, quarters, hidden, 0)
+                advance(steps, 2)
+                outgoing.append(
+                    pltpu.make_async_copy(
+                        out_s.at[pl.ds((1 + x) * part, part)],
+                        up_all.at[x, part_rows],
+                        save.at[base + 1 + x],
+                    )
+                )
+                outgoing[-1].start()
+            outgoing.append(
+                pltpu.make_async_copy(out_s.at[pl.ds(0, part)], gated_all.at[part_rows], save.at[base])
+            )
+            outgoing[-1].start()
+        spread = pltpu.make_async_copy(back_s, back_all, local)
+        spread.start()
+        for k in range(n):
+            gate_back[k] = jnp.transpose(sum_s[pl.ds(k * tok_rows, tok_rows)])[:8]
+        for copy in saves + outgoing:
+            copy.wait()
+        spread.wait()
+
+    return pl.pallas_call(
+        body,
+        out_shape=(
+            jax.ShapeDtypeStruct((n, tok_rows, width), bf16),
+            jax.ShapeDtypeStruct((n, tok_rows, width), bf16),
+            jax.ShapeDtypeStruct((rows, local_experts * ff), bf16),
+            jax.ShapeDtypeStruct((local_experts, rows, 2 * ff), bf16),
+            jax.ShapeDtypeStruct((tok_rows, LANES), f32),
+            jax.ShapeDtypeStruct((n, 8, LANES), f32),
+            jax.ShapeDtypeStruct((tok_rows, width), f32),
+        ),
+        in_specs=[ANY] * 6 + [VMEM] * 3,
+        out_specs=(ANY,) * 4 + (VMEM,) * 3,
+        scratch_shapes=[
+            pltpu.VMEM(out_all.shape, bf16),
+            pltpu.VMEM(first.shape, bf16),
+            pltpu.VMEM(second.shape, bf16),
+            pltpu.VMEM((n, tok_rows, width), bf16),
+            pltpu.VMEM((n, tok_rows, width), bf16),
+            pltpu.VMEM((2, pair, width), bf16),
+            pltpu.VMEM((2, pair, width), bf16),
+            pltpu.VMEM((pair, width), f32),
+            pltpu.VMEM((rows, LANES), f32),
+            pltpu.VMEM((rows, LANES), f32),
+            sems(2, 2, n // 2),
+            sems(2, 2, n // 2),
+            sems(2, 2, 2),
+            sems(2 + local_experts),
+            sems(n // 2 + 1 + local_experts),
+            pltpu.SemaphoreType.DMA,
+        ],
+        name="experts_in",
+        cost_estimate=pl.CostEstimate(
+            flops=2 * rows * width * (width + 3 * ff * local_experts),
+            bytes_accessed=60_000_000,
+            transcendentals=0,
+        ),
+        compiler_params=pltpu.CompilerParams(
+            collective_id=identity, has_side_effects=True, vmem_limit_bytes=BIG_VMEM
+        ),
+    )(attend_all, token_all, cotangent, out_all, first, second, gain, router, named)
+
+
+BIG_VMEM = 60 * 1024 * 1024
+
+
+def slot_scatter_steps(ring, parts, slots, store, send, receive, need):
+    signs = (1, -1)
+    half_rows = parts.shape[1] // 2
+    f32 = jnp.float32
+
+    def part(offset, half):
+        return parts.at[slot_of(offset, ring.n), pl.ds(half * half_rows, half_rows)]
+
+    def copy(way, half, hop, source):
+        return remote(
+            source,
+            slots.at[way, half, hop],
+            send.at[way, half, hop],
+            receive.at[way, half, hop],
+            {"ctx": ring.at(signs[way])},
+        )
+
+    started = []
+    firsts = [(way, half) for half in (0, 1) for way in (0, 1)]
+    firsts.sort(key=lambda one: -slot_of(signs[one[0]] * ring.hops(*one), ring.n))
+    for way, half in firsts:
+        goal = signs[way] * ring.hops(way, half)
+        need(slot_of(goal, ring.n))
+        started.append(copy(way, half, 0, part(goal, half)))
+        started[-1].start()
+    for hop in range(ring.n // 2):
+        for way, half in firsts:
+            last = ring.hops(way, half) - 1
+            if hop <= last:
+                slot = slots.at[way, half, hop]
+                if hop < last:
+                    goal = signs[way] * (last - hop)
+                    need(slot_of(goal, ring.n))
+                copy(way, half, hop, slot).wait_recv()
+                if hop < last:
+                    slot[...] = (
+                        slot[...].astype(f32) + part(goal, half)[...].astype(f32)
+                    ).astype(slot.dtype)
+                    started.append(copy(way, half, hop + 1, slot))
+                    started[-1].start()
+                yield
+    need(0)
+    for half in (0, 1):
+        total = part(0, half)[...].astype(f32)
+        for way in (0, 1):
+            total = total + slots[way, half, ring.hops(way, half) - 1].astype(f32)
+        store(half, total)
+    for one in started:
+        one.wait_send()
+
+
+def experts_out(up_all, gated_all, first, second, gate_back, n, identity):
+    local_experts, rows, inner = up_all.shape
+    width = first.shape[1]
+    tok_rows = rows // n
+    half_rows = tok_rows // 2
+    pair = 2 * tok_rows
+    wide = 512
+    count = width // wide
+    bf16, f32 = jnp.bfloat16, jnp.float32
+    offsets = slot_offsets(n)
+
+    def body(
+        up_ref,
+        gated_ref,
+        first_ref,
+        second_ref,
+        gate_ref,
+        row_sum,
+        result_all,
+        gate_got,
+        first_s,
+        second_s,
+        up_s,
+        gated_s,
+        part_s,
+        result_s,
+        slots,
+        send,
+        receive,
+        gate_send,
+        gate_receive,
+        load,
+        first_load,
+        other_load,
+        save,
+    ):
+        ring = Ring(n)
+
+        def up_load(j):
+            return pltpu.make_async_copy(
+                up_ref.at[:, pl.ds(j * pair, pair)], up_s.at[:, pl.ds(j * pair, pair)], load.at[j]
+            )
+
+        def weight_load(t):
+            return pltpu.make_async_copy(
+                first_ref.at[:, pl.ds(t * wide, wide)],
+                first_s.at[:, pl.ds(t * wide, wide)],
+                first_load.at[t],
+            )
+
+        groups = n // 2
+        up_load(groups - 1).start()
+        for t in range(count):
+            weight_load(t).start()
+        for j in range(groups - 1):
+            up_load(groups - 2 - j).start()
+        others = [
+            pltpu.make_async_copy(gated_ref, gated_s, other_load.at[0]),
+            pltpu.make_async_copy(second_ref, second_s, other_load.at[1]),
+        ]
+        for copy in others:
+            copy.start()
+        ring.barrier([{"ctx": ring.at(k)} for k in range(1, n)])
+        gate_copies = []
+        for k in range(1, n):
+            offset = k if k <= n // 2 else k - n
+            back = -offset if offset < n // 2 else offset
+            gate_copies.append(
+                remote(
+                    gate_ref.at[slot_of(offset, n)],
+                    gate_got.at[slot_of(back, n)],
+                    gate_send.at[slot_of(back, n)],
+                    gate_receive.at[slot_of(back, n)],
+                    {"ctx": ring.at(k)},
+                )
+            )
+            gate_copies[-1].start()
+        gate_got[0] = gate_ref[0]
+
+        done = set()
+
+        def product(j):
+            rows_j = pl.ds(j * pair, pair)
+            up_load(j).wait()
+
+            def columns(t):
+                at = pl.ds(pl.multiple_of(t * wide, wide), wide)
+                value = dot_across(up_s[0, rows_j], first_s[0, at, :])
+                for x in range(1, local_experts):
+                    value = value + dot_across(up_s[x, rows_j], first_s[x, at, :])
+                value = value.astype(bf16)
+                for k in range(2):
+                    part_s[2 * j + k, :, at] = value[k * tok_rows : (k + 1) * tok_rows]
+
+            if not done:
+                for t in range(count):
+                    weight_load(t).wait()
+                    columns(t)
+            else:
+
+                def step(t, carry):
+                    columns(t)
+                    return carry
+
+                lax.fori_loop(0, count, step, 0)
+            done.add(j)
+
+        def need(slot):
+            if slot // 2 not in done:
+                product(slot // 2)
+
+        def store(half, total):
+            row_sum[pl.ds(half * half_rows, half_rows)] = total
+
+        steps = slot_scatter_steps(ring, part_s, slots, store, send, receive, need)
+        for j in reversed(range(groups)):
+            need(2 * j)
+            advance(steps, 3)
+        for copy in others:
+            copy.wait()
+        saves = []
+        chunk = 2
+        for j in range(n // chunk):
+            rows_j = pl.ds(j * chunk * tok_rows, chunk * tok_rows)
+
+            def result(t, carry, rows_j=rows_j, j=j):
+                at = pl.ds(pl.multiple_of(t * wide, wide), wide)
+                value = dot(gated_s[rows_j], second_s[:, at]).astype(bf16)
+                for k in range(chunk):
+                    result_s[chunk * j + k, :, at] = value[k * tok_rows : (k + 1) * tok_rows]
+                return carry
+
+            lax.fori_loop(0, count, result, 0)
+            for k in range(chunk):
+                slot = chunk * j + k
+                device = ring.at(offsets[slot])
+                saves.append(
+                    pltpu.make_async_copy(
+                        result_s.at[slot],
+                        result_all.at[pl.ds(pl.multiple_of(device * tok_rows, 16), tok_rows)],
+                        save.at[slot],
+                    )
+                )
+                saves[-1].start()
+            advance(steps, 2)
+        advance(steps, 64)
+        for copy in saves:
+            copy.wait()
+        for copy in gate_copies:
+            copy.wait()
+
+    return pl.pallas_call(
+        body,
+        out_shape=(
+            jax.ShapeDtypeStruct((tok_rows, width), f32),
+            jax.ShapeDtypeStruct((rows, width), bf16),
+            jax.ShapeDtypeStruct(gate_back.shape, f32),
+        ),
+        in_specs=[ANY] * 4 + [VMEM],
+        out_specs=(VMEM, ANY, VMEM),
+        scratch_shapes=[
+            pltpu.VMEM(first.shape, bf16),
+            pltpu.VMEM(second.shape, bf16),
+            pltpu.VMEM(up_all.shape, bf16),
+            pltpu.VMEM(gated_all.shape, bf16),
+            pltpu.VMEM((n, tok_rows, width), bf16),
+            pltpu.VMEM((n, tok_rows, width), bf16),
+            pltpu.VMEM((2, 2, n // 2, half_rows, width), bf16),
+            sems(2, 2, n // 2),
+            sems(2, 2, n // 2),
+            sems(n),
+            sems(n),
+            sems(n // 2),
+            sems(count),
+            sems(2),
+            sems(n),
+        ],
+        name="experts_out",
+        cost_estimate=pl.CostEstimate(
+            flops=2 * rows * width * 3 * inner // 2 * local_experts,
+            bytes_accessed=60_000_000,
+            transcendentals=0,
+        ),
+        compiler_params=pltpu.CompilerParams(
+            collective_id=identity, has_side_effects=True, vmem_limit_bytes=BIG_VMEM
+        ),
+    )(up_all, gated_all, first, second, gate_back)
+
+
+def gather_and_scatter(block, partial, n, identity):
+    rows, width = block.shape
+    half_rows = rows // 2
+
+    def body(block_ref, part_ref, all_ref, sum_ref, slots, send, receive, sum_send, sum_receive, local):
+        ring = Ring(n)
+
+        def half_of(ref, device, half):
+            return ref.at[pl.ds(pl.multiple_of(device * rows + half * half_rows, 16), half_rows)]
+
+        def store(half, total):
+            sum_ref[pl.ds(half * half_rows, half_rows)] = total
+
+        own = pltpu.make_async_copy(
+            block_ref, all_ref.at[pl.ds(pl.multiple_of(ring.me * rows, 16), rows)], local
+        )
+        own.start()
+        ring.barrier(ring.neighbours())
+        run_steps(
+            gather_steps(
+                ring,
+                lambda half: block_ref.at[pl.ds(half * half_rows, half_rows)],
+                lambda device, half: half_of(all_ref, device, half),
+                send,
+                receive,
+            ),
+            scatter_steps(
+                ring,
+                lambda device, half: half_of(part_ref, device, half),
+                slots,
+                store,
+                sum_send,
+                sum_receive,
+            ),
+        )
+        own.wait()
+
+    return kernel_call(
+        body,
+        (
+            jax.ShapeDtypeStruct((rows * n, width), block.dtype),
+            jax.ShapeDtypeStruct((rows, width), jnp.float32),
+        ),
+        [ANY, VMEM],
+        (ANY, VMEM),
+        [pltpu.VMEM((2, 2, n // 2, half_rows, width), partial.dtype)]
+        + [sems(2, 2, n // 2)] * 4
+        + [pltpu.SemaphoreType.DMA],
+        identity,
+        "gather_and_scatter",
+        200_000_000,
+    )(block, partial)
+
+
 def gather_ctx(block):
     return lax.all_gather(block, "ctx", axis=0, tiled=True)
 
@@ -1150,14 +1756,14 @@
     token_all, named_all, in_all, out_all = gather_inputs(
         tokens[0], named, in_blocks, project_out, n, n_dp, 1
     )
-    named_all = named_all.reshape(rows, LANES)[:, :expert_count] > 0
+    named_all = named_all.reshape(rows, LANES)
     in_all = in_all.reshape(width, 3 * cols + LANES)
     in_own, small_all = in_all[:, : 3 * cols], in_all[:, 3 * cols :]
     gains = small_all[:, :4].astype(f32)
     router_all = small_all[:, 4 : 4 + expert_count]
+    router_wide = jnp.pad(router_all, ((0, 0), (0, LANES - expert_count)))
     first = lax.all_gather(expert_in, "dp", axis=1, tiled=True)
-    second = lax.all_gather(expert_out, "dp", axis=1, tiled=True)
-    upstream_all = gather_ctx(cotangent[0])
+    second = lax.all_gather(expert_out, "dp", axis=1, tiled=True).reshape(local_experts * FF, width)
 
     def sum_ctx(values):
         shape = values.shape
@@ -1167,10 +1773,16 @@
         )
         return jnp.sum(got, axis=0).reshape(shape)
 
-    places = dealt_positions(jnp.arange(rows, dtype=jnp.int32), tok_rows, n)
+    half_rows = tok_rows // 2
+
+    def dealt(row):
+        blocks = row.reshape(2 * n, half_rows)
+        return jnp.stack([blocks[:n], blocks[n:][::-1]], axis=1).reshape(rows)
+
+    places = dealt(jnp.arange(rows, dtype=jnp.int32))
     document_row = document_ids[0]
-    documents = jnp.take(document_row, places)
-    relative = places - jnp.take(document_starts(document_row), places)
+    documents = dealt(document_row)
+    relative = places - dealt(document_starts(document_row))
     cosine, sine = rotary_tables(relative, HEAD_DIM)
     visible = (documents[None, :] == documents[:, None]) & (places[None, :] <= places[:, None])
 
@@ -1198,56 +1810,52 @@
     attend_low = attend_out.reshape(rows, cols).astype(bf16)
     attend_all = ring_gather(attend_low, n, 3, "gather_attention", axis=1)
 
-    residual = inputs + jnp.dot(attend_all, out_all, preferred_element_type=f32)
-    mixed_inverse = inverse_rms(residual)
-    mixed_low = (residual * mixed_inverse * gains[:, 3]).astype(bf16)
-    logits = jnp.dot(mixed_low, router_all, preferred_element_type=f32)
-    chosen = jnp.where(named_all, logits, MASKED)
-    chosen = jnp.where(named_all, jnp.exp(chosen - jnp.max(chosen, axis=-1, keepdims=True)), 0.0)
-    gates = chosen / jnp.sum(chosen, axis=-1, keepdims=True)
-    gate_own = own(gates, local_experts, 1).T[..., None]
-
-    expert_up = jnp.einsum("td,xdf->xtf", mixed_low, first, preferred_element_type=f32)
-    gate_part, up_part = expert_up[..., :FF], expert_up[..., FF:]
-    sigmoid = jax.nn.sigmoid(gate_part)
-    swish = gate_part * sigmoid
-    hidden = swish * up_part
-    hidden_gated = (hidden * gate_own).astype(bf16)
-    mixture = jnp.einsum("xtf,xfd->td", hidden_gated, second, preferred_element_type=f32)
-    mixture = scatter_ctx(mixture)
-    own_residual = own(residual, tok_rows)
-    layer_output = (own_residual + mixture).astype(bf16)
-
-    hidden_back = jnp.einsum("td,xfd->xtf", upstream_all, second, preferred_element_type=f32)
-    gate_back = jnp.sum(hidden.astype(bf16).astype(f32) * hidden_back, axis=-1)
-    hidden_back = hidden_back * gate_own
-    slope = sigmoid * (1.0 + gate_part * (1.0 - sigmoid))
-    up_back = jnp.concatenate(
-        [hidden_back * up_part * slope, hidden_back * swish], axis=-1
+    upstream_all, mixed_all, gated_all, up_all, own_gates, gate_back, own_residual = experts_in(
+        attend_all,
+        token_all,
+        cotangent[0],
+        out_all,
+        first,
+        second,
+        jnp.broadcast_to(gains[:, 3][None], (8, width)),
+        router_wide,
+        named_all,
+        n,
+        8,
+    )
+    mixed_slots = mixed_all.reshape(rows, width)
+    second_back = jnp.einsum(
+        "tf,td->fd", gated_all, upstream_all.reshape(rows, width), preferred_element_type=f32
     ).astype(bf16)
-    second_back = jnp.einsum("xtf,td->xfd", hidden_gated, upstream_all, preferred_element_type=f32)
-    first_back = jnp.einsum("td,xtf->xdf", mixed_low, up_back, preferred_element_type=f32)
-    first_back, second_back, up_back = lax.optimization_barrier(
-        (first_back.astype(bf16), second_back.astype(bf16), up_back)
-    )
-    expert_in_gradient, expert_out_gradient = (
-        lax.psum_scatter(part, "dp", scatter_dimension=1, tiled=True).astype(f32)
-        for part in (first_back, second_back)
-    )
-    mixed_back = ring_scatter(
-        jnp.einsum("xtf,xdf->td", up_back, first, preferred_element_type=f32).astype(bf16),
-        n,
-        4,
-        "scatter_rows",
-    )
-    gate_blocks = gate_back.reshape(local_experts, n, tok_rows).transpose(1, 0, 2)
-    gate_blocks = jnp.pad(gate_blocks, ((0, 0), (0, 2 * rows // LANES - local_experts), (0, 0)))
-    gate_back = direct_exchange(gate_blocks, n, 2, "exchange")[:, :local_experts]
+    first_backs = [
+        jnp.einsum("td,tf->df", mixed_slots, up_all[x], preferred_element_type=f32).astype(bf16)
+        for x in range(local_experts)
+    ]
+    second_back, first_backs, up_all = lax.optimization_barrier(
+        (second_back, first_backs, up_all)
+    )
+    expert_out_gradient = lax.psum_scatter(
+        second_back.reshape(local_experts, FF, width), "dp", scatter_dimension=1, tiled=True
+    ).astype(f32)
+    expert_in_gradient = jnp.stack(
+        [lax.psum_scatter(one, "dp", scatter_dimension=0, tiled=True) for one in first_backs]
+    ).astype(f32)
+    mixed_back, mixture, gate_back = experts_out(up_all, gated_all, first, second, gate_back, n, 9)
+    gate_back = gate_back[:, :local_experts]
+    place = ring_place(me, n)
+    gate_back = sum(
+        jnp.where(
+            (jnp.arange(n) == ring_device((place + offset + n) % n, n))[:, None, None],
+            gate_back[slot],
+            0.0,
+        )
+        for slot, offset in enumerate(slot_offsets(n))
+    )
     gate_back = gate_back.reshape(expert_count, tok_rows).T
 
-    own_gates = own(gates, tok_rows)
-    own_mixed = own(mixed_low, tok_rows)
-    own_mixed_inverse = own(mixed_inverse, tok_rows)
+    own_gates = own_gates[:, :expert_count]
+    own_mixed = mixed_all[0]
+    own_mixed_inverse = inverse_rms(own_residual)
     own_mixed_normed = own_residual * own_mixed_inverse
     chosen_back = own_gates * (
         gate_back - jnp.sum(own_gates * gate_back, axis=-1, keepdims=True)
@@ -1261,7 +1869,8 @@
     residual_back = cotangent[0].astype(f32) + normalize_back(
         mixed_back * gains[:, 3], own_mixed_normed, own_mixed_inverse
     )
-    back_all = ring_gather(residual_back.astype(bf16), n, 5, "gather_back")
+    back_all, mixture = gather_and_scatter(residual_back.astype(bf16), mixture, n, 5)
+    layer_output = (own_residual + mixture).astype(bf16)
 
     out_part = jnp.einsum("td,te->de", attend_low, back_all, preferred_element_type=f32)
     attend_back = jnp.einsum(

time: 706 us -> 676 us (0.958)
  matrix products: 178 us -> 78.6 us
  Pallas kernels: 395 us -> 485 us
  local copies, waits for them, and re-layouts: 59.7 us -> 46 us
    pallas_call x1 -> x3, Pallas kernels: 51 us -> 223 us  [the longest x1 79.9 us: gather_and_scatter(): kernel_call(body, (jax.ShapeDtypeStruct((rows * n, width), block.dtype),...]
    dot_general x8 -> x3, matrix products: 137 us -> 42.3 us  [the longest x2 28 us: heads_local(): jnp.einsum('td,tf->df', mixed_slots, up_all[x], preferred_element_type=f32)]
    pallas_call x2 -> x1, Pallas kernels: 110 us -> 40.7 us  [ring_gather(): kernel_call(body, jax.ShapeDtypeStruct(shape, block.dtype), [ANY], ANY, [...]
    unnamed x111 -> x107, local copies, waits for them, and re-layouts: 28.6 us -> 13.9 us
    broadcast_in_dim x0 -> x33, local copies, waits for them, and re-layouts: none -> 11.1 us  [the longest x32 10.5 us: heads_local(): jnp.where((jnp.arange(n) == ring_device((place + offset + n) % n, n))[:,...]
    gather x2 -> x0, local copies, waits for them, and re-layouts: 9.05 us -> none  [the longest x1 4.53 us: heads_local(): documents = jnp.take(document_row, places)]
    concatenate x1 -> x0, other arithmetic: 8.15 us -> none  [heads_local(): jnp.concatenate([hidden_back * up_part * slope, hidden_back * swish], axi...]
    pallas_call x3 -> x2, Pallas kernels: 21.7 us -> 15.8 us  [direct_exchange(): kernel_call(body, jax.ShapeDtypeStruct(blocks.shape, blocks.dtype), [VMEM...]
  transfers between devices with their start and end apart: 7 -> 6, of which waited for: 0 -> 0; matrix products, arithmetic and copies ran while one was open for 32% -> 16% of each run, Pallas kernels for 57% -> 61%
where the time goes in v3:
time: 676 us; the launch traced here: 666 us
  Pallas kernels  485 us (72%)
  matrix products  78.6 us (12%)
  local copies, waits for them, and re-layouts  46 us (7%)
  other arithmetic  36.4 us (5%)
  between operations  15.2 us (2%)
    pallas_call x1, Pallas kernels, gather_inputs(): kernel_call(body, (jax.ShapeDtypeStruct((tok_rows * n, width), tokens.dty...  110 us
    pallas_call x1, Pallas kernels, gather_and_scatter(): kernel_call(body, (jax.ShapeDtypeStruct((rows * n, width), block.dtype),...  79.9 us
    pallas_call x1, Pallas kernels, experts_in(): pl.pallas_call(body, out_shape=(jax.ShapeDtypeStruct((n, tok_rows, width)...  79.8 us
    pallas_call x1, Pallas kernels, scatter_end(): kernel_call(body, (jax.ShapeDtypeStruct((rows, width), f32), jax.ShapeDty...  79.5 us
    pallas_call x1, Pallas kernels, experts_out(): pl.pallas_call(body, out_shape=(jax.ShapeDtypeStruct((tok_rows, width), f...  63.7 us
    pallas_call x1, Pallas kernels, ring_gather(): kernel_call(body, jax.ShapeDtypeStruct(shape, block.dtype), [ANY], ANY, [...  40.7 us
    dot_general x2, matrix products, heads_local(): jnp.einsum('td,tf->df', mixed_slots, up_all[x], preferred_element_type=f32)  28 us
    pallas_call x2, Pallas kernels, direct_exchange(): kernel_call(body, jax.ShapeDtypeStruct(blocks.shape, blocks.dtype), [VMEM...  15.8 us
  transfers between devices with their start and end apart: 6, of which 0 were waited for; matrix products, arithmetic and copies ran while one was open for 16% of the time, Pallas kernels for 61%

profile of v3, /device:TPU:1, one launch (start us, length us, event | category | flops | bytes accessed | tf_op | source)
XLA Modules:
  0.0 665.8 jit_solution(14572894391273040995)
XLA Ops:
  11.2 110.2 %gather_inputs.1 = (bf16[1024,2048]{1,0:T(8,128)(2,1)}, bf16[8,128,128]{2,1,0:T(8,128)(2,1)S(1)}, bf16[4,8,64,896]{3,2,1,0:T(8,128)(2,1)S(1)}, bf16[2048,2048]{1,0:T(8,128)(2,1)}) custom-call(bf16[128,2048]{1,0:T(8,128)(2,1)S(1)} %bitcast.199, bf16[128,128]{1,0:T(8,128)(2,1)S(1)} %convert_element_type.104.named_ref, ...), custom_call_target="tpu_custom_call" | custom-call | bytes 300000000 | tf_op jit(solution)/shard_map/gather_inputs/pallas_call | solution.py:908
  123.4 4.2 fusion.1
  127.6 3.9 fusion.13
  136.0 10.1 %exchange.2 = f32[8,16,128]{2,1,0:T(8,128)S(1)} custom-call(f32[8,16,128]{2,1,0:T(8,128)S(1)} %broadcast_in_dim.224.block_ref), custom_call_target="tpu_custom_call" | custom-call | bytes 1048576 | tf_op jit(solution)/shard_map/exchange/pallas_call | solution.py:713
  151.5 1.8 fusion.33
  156.2 6.4 fusion.46
  162.6 4.6 divide_convert_fusion
  167.3 2.1 bitcast_convert_fusion
  169.8 40.7 %gather_attention.1.attend_ref = bf16[1024,2048]{1,0:T(8,128)(2,1)S(1)} custom-call(bf16[1024,256]{1,0:T(8,128)(2,1)S(1)} %copy.202.block_ref), custom_call_target="tpu_custom_call" | custom-call | bytes 134217728 | tf_op jit(solution)/shard_map/gather_attention/pallas_call | solution.py:642
  210.5 2.0 copy-done.1
  214.1 79.8 %experts_in.1 = (bf16[8,128,2048]{2,1,0:T(8,128)(2,1)}, bf16[8,128,2048]{2,1,0:T(8,128)(2,1)}, bf16[1024,2048]{1,0:T(8,128)(2,1)}, bf16[2,1024,2048]{2,1,0:T(8,1...) custom-call(bf16[1024,2048]{1,0:T(8,128)(2,1)} %copy-done.1, ...), custom_call_target="tpu_custom_call" | custom-call | flops 34359738368 | bytes 60000000 | tf_op jit(solution)/shard_map/experts_in/pallas_call | solution.py:1366
  293.9 14.0 %convolution_convert_fusion = bf16[2048,2048]{1,0:T(8,128)(2,1)} fusion(bf16[1024,2048]{1,0:T(8,128)(2,1)} %bitcast.232, bf16[2,1024,2048]{2,1,0:T(8,128)(2,1)} %get-tuple-element.40.up_ref), kind=kOutput, calls=%fused_computation.10 | convolution fusion | flops 8594128896 | bytes 16777216 | tf_op jit(solution)/shard_map/td,tf->df/dot_general | solution.py:1831
  307.9 14.0 %convolution_convert_fusion.1 = bf16[2048,2048]{1,0:T(8,128)(2,1)} fusion(bf16[1024,2048]{1,0:T(8,128)(2,1)} %bitcast.233, bf16[2,1024,2048]{2,1,0:T(8,128)(2,1)} %get-tuple-element.40.up_ref), kind=kOutput, calls=%fused_computation.11 | convolution fusion | flops 8594128896 | bytes 16777216 | tf_op jit(solution)/shard_map/td,tf->df/dot_general | solution.py:1831
  321.9 14.3 %convolution_convert_fusion.2 = bf16[2048,2048]{1,0:T(8,128)(2,1)} fusion(bf16[1024,2048]{1,0:T(8,128)(2,1)} %get-tuple-element.36.gated_ref, bf16[1024,2048]{1,0:T(8,128)(2,1)} %bitcast.255), kind=kOutput, calls=%fused_computation.12 | convolution fusion | flops 8594128896 | bytes 16777216 | tf_op jit(solution)/shard_map/tf,td->fd/dot_general | solution.py:1827
  344.6 63.7 %experts_out.1 = (f32[128,2048]{1,0:T(8,128)}, bf16[1024,2048]{1,0:T(8,128)(2,1)}, f32[8,8,128]{2,1,0:T(8,128)}) custom-call(bf16[2,1024,2048]{2,1,0:T(8,128)(2,1)} %get-tuple-element.40.up_ref, bf16[1024,2048]{1,0:T(8,128)(2,1)} %get-tuple-element.36.gated_ref, bf16[2,2048,2048]{2,1,0:T(8,128)(2,1)} %all-gather.3.cloned.1.call-done.first_ref, ...), custom_call_target="tpu_custom_call" | custom-call | flops 25769803776 | bytes 60000000 | tf_op jit(solution)/shard_map/experts_out/pallas_call | solution.py:1614
  415.7 2.0 multiply_reduce_fusion.1
  418.6 79.9 %gather_and_scatter.1 = (bf16[1024,2048]{1,0:T(8,128)(2,1)S(1)}, f32[128,2048]{1,0:T(8,128)S(1)}) custom-call(bf16[128,2048]{1,0:T(8,128)(2,1)S(1)} %fusion.43.block_ref, bf16[1024,2048]{1,0:T(8,128)(2,1)} %get-tuple-element.45.part_ref), custom_call_target="tpu_custom_call" | custom-call | bytes 200000000 | tf_op jit(solution)/shard_map/gather_and_scatter/pallas_call | solution.py:1689
  498.6 3.7 fusion.22
  509.3 1.8 multiply_reduce_fusion
  511.7 5.7 exchange.3
  518.1 3.1 fusion.19
  525.3 5.2 convolution_convert_fusion.3.row_ref
  530.5 5.4 convolution_convert_fusion.4
  536.0 79.5 %scatter_end.1 = (f32[128,2048]{1,0:T(8,128)S(1)}, bf16[8,64,768]{2,1,0:T(8,128)(2,1)S(1)}, bf16[64,2048]{1,0:T(8,128)(2,1)S(1)}) custom-call(bf16[1024,2048]{1,0:T(8,128)(2,1)} %convolution_convert_fusion.3.row_ref, bf16[4,8,64,768]{3,2,1,0:T(8,128)(2,1)} %bitcast.219, bf16[4,64,2048]{2,1,0:T(8,128)(2,1)S(1)} %bitcast.200), custom_call_target="tpu_custom_call" | custom-call | bytes 200000000 | tf_op jit(solution)/shard_map/scatter_end/pallas_call | solution.py:1027
  616.2 1.8 reshape.444
  618.0 2.6 copy.184
  622.2 1.9 collective-permute-start
  625.8 3.0 fusion.27
  630.0 15.5 %small_scatter.1 = f32[16,128]{1,0:T(8,128)S(1)} custom-call(f32[4,8,16,128]{3,2,1,0:T(8,128)S(1)} %copy.211), custom_call_target="tpu_custom_call" | custom-call | bytes 40000000 | tf_op jit(solution)/shard_map/small_scatter/pallas_call | solution.py:1088
  647.0 1.8 convert_element_type.132
  648.8 6.2 maximum_convert_fusion
  655.0 4.1 convert_element_type.134
  (261 shorter events, 55.8 us)
Async XLA Ops:
  7.2 206.3 %all-gather.5.cloned.1.call-start = ((), (), s32[]{:S(2)}) async-start(), calls=%async_computation.4 | async-start | bytes 10485760 | tf_op jit(solution)/shard_map/all_gather | solution.py:1766
  7.9 205.5 %all-gather.3.cloned.1.call-start = ((), (), s32[]{:S(2)}) async-start(), calls=%async_computation.3 | async-start | bytes 20971520 | tf_op jit(solution)/shard_map/all_gather | solution.py:1765
  8.7 640.1 %reduce-scatter.4.cloned.1.call-start = ((), (), s32[]{:S(2)}) async-start(), calls=%async_computation.5 | async-start | bytes 10485760 | tf_op jit(solution)/shard_map/reduce_scatter | solution.py:1841
  121.4 10.1 %copy-start.7 = (bf16[8,128,128]{2,1,0:T(8,128)(2,1)}, bf16[8,128,128]{2,1,0:T(8,128)(2,1)S(1)}, u32[]{:S(2)}) copy-start(bf16[8,128,128]{2,1,0:T(8,128)(2,1)S(1)} %get-tuple-element.34) | copy-start | bytes 786436
  121.5 10.2 %copy-start.2 = (bf16[4,8,64,896]{3,2,1,0:T(8,128)(2,1)}, bf16[4,8,64,896]{3,2,1,0:T(8,128)(2,1)S(1)}, u32[]{:S(2)}) copy-start(bf16[4,8,64,896]{3,2,1,0:T(8,128)(2,1)S(1)} %get-tuple-element.32) | copy-start | bytes 11010052
  121.5 6.2 copy-start.18
  123.4 8.1 %copy-start.35 = (f32[2048]{0:T(1024)}, f32[2048]{0:T(1024)S(1)}, u32[]{:S(2)}) copy-start(f32[2048]{0:T(1024)S(1)} %get-tuple-element.91) | copy-start | bytes 24580
  127.6 216.4 %copy-start.45 = (f32[1024]{0:T(1024)}, f32[1024]{0:T(1024)S(1)}, u32[]{:S(2)}) copy-start(f32[1024]{0:T(1024)S(1)} %add_rsqrt_fusion.1) | copy-start | bytes 12292
  131.5 18.8 %copy-start.39 = (s32[1,1024]{1,0:T(1,128)S(1)}, s32[1,1024]{1,0:T(1,128)}, u32[]{:S(2)}) copy-start(s32[1,1024]{1,0:T(1,128)} %param.11) | copy-start | bytes 12292
  133.6 19.7 %slice-start = ((f32[1024,768]{0,1:T(8,128)}), f32[1024,512]{0,1:T(8,128)S(1)}, s32[]{:S(2)}) async-start(f32[1024,768]{0,1:T(8,128)} %copy-done.13), calls=%async_computation.8 | async-start | bytes 4194304 | tf_op jit(solution)/shard_map/slice | solution.py:1793
  149.2 4.7 copy-start.32
  169.4 124.5 %copy-start.24 = (bf16[1024,2,128]{0,2,1:T(8,128)(2,1)}, bf16[1024,2,128]{0,2,1:T(8,128)(2,1)S(1)}, u32[]{:S(2)}) copy-start(bf16[1024,2,128]{0,2,1:T(8,128)(2,1)S(1)} %get-tuple-element.123) | copy-start | bytes 1572868
  169.8 42.7 %copy-start.28 = (bf16[2048,16]{1,0:T(8,128)(2,1)S(1)}, bf16[2048,16]{1,0:T(8,128)(2,1)}, u32[]{:S(2)}) copy-start(bf16[2048,16]{1,0:T(8,128)(2,1)} %slice.198) | copy-start | bytes 196612
  336.2 312.6 %reduce-scatter.6.cloned.1.call-start = ((), (), s32[]{:S(2)}) async-start(), calls=%async_computation.6 | async-start | bytes 10485760 | tf_op jit(solution)/shard_map/reduce_scatter | solution.py:1841
  336.8 318.1 %reduce-scatter.8.cloned.1.call-start = ((), (), s32[]{:S(2)}) async-start(), calls=%async_computation.7 | async-start | bytes 10485760 | tf_op jit(solution)/shard_map/reduce_scatter | solution.py:1837
  344.6 69.7 %copy-start.15 = (f32[128,2048]{1,0:T(8,128)S(1)}, f32[128,2048]{1,0:T(8,128)}, u32[]{:S(2)}) copy-start(f32[128,2048]{1,0:T(8,128)} %get-tuple-element.35) | copy-start | bytes 3145732
  344.6 69.9 %copy-start.34 = (f32[128,128]{1,0:T(8,128)S(1)}, f32[128,128]{1,0:T(8,128)}, u32[]{:S(2)}) copy-start(f32[128,128]{1,0:T(8,128)} %get-tuple-element.43) | copy-start | bytes 196612
  417.7 80.9 %copy-start.30 = (f32[2,128,1024]{2,1,0:T(8,128)S(1)}, f32[2,128,1024]{2,1,0:T(8,128)}, u32[]{:S(2)}) copy-start(f32[2,128,1024]{2,1,0:T(8,128)} %get-tuple-element.124) | copy-start | bytes 3145732
  498.5 6.6 copy-start.5
  498.5 5.2 copy-start.11
  509.3 8.7 %copy-start.38 = (f32[1024,2]{0,1:T(2,128)S(1)}, f32[1024,2]{0,1:T(2,128)}, u32[]{:S(2)}) copy-start(f32[1024,2]{0,1:T(2,128)} %copy-done.37) | copy-start | bytes 24580
  509.3 8.7 %copy-start.42 = (f32[1,2,2,128]{3,1,2,0:T(2,128)S(1)}, f32[1,2,2,128]{3,1,2,0:T(2,128)}, u32[]{:S(2)}) copy-start(f32[1,2,2,128]{3,1,2,0:T(2,128)} %copy.205) | copy-start | bytes 6148
  511.1 10.0 %copy-start.23 = (bf16[1024,256]{0,1:T(8,128)(2,1)S(1)}, bf16[1024,256]{0,1:T(8,128)(2,1)}, u32[]{:S(2)}) copy-start(bf16[1024,256]{0,1:T(8,128)(2,1)} %copy-done.22) | copy-start | bytes 1572868
  518.1 5.2 copy-start.6
  518.1 5.2 copy-start.25
  525.3 5.2 copy-start.19
  525.3 5.2 copy-start.36
  525.3 5.2 copy-start.46
  616.2 8.0 %copy-start.47 = (f32[128]{0:T(128)S(1)}, f32[128]{0:T(128)}, u32[]{:S(2)}) copy-start(f32[128]{0:T(128)} %dynamic-slice.3) | copy-start | bytes 1540
  618.0 4.2 copy-start.9
  618.0 7.8 %copy-start.27 = (bf16[1,128,2048]{2,1,0:T(8,128)(2,1)S(1)}, bf16[1,128,2048]{2,1,0:T(8,128)(2,1)}, u32[]{:S(2)}) copy-start(bf16[1,128,2048]{2,1,0:T(8,128)(2,1)} %param.19) | copy-start | bytes 1572868
  622.2 24.8 %collective-permute-start = (bf16[64,2048]{1,0:T(8,128)(2,1)S(1)}, bf16[64,2048]{1,0:T(8,128)(2,1)}, u32[]{:S(2)}, u32[]{:S(2)}) collective-permute-start(bf16[64,2048]{1,0:T(8,128)(2,1)S(1)} %copy-done.9), channel_id=1, source_target_pairs={{0,0},{1,4},{2,8},{3,12},{4,16},{5,20},{6,24},{7,28},{8,1},{9,5},{... | collective-permute-start | bytes 786440 | tf_op jit(solution)/shard_map/ppermute | solution.py:1904
  (24 other events, 49.1 us)
Sparse Core Ops, SparseCore 0:
  9.6 81.5 all-gather.4
  92.8 104.7 all-gather.2
  336.3 74.6 reduce-scatter.3
  414.2 71.6 reduce-scatter.5
  488.3 76.5 reduce-scatter.7

commit v4 on v3

--- a/solution.py
+++ b/solution.py
@@ -14,6 +14,8 @@
 ROPE_BASE = 10000.0
 MASKED = -1e30
 LANES = 128
+TILE = 512
+WIDE = 1024
 
 
 def inverse_rms(values):
@@ -683,45 +685,6 @@
     )(partial)
 
 
-def direct_exchange(blocks, n, identity, name):
-    def body(block_ref, got_ref, send, receive):
-        me = lax.axis_index("ctx")
-        ring = Ring(n)
-        ring.barrier([{"ctx": (me + k) % n} for k in range(1, n)])
-        got_ref[me] = block_ref[me]
-        copies = []
-        for k in range(1, n):
-            other = (me + k) % n
-            copies.append(
-                remote(
-                    block_ref.at[other],
-                    got_ref.at[me],
-                    send.at[k - 1],
-                    receive.at[k - 1],
-                    {"ctx": other},
-                )
-            )
-            copies[-1].start()
-        for k in range(1, n):
-            spot = got_ref.at[(me - k + n) % n]
-            remote(
-                spot, spot, send.at[k - 1], receive.at[k - 1], {"ctx": (me + k) % n}
-            ).wait_recv()
-        for copy in copies:
-            copy.wait_send()
-
-    return kernel_call(
-        body,
-        jax.ShapeDtypeStruct(blocks.shape, blocks.dtype),
-        [VMEM],
-        VMEM,
-        [sems(n - 1), sems(n - 1)],
-        identity,
-        name,
-        blocks.size * 64,
-    )(blocks)
-
-
 def partners():
     dp = lax.axis_index("dp")
     core = dp + 1 - 2 * (dp % 2)
@@ -729,27 +692,18 @@
     return dp, core, chip, (core + 2) % 4
 
 
-def gather_inputs(tokens, named, in_blocks, out_rows, n, n_dp, identity):
+def gather_inputs(tokens, named, in_blocks, n, n_dp, identity):
     tok_rows, width = tokens.shape
-    weight_rows, in_width = in_blocks.shape[1:]
 
     def body(
         token_ref,
         named_ref,
         in_ref,
-        out_ref,
         token_all,
         named_all,
         in_all,
-        out_all,
         token_send,
         token_receive,
-        out_send,
-        out_receive,
-        core_send,
-        core_receive,
-        own_send,
-        own_receive,
         named_send,
         named_receive,
         in_send,
@@ -768,11 +722,6 @@
                 pl.ds(pl.multiple_of(device * tok_rows + half * half_rows, 16), half_rows)
             ]
 
-        def out_place(group, device):
-            return out_all.at[
-                pl.ds(pl.multiple_of((group * n + device) * weight_rows, 16), weight_rows)
-            ]
-
         locals_ = [
             pltpu.make_async_copy(in_ref.at[me], in_all.at[dp, me], local.at[0]),
             pltpu.make_async_copy(
@@ -781,19 +730,12 @@
                 local.at[1],
             ),
             pltpu.make_async_copy(named_ref, named_all.at[me], local.at[2]),
-            pltpu.make_async_copy(out_ref, out_place(dp, me), local.at[3]),
         ]
         for copy in locals_:
             copy.start()
         others = [(me + k) % n for k in range(1, n)]
         ring.barrier([{"ctx": other} for other in others] + [{"dp": core}, {"dp": chip}])
 
-        out_copies = [
-            remote(out_ref, out_place(dp, me), own_send.at[0], own_receive.at[0], {"dp": chip}),
-            remote(out_ref, out_place(dp, me), own_send.at[1], own_receive.at[1], {"dp": core}),
-        ]
-        for copy in out_copies:
-            copy.start()
         direct = []
         for k, other in enumerate(others):
             direct.append(
@@ -804,28 +746,6 @@
             )
         for copy in direct:
             copy.start()
-
-        def out_ready(half):
-            if half == 1:
-                spot = out_place(chip, me)
-                remote(spot, spot, own_send.at[0], own_receive.at[0], {"dp": chip}).wait_recv()
-                out_copies.append(
-                    remote(spot, spot, own_send.at[2], own_receive.at[2], {"dp": core})
-                )
-                out_copies[-1].start()
-
-        def out_arrived(way, half, hop, origin):
-            spot = out_place(chip if half else dp, origin)
-            out_copies.append(
-                remote(
-                    spot,
-                    spot,
-                    core_send.at[way, half, hop],
-                    core_receive.at[way, half, hop],
-                    {"dp": core},
-                )
-            )
-            out_copies[-1].start()
 
         def in_steps():
             for _ in range(2):
@@ -844,7 +764,7 @@
                     )
                 )
                 passed[-1].start()
-            for _ in range(6):
+            for _ in range(8):
                 yield
             spot = in_all.at[chip]
             remote(spot, spot, pass_send.at[0], pass_receive.at[0], {"dp": chip}).wait_recv()
@@ -852,7 +772,7 @@
                 remote(spot, spot, pass_send.at[2], pass_receive.at[2], {"dp": core})
             )
             passed[-1].start()
-            for _ in range(6):
+            for _ in range(4):
                 yield
             for at, source in ((1, core), (2, core_chip)):
                 spot = in_all.at[source]
@@ -870,15 +790,6 @@
                 token_send,
                 token_receive,
             ),
-            gather_steps(
-                ring,
-                lambda half: out_place(chip, me) if half else out_ref,
-                lambda device, half: out_place(chip if half else dp, device),
-                out_send,
-                out_receive,
-                out_arrived,
-                out_ready,
-            ),
             in_steps(),
         )
         for k in range(1, n):
@@ -886,21 +797,7 @@
             remote(
                 spot, spot, named_send.at[k - 1], named_receive.at[k - 1], {"ctx": others[k - 1]}
             ).wait_recv()
-        for at, group in ((1, core), (2, core_chip)):
-            spot = out_place(group, me)
-            remote(spot, spot, own_send.at[at], own_receive.at[at], {"dp": core}).wait_recv()
-        for way, sign in ((0, 1), (1, -1)):
-            for half in (0, 1):
-                for hop in range(ring.hops(way, half)):
-                    spot = out_place(core_chip if half else core, ring.at(-sign * (hop + 1)))
-                    remote(
-                        spot,
-                        spot,
-                        core_send.at[way, half, hop],
-                        core_receive.at[way, half, hop],
-                        {"dp": core},
-                    ).wait_recv()
-        for copy in direct + out_copies:
+        for copy in direct:
             copy.wait_send()
         for copy in locals_[1:]:
             copy.wait()
@@ -911,93 +808,168 @@
             jax.ShapeDtypeStruct((tok_rows * n, width), tokens.dtype),
             jax.ShapeDtypeStruct((n,) + named.shape, named.dtype),
             jax.ShapeDtypeStruct((n_dp,) + in_blocks.shape, in_blocks.dtype),
-            jax.ShapeDtypeStruct((weight_rows * n * n_dp, out_rows.shape[1]), out_rows.dtype),
         ),
-        [ANY] * 4,
-        (ANY,) * 4,
-        [sems(2, 2, n // 2)] * 6
-        + [sems(3)] * 2
+        [ANY] * 3,
+        (ANY,) * 3,
+        [sems(2, 2, n // 2)] * 2
         + [sems(n - 1)] * 4
         + [sems(3)] * 2
-        + [sems(4)],
+        + [sems(3)],
         identity,
         "gather_inputs",
-        300_000_000,
-    )(tokens, named, in_blocks, out_rows)
-
-
-def scatter_end(row_part, in_part, out_part, n, identity):
+        200_000_000,
+    )(tokens, named, in_blocks)
+
+
+def sum_small_steps(ring, small, core_s, chip_s, quarter, got, total, sem):
+    pass_send, pass_receive, send, receive = sem
+    dp, core, chip, core_chip = partners()
+    n, me = ring.n, ring.me
+    lanes = quarter.shape[1]
+    per_tile = LANES * n // lanes
+
+    def group(at):
+        return small.at[:, pl.ds(pl.multiple_of(at * lanes, LANES), lanes)]
+
+    copies = [
+        remote(group(core_chip), core_s.at[1], pass_send.at[0], pass_receive.at[0], {"dp": core}),
+        remote(group(core), core_s.at[0], pass_send.at[1], pass_receive.at[1], {"dp": core}),
+    ]
+    for copy in copies:
+        copy.start()
+    copies[0].wait_recv()
+    core_s[1] = core_s[1] + group(chip)[...]
+    copies.append(
+        remote(core_s.at[1], chip_s, pass_send.at[2], pass_receive.at[2], {"dp": chip})
+    )
+    copies[-1].start()
+    copies[1].wait_recv()
+    copies[2].wait_recv()
+    quarter[...] = group(dp)[...] + core_s[0] + chip_s[...]
+
+    def tile(device):
+        return quarter.at[:, pl.ds(pl.multiple_of(device // per_tile * LANES, LANES), LANES)]
+
+    for k in range(1, n):
+        other = (me + k) % n
+        copies.append(
+            remote(tile(other), got.at[k - 1], send.at[k - 1], receive.at[k - 1], {"ctx": other})
+        )
+        copies[-1].start()
+    value = tile(me)[...]
+    for k in range(1, n):
+        copies[2 + k].wait_recv()
+        value = value + got[k - 1]
+    total[...] = value
+    for copy in copies:
+        copy.wait_send()
+
+
+def scatter_end(
+    row_part, attend_in, raw_back, tokens, residual_back, gain, small, pair_sum, n, n_dp, identity
+):
     rows, width = row_part.shape[0] // n, row_part.shape[1]
     half_rows = rows // 2
-    f32 = jnp.float32
+    span = width // n_dp
+    weight_rows = span // n
+    in_cols = raw_back.shape[1]
+    cols = in_cols // 3
+    small_rows = small.shape[0]
+    bf16, f32 = jnp.bfloat16, jnp.float32
 
     def body(
         row_ref,
-        in_ref,
-        out_ref,
-        row_sum,
-        in_got,
-        out_sum,
+        attend_ref,
+        raw_ref,
+        token_ref,
+        back_ref,
+        gain_ref,
+        small_ref,
+        pair_ref,
+        token_back,
+        in_sum,
+        small_sum,
         slots,
+        row_s,
+        attend_s,
+        in_part,
         in_core,
         in_chip,
-        out_core,
-        out_chip,
+        in_got,
+        small_s,
+        small_core,
+        small_chip,
+        small_quarter,
+        small_got,
         row_send,
         row_receive,
         pass_send,
         pass_receive,
         in_send,
         in_receive,
+        small_pass_send,
+        small_pass_receive,
+        small_send,
+        small_receive,
+        load,
     ):
         ring = Ring(n)
         me = ring.me
         dp, core, chip, core_chip = partners()
         others = [(me + k) % n for k in range(1, n)]
+        loaded = pltpu.make_async_copy(attend_ref, attend_s, load)
+        loaded.start()
         ring.barrier([{"ctx": other} for other in others] + [{"dp": core}, {"dp": chip}])
 
         def part(device, half):
             return row_ref.at[pl.ds(pl.multiple_of(device * rows + half * half_rows, 16), half_rows)]
 
         def store(half, total):
-            row_sum[pl.ds(half * half_rows, half_rows)] = total
+            row_s[pl.ds(half * half_rows, half_rows)] = total
 
         def passing(at, source, target, to):
             return remote(source, target, pass_send.at[at], pass_receive.at[at], {"dp": to})
 
+        def product(group):
+            value = lax.dot_general(
+                attend_s[:, pl.ds(pl.multiple_of(group * span, LANES), span)],
+                raw_ref[...],
+                (((0,), (0,)), ((), ())),
+                preferred_element_type=f32,
+            )
+            in_part[group] = value.astype(bf16).reshape(n, weight_rows, in_cols)
+
         def weight_steps():
-            passed = [
-                passing(0, in_ref.at[core_chip], in_core.at[1], core),
-                passing(1, out_ref.at[core_chip], out_core.at[1], core),
-                passing(2, in_ref.at[core], in_core.at[0], core),
-                passing(3, out_ref.at[core], out_core.at[0], core),
-            ]
-            for copy in passed:
-                copy.start()
+            loaded.wait()
+            product(core_chip)
+            passed = [passing(0, in_part.at[core_chip], in_core.at[1], core)]
+            passed[-1].start()
             yield
+            product(core)
+            passed.append(passing(1, in_part.at[core], in_core.at[0], core))
+            passed[-1].start()
+            yield
+            product(chip)
             passed[0].wait_recv()
 
             def add_far(k, carry):
-                in_core[1, k] = (in_core[1, k].astype(f32) + in_ref[chip, k].astype(f32)).astype(in_ref.dtype)
+                in_core[1, k] = (in_core[1, k].astype(f32) + in_part[chip, k].astype(f32)).astype(bf16)
                 return carry
 
             lax.fori_loop(0, n, add_far, 0)
-            passed.append(passing(4, in_core.at[1], in_chip, chip))
+            passed.append(passing(2, in_core.at[1], in_chip, chip))
             passed[-1].start()
+            yield
+            product(dp)
             passed[1].wait_recv()
-            out_core[1] = (out_core[1].astype(f32) + out_ref[chip].astype(f32)).astype(out_ref.dtype)
-            passed.append(passing(5, out_core.at[1], out_chip, chip))
-            passed[-1].start()
             for _ in range(4):
                 yield
             passed[2].wait_recv()
-            passed[3].wait_recv()
-            passed[4].wait_recv()
 
             def add_near(k, carry):
                 in_core[0, k] = (
-                    in_core[0, k].astype(f32) + in_ref[dp, k].astype(f32) + in_chip[k].astype(f32)
-                ).astype(in_ref.dtype)
+                    in_core[0, k].astype(f32) + in_part[dp, k].astype(f32) + in_chip[k].astype(f32)
+                ).astype(bf16)
                 return carry
 
             lax.fori_loop(0, n, add_near, 0)
@@ -1008,10 +980,6 @@
                 )
                 direct[-1].start()
             in_got[me] = in_core[0, me]
-            passed[5].wait_recv()
-            out_sum[...] = (
-                out_core[0].astype(f32) + out_ref[dp].astype(f32) + out_chip[...].astype(f32)
-            ).astype(out_ref.dtype)
             for _ in range(8):
                 yield
             for k in range(1, n):
@@ -1019,82 +987,82 @@
                 remote(
                     spot, spot, in_send.at[k - 1], in_receive.at[k - 1], {"ctx": others[k - 1]}
                 ).wait_recv()
+            for device in range(n):
+                for which in range(3):
+                    in_sum[:, pl.ds(which * width + device * cols, cols)] = in_got[
+                        device, :, pl.ds(which * cols, cols)
+                    ].astype(f32)
             for copy in passed + direct:
                 copy.wait_send()
 
-        run_steps(scatter_steps(ring, part, slots, store, row_send, row_receive), weight_steps())
-
+        def row_steps():
+            yield from scatter_steps(ring, part, slots, store, row_send, row_receive)
+            values = token_ref[...].astype(f32)
+            inverse = lax.rsqrt(jnp.mean(values * values, axis=-1, keepdims=True) + EPSILON)
+            normed = values * inverse
+            back = row_s[...]
+            small_s[...] = small_ref[...]
+            small_s[0:1, :] = jnp.sum(back * normed, axis=0, keepdims=True)
+            own = pl.ds(pl.multiple_of(me * cols, LANES), cols)
+            small_s[1:2, own] = pair_ref[0:1, :cols]
+            small_s[2:3, own] = pair_ref[0:1, cols:]
+            back = back * gain_ref[0:1, :]
+            token_back[...] = (
+                back_ref[...]
+                + inverse * (back - normed * jnp.mean(back * normed, axis=-1, keepdims=True))
+            ).astype(bf16)
+            sum_small_steps(
+                ring,
+                small_s,
+                small_core,
+                small_chip,
+                small_quarter,
+                small_got,
+                small_sum,
+                (small_pass_send, small_pass_receive, small_send, small_receive),
+            )
+
+        run_steps(row_steps(), weight_steps())
+
+    block = (n, weight_rows, in_cols)
     return kernel_call(
         body,
         (
-            jax.ShapeDtypeStruct((rows, width), f32),
-            jax.ShapeDtypeStruct(in_part.shape[1:], in_part.dtype),
-            jax.ShapeDtypeStruct(out_part.shape[1:], out_part.dtype),
+            jax.ShapeDtypeStruct((rows, width), bf16),
+            jax.ShapeDtypeStruct((weight_rows, 3 * width), f32),
+            jax.ShapeDtypeStruct((small_rows, LANES), f32),
         ),
-        [VMEM] * 3,
+        [VMEM, ANY] + [VMEM] * 6,
         (VMEM,) * 3,
         [
             pltpu.VMEM((2, 2, n // 2, half_rows, width), row_part.dtype),
-            pltpu.VMEM((2,) + in_part.shape[1:], in_part.dtype),
-            pltpu.VMEM(in_part.shape[1:], in_part.dtype),
-            pltpu.VMEM((2,) + out_part.shape[1:], out_part.dtype),
-            pltpu.VMEM(out_part.shape[1:], out_part.dtype),
+            pltpu.VMEM((rows, width), f32),
+            pltpu.VMEM(attend_in.shape, bf16),
+            pltpu.VMEM((n_dp,) + block, bf16),
+            pltpu.VMEM((2,) + block, bf16),
+            pltpu.VMEM(block, bf16),
+            pltpu.VMEM(block, bf16),
+            pltpu.VMEM((small_rows, width), f32),
+            pltpu.VMEM((2, small_rows, span), f32),
+            pltpu.VMEM((small_rows, span), f32),
+            pltpu.VMEM((small_rows, span), f32),
+            pltpu.VMEM((n - 1, small_rows, LANES), f32),
             sems(2, 2, n // 2),
             sems(2, 2, n // 2),
-            sems(6),
-            sems(6),
+            sems(3),
+            sems(3),
             sems(n - 1),
             sems(n - 1),
+            sems(3),
+            sems(3),
+            sems(n - 1),
+            sems(n - 1),
+            pltpu.SemaphoreType.DMA,
         ],
         identity,
         "scatter_end",
         200_000_000,
-    )(row_part, in_part, out_part)
-
-
-def small_scatter(parts, n, n_dp, identity):
-    def body(part_ref, sum_ref, got, send, receive):
-        me, dp = lax.axis_index("ctx"), lax.axis_index("dp")
-        flat = dp * n + me
-        count = n * n_dp
-        semaphore = pltpu.get_barrier_semaphore()
-
-        def spot(at):
-            return (at // n, at % n)
-
-        for k in range(1, count):
-            pl.semaphore_signal(
-                semaphore, inc=1, device_id=spot((flat + k) % count), device_id_type=MESH
-            )
-        pl.semaphore_wait(semaphore, count - 1)
-        copies = []
-        for k in range(1, count):
-            to = (flat + k) % count
-            copies.append(
-                remote(
-                    part_ref.at[to // n, to % n], got.at[k], send.at[k], receive.at[k], spot(to)
-                )
-            )
-            copies[-1].start()
-        total = part_ref[dp, me]
-        for k in range(1, count):
-            copies[k - 1].wait_recv()
-            total = total + got[k]
-        sum_ref[...] = total
-        for copy in copies:
-            copy.wait_send()
-
-    shape = parts.shape[2:]
-    return kernel_call(
-        body,
-        jax.ShapeDtypeStruct(shape, parts.dtype),
-        [VMEM],
-        VMEM,
-        [pltpu.VMEM((n * n_dp,) + shape, parts.dtype), sems(n * n_dp), sems(n * n_dp)],
-        identity,
-        "small_scatter",
-        40_000_000,
-    )(parts)
+    )(row_part, attend_in, raw_back, tokens, residual_back, gain, small, pair_sum)
 
 
 def slot_offsets(n):
@@ -1165,7 +1133,7 @@
     rows = tok_rows * n
     pair = 2 * tok_rows
     part = 4 * tok_rows
-    tile, wide = 256, 512
+    tile, wide = TILE, WIDE
     bf16, f32 = jnp.bfloat16, jnp.float32
     offsets = slot_offsets(n)
 
@@ -1298,7 +1266,7 @@
         for s in range(counts):
             slots = pl.ds(s * 4, 4)
             part_rows = pl.ds(s * part, part)
-            advance(steps, 8 if s < counts - 1 else 64)
+            advance(steps, 0 if s < counts - 1 else 64)
             if s == 0:
                 own.wait()
             sum_s[part_rows] = jnp.zeros((part, LANES), f32)
@@ -1338,10 +1306,10 @@
                     ).astype(bf16)
                     return carry
 
-                quarters = ff // tile
-                lax.fori_loop(0, quarters // 2, hidden, 0)
+                pieces = ff // tile
+                lax.fori_loop(0, pieces // 2, hidden, 0)
                 advance(steps, 2)
-                lax.fori_loop(quarters // 2, quarters, hidden, 0)
+                lax.fori_loop(pieces // 2, pieces, hidden, 0)
                 advance(steps, 2)
                 outgoing.append(
                     pltpu.make_async_copy(
@@ -1577,7 +1545,7 @@
         steps = slot_scatter_steps(ring, part_s, slots, store, send, receive, need)
         for j in reversed(range(groups)):
             need(2 * j)
-            advance(steps, 3)
+            advance(steps, 1 if j in (0, groups - 1) else 2)
         for copy in others:
             copy.wait()
         saves = []
@@ -1649,68 +1617,561 @@
     )(up_all, gated_all, first, second, gate_back)
 
 
-def gather_and_scatter(block, partial, n, identity):
-    rows, width = block.shape
-    half_rows = rows // 2
-
-    def body(block_ref, part_ref, all_ref, sum_ref, slots, send, receive, sum_send, sum_receive, local):
+def exchange_rows(ring, sums, flat, got, send, receive, steps):
+    n, rows = ring.n, sums.shape[0]
+    for k in range(rows // LANES):
+        flat[:, pl.ds(k * LANES, LANES)] = jnp.transpose(sums[pl.ds(k * LANES, LANES)])[:8]
+    copies = []
+    for k in range(1, n):
+        copies.append(
+            remote(
+                flat,
+                got.at[k - 1],
+                send.at[k - 1],
+                receive.at[k - 1],
+                {"ctx": (ring.me + k) % n},
+            )
+        )
+        copies[-1].start()
+    advance(steps, 1)
+    for copy in copies:
+        copy.wait_recv()
+    total = flat[...]
+    for k in range(n - 1):
+        total = total + got[k]
+    for k in range(rows // LANES):
+        block = total[:, k * LANES : (k + 1) * LANES]
+        block = jnp.concatenate([block, jnp.zeros((LANES - 8, LANES), jnp.float32)], axis=0)
+        sums[pl.ds(k * LANES, LANES)] = jnp.transpose(block)
+    for copy in copies:
+        copy.wait_send()
+
+
+def turn(values, cosine, sine):
+    return values * cosine + pltpu.roll(values, HEAD_DIM // 2, 1) * sine
+
+
+def out_gather_steps(ring, out_ref, out_all, sem):
+    own_send, own_receive, ring_send, ring_receive, core_send, core_receive, local = sem
+    dp, core, chip, core_chip = partners()
+    weight_rows, n, me = out_ref.shape[0], ring.n, ring.me
+
+    def place(group, device):
+        return out_all.at[pl.ds(pl.multiple_of((group * n + device) * weight_rows, 16), weight_rows)]
+
+    own = pltpu.make_async_copy(out_ref, place(dp, me), local)
+    own.start()
+    copies = [
+        remote(out_ref, place(dp, me), own_send.at[0], own_receive.at[0], {"dp": chip}),
+        remote(out_ref, place(dp, me), own_send.at[1], own_receive.at[1], {"dp": core}),
+    ]
+    for copy in copies:
+        copy.start()
+
+    def ready(half):
+        if half == 1:
+            spot = place(chip, me)
+            remote(spot, spot, own_send.at[0], own_receive.at[0], {"dp": chip}).wait_recv()
+            copies.append(remote(spot, spot, own_send.at[2], own_receive.at[2], {"dp": core}))
+            copies[-1].start()
+
+    def arrived(way, half, hop, origin):
+        spot = place(chip if half else dp, origin)
+        copies.append(
+            remote(
+                spot, spot, core_send.at[way, half, hop], core_receive.at[way, half, hop], {"dp": core}
+            )
+        )
+        copies[-1].start()
+
+    yield from gather_steps(
+        ring,
+        lambda half: place(chip, me) if half else out_ref,
+        lambda device, half: place(chip if half else dp, device),
+        ring_send,
+        ring_receive,
+        arrived,
+        ready,
+    )
+    for at, group in ((1, core), (2, core_chip)):
+        spot = place(group, me)
+        remote(spot, spot, own_send.at[at], own_receive.at[at], {"dp": core}).wait_recv()
+    for way, sign in ((0, 1), (1, -1)):
+        for half in (0, 1):
+            for hop in range(ring.hops(way, half)):
+                spot = place(core_chip if half else core, ring.at(-sign * (hop + 1)))
+                remote(
+                    spot,
+                    spot,
+                    core_send.at[way, half, hop],
+                    core_receive.at[way, half, hop],
+                    {"dp": core},
+                ).wait_recv()
+    for copy in copies:
+        copy.wait_send()
+    own.wait()
+
+
+def attention_in(
+    token_all, in_all, out_rows, gain, pair_gains, cosine, sine, bounds, place_row, n, n_dp, identity
+):
+    rows, width = token_all.shape
+    pair = pair_gains.shape[1]
+    cols = pair // 2
+    heads = cols // HEAD_DIM
+    chunk = 256
+    weight_rows = out_rows.shape[0]
+    bf16, f32 = jnp.bfloat16, jnp.float32
+    scale = HEAD_DIM ** (-0.5)
+
+    def body(
+        token_ref,
+        in_ref,
+        out_ref,
+        gain_ref,
+        pair_ref,
+        cos_ref,
+        sin_ref,
+        bound_ref,
+        place_ref,
+        attend_all,
+        out_all,
+        probs_all,
+        normed_all,
+        attend_ref,
+        qkv_ref,
+        raw_ref,
+        inverse_ref,
+        probs_s,
+        normed_s,
+        flat,
+        got,
+        *sem,
+    ):
+        out_sem, sem = sem[:7], sem[7:]
+        sum_send, sum_receive, ring_send, ring_receive, save = sem
         ring = Ring(n)
-
-        def half_of(ref, device, half):
-            return ref.at[pl.ds(pl.multiple_of(device * rows + half * half_rows, 16), half_rows)]
-
-        def store(half, total):
-            sum_ref[pl.ds(half * half_rows, half_rows)] = total
-
+        dp, core, chip, core_chip = partners()
+        ring.barrier(
+            [{"ctx": (ring.me + k) % n} for k in range(1, n)] + [{"dp": core}, {"dp": chip}]
+        )
+        steps = out_gather_steps(ring, out_ref, out_all, out_sem)
+        advance(steps, 1)
+        lanes = lax.broadcasted_iota(jnp.int32, (chunk, LANES), 1)
+
+        def chunks(step, count=2):
+            total = rows // chunk
+            for first in range(0, total, count):
+                lax.fori_loop(first, min(first + count, total), step, 0)
+                advance(steps, 2)
+
+        def project(j, carry):
+            at = pl.ds(pl.multiple_of(j * chunk, chunk), chunk)
+            values = token_ref[at].astype(f32)
+            inverse = lax.rsqrt(jnp.mean(values * values, axis=-1, keepdims=True) + EPSILON)
+            normed = (values * inverse * gain_ref[0:1, :]).astype(bf16)
+            normed_s[at] = normed
+            projected = dot(normed, in_ref[:, : pair + cols])
+            raw_ref[at] = projected[:, :pair]
+            qkv_ref[at, pair:] = projected[:, pair:].astype(bf16)
+            squares = projected[:, :pair] * projected[:, :pair]
+            inverse_ref[at] = jnp.where(
+                lanes == 0,
+                jnp.sum(squares[:, :cols], axis=-1, keepdims=True),
+                jnp.where(lanes == 1, jnp.sum(squares[:, cols:], axis=-1, keepdims=True), 0.0),
+            )
+            return carry
+
+        chunks(project)
+        saves = [pltpu.make_async_copy(normed_s, normed_all, save.at[heads])]
+        saves[0].start()
+        exchange_rows(ring, inverse_ref, flat, got, sum_send, sum_receive, steps)
+
+        def norm(j, carry):
+            at = pl.ds(pl.multiple_of(j * chunk, chunk), chunk)
+            inverse = lax.rsqrt(inverse_ref[at] / width + EPSILON)
+            inverse_ref[at] = inverse
+            for which in range(2):
+                for head in range(heads):
+                    columns = pl.ds(which * cols + head * HEAD_DIM, HEAD_DIM)
+                    values = raw_ref[at, columns] * inverse[:, which : which + 1]
+                    values = values * pair_ref[0:1, columns]
+                    qkv_ref[at, columns] = turn(values, cos_ref[at], sin_ref[at]).astype(bf16)
+            return carry
+
+        chunks(norm)
+        for head in range(heads):
+
+            def attend(j, carry, head=head):
+                at = pl.ds(pl.multiple_of(j * chunk, chunk), chunk)
+                columns = pl.ds(head * HEAD_DIM, HEAD_DIM)
+                scores = (
+                    dot_across(
+                        qkv_ref[at, columns], qkv_ref[:, pl.ds(cols + head * HEAD_DIM, HEAD_DIM)]
+                    )
+                    * scale
+                )
+                place = place_ref[0:1, :]
+                visible = (place >= bound_ref[at, 0:1]) & (place <= bound_ref[at, 1:2])
+                scores = jnp.where(visible, scores, MASKED)
+                powers = jnp.where(
+                    visible, jnp.exp(scores - jnp.max(scores, axis=-1, keepdims=True)), 0.0
+                )
+                share = 1.0 / jnp.sum(powers, axis=-1, keepdims=True)
+                probs = (powers * share).astype(bf16)
+                probs_s[head, at] = probs
+                attend_ref[at, columns] = dot(
+                    probs, qkv_ref[:, pl.ds(pair + head * HEAD_DIM, HEAD_DIM)]
+                ).astype(bf16)
+                return carry
+
+            chunks(attend)
+            saves.append(pltpu.make_async_copy(probs_s.at[head], probs_all.at[head], save.at[head]))
+            saves[-1].start()
+
+        half_rows = rows // 2
         own = pltpu.make_async_copy(
-            block_ref, all_ref.at[pl.ds(pl.multiple_of(ring.me * rows, 16), rows)], local
+            attend_ref,
+            attend_all.at[:, pl.ds(pl.multiple_of(ring.me * cols, LANES), cols)],
+            save.at[heads + 1],
         )
         own.start()
-        ring.barrier(ring.neighbours())
         run_steps(
+            steps,
             gather_steps(
                 ring,
-                lambda half: block_ref.at[pl.ds(half * half_rows, half_rows)],
-                lambda device, half: half_of(all_ref, device, half),
-                send,
-                receive,
-            ),
-            scatter_steps(
-                ring,
-                lambda device, half: half_of(part_ref, device, half),
-                slots,
-                store,
-                sum_send,
-                sum_receive,
+                lambda half: attend_ref.at[pl.ds(half * half_rows, half_rows)],
+                lambda device, half: attend_all.at[
+                    pl.ds(half * half_rows, half_rows),
+                    pl.ds(pl.multiple_of(device * cols, LANES), cols),
+                ],
+                ring_send,
+                ring_receive,
             ),
         )
         own.wait()
-
-    return kernel_call(
+        for copy in saves:
+            copy.wait()
+
+    return pl.pallas_call(
         body,
-        (
-            jax.ShapeDtypeStruct((rows * n, width), block.dtype),
-            jax.ShapeDtypeStruct((rows, width), jnp.float32),
+        out_shape=(
+            jax.ShapeDtypeStruct((rows, width), bf16),
+            jax.ShapeDtypeStruct((weight_rows * n * n_dp, width), bf16),
+            jax.ShapeDtypeStruct((heads, rows, rows), bf16),
+            jax.ShapeDtypeStruct((rows, width), bf16),
+            jax.ShapeDtypeStruct((rows, cols), bf16),
+            jax.ShapeDtypeStruct((rows, 3 * cols), bf16),
+            jax.ShapeDtypeStruct((rows, pair), f32),
+            jax.ShapeDtypeStruct((rows, LANES), f32),
         ),
-        [ANY, VMEM],
-        (ANY, VMEM),
-        [pltpu.VMEM((2, 2, n // 2, half_rows, width), partial.dtype)]
-        + [sems(2, 2, n // 2)] * 4
-        + [pltpu.SemaphoreType.DMA],
-        identity,
-        "gather_and_scatter",
-        200_000_000,
-    )(block, partial)
-
-
-def gather_ctx(block):
-    return lax.all_gather(block, "ctx", axis=0, tiled=True)
-
-
-def scatter_ctx(partial):
-    return lax.psum_scatter(
-        partial.astype(jnp.bfloat16), "ctx", scatter_dimension=0, tiled=True
-    ).astype(jnp.float32)
+        in_specs=[VMEM, VMEM, ANY] + [VMEM] * 6,
+        out_specs=(ANY,) * 4 + (VMEM,) * 4,
+        scratch_shapes=[
+            pltpu.VMEM((heads, rows, rows), bf16),
+            pltpu.VMEM((rows, width), bf16),
+            pltpu.VMEM((8, rows), f32),
+            pltpu.VMEM((n - 1, 8, rows), f32),
+            sems(3),
+            sems(3),
+            sems(2, 2, n // 2),
+            sems(2, 2, n // 2),
+            sems(2, 2, n // 2),
+            sems(2, 2, n // 2),
+            pltpu.SemaphoreType.DMA,
+            sems(n - 1),
+            sems(n - 1),
+            sems(2, 2, n // 2),
+            sems(2, 2, n // 2),
+            sems(heads + 2),
+        ],
+        name="attention_in",
+        cost_estimate=pl.CostEstimate(
+            flops=2 * rows * width * 3 * cols, bytes_accessed=200_000_000, transcendentals=0
+        ),
+        compiler_params=pltpu.CompilerParams(
+            collective_id=identity, has_side_effects=True, vmem_limit_bytes=BIG_VMEM
+        ),
+    )(token_all, in_all, out_rows, gain, pair_gains, cosine, sine, bounds, place_row)
+
+
+def attention_back(
+    back_all,
+    out_all,
+    in_all,
+    probs,
+    attend_low,
+    qkv,
+    raw,
+    inverse,
+    pair_gains,
+    cosine,
+    sine,
+    partial,
+    n,
+    n_dp,
+    identity,
+):
+    rows, width = back_all.shape
+    weight_rows = width // (n * n_dp)
+    pair = pair_gains.shape[1]
+    cols = pair // 2
+    heads = cols // HEAD_DIM
+    chunk, wide = 256, 512
+    tok_rows = rows // n
+    half_rows = tok_rows // 2
+    bf16, f32 = jnp.bfloat16, jnp.float32
+    scale = HEAD_DIM ** (-0.5)
+
+    def body(
+        back_ref,
+        out_ref,
+        in_ref,
+        probs_ref,
+        attend_ref,
+        qkv_ref,
+        raw_ref,
+        inverse_ref,
+        pair_ref,
+        cos_ref,
+        sin_ref,
+        part_ref,
+        raw_back,
+        row_part,
+        pair_sum,
+        part_sum,
+        out_sum,
+        out_s,
+        in_s,
+        probs_s,
+        part_s,
+        attend_back,
+        pair_s,
+        value_s,
+        sum_s,
+        slots,
+        flat,
+        got,
+        sum_send,
+        sum_receive,
+        ring_send,
+        ring_receive,
+        load,
+        out_p,
+        out_core,
+        out_chip,
+        pass_send,
+        pass_receive,
+    ):
+        ring = Ring(n)
+        dp, core, chip, core_chip = partners()
+        loads = [
+            pltpu.make_async_copy(part_ref, part_s, load.at[0]),
+            pltpu.make_async_copy(
+                out_ref.at[pl.ds(pl.multiple_of(ring.me * cols, 16), cols)], out_s, load.at[1]
+            ),
+            pltpu.make_async_copy(probs_ref, probs_s, load.at[2]),
+            pltpu.make_async_copy(in_ref.at[:, pl.ds(0, pair + cols)], in_s, load.at[3]),
+        ]
+        for copy in loads:
+            copy.start()
+        ring.barrier(
+            [{"ctx": (ring.me + k) % n} for k in range(1, n)] + [{"dp": core}, {"dp": chip}]
+        )
+
+        def store(half, total):
+            part_sum[pl.ds(half * half_rows, half_rows)] = total
+
+        steps = scatter_steps(
+            ring,
+            lambda device, half: part_s.at[
+                pl.ds(pl.multiple_of(device * tok_rows + half * half_rows, 16), half_rows)
+            ],
+            slots,
+            store,
+            ring_send,
+            ring_receive,
+        )
+        loads[0].wait()
+        advance(steps, 1)
+        lanes = lax.broadcasted_iota(jnp.int32, (chunk, LANES), 1)
+
+        def chunks(step, count=2):
+            total = rows // chunk
+            for first in range(0, total, count):
+                lax.fori_loop(first, min(first + count, total), step, 0)
+                advance(steps, 2)
+
+        loads[1].wait()
+
+        def project(j, carry):
+            at = pl.ds(pl.multiple_of(j * chunk, chunk), chunk)
+            attend_back[at] = dot_across(back_ref[at], out_s[...]).astype(bf16)
+            return carry
+
+        chunks(project, 4)
+
+        def out_product(group):
+            for t in range(width // wide):
+                value = lax.dot_general(
+                    attend_ref[:, group * LANES : (group + 1) * LANES],
+                    back_ref[:, t * wide : (t + 1) * wide],
+                    (((0,), (0,)), ((), ())),
+                    preferred_element_type=f32,
+                ).astype(bf16)
+                for k in range(LANES // weight_rows):
+                    out_p[group * LANES // weight_rows + k, :, t * wide : (t + 1) * wide] = value[
+                        k * weight_rows : (k + 1) * weight_rows
+                    ]
+
+        for group in range(cols // LANES):
+            out_product(group)
+
+        def passing(at, source, target, to):
+            return remote(source, target, pass_send.at[at], pass_receive.at[at], {"dp": to})
+
+        passed = [
+            passing(0, out_p.at[core_chip], out_core.at[1], core),
+            passing(1, out_p.at[core], out_core.at[0], core),
+        ]
+        for copy in passed:
+            copy.start()
+        loads[2].wait()
+        for head in range(heads):
+            columns = pl.ds(head * HEAD_DIM, HEAD_DIM)
+            key_columns = pl.ds(cols + head * HEAD_DIM, HEAD_DIM)
+            value_columns = pl.ds(pair + head * HEAD_DIM, HEAD_DIM)
+            pair_s[:, key_columns] = jnp.zeros((rows, HEAD_DIM), f32)
+            value_s[:, columns] = jnp.zeros((rows, HEAD_DIM), f32)
+
+            def scores(j, carry, head=head, columns=columns, key_columns=key_columns, value_columns=value_columns):
+                at = pl.ds(pl.multiple_of(j * chunk, chunk), chunk)
+                back = attend_back[at, columns]
+                delta = jnp.sum(
+                    back.astype(f32) * attend_ref[at, columns].astype(f32), axis=-1, keepdims=True
+                )
+                probs_low = probs_s[head, at]
+                score_back = (
+                    probs_low.astype(f32) * (dot_across(back, qkv_ref[:, value_columns]) - delta)
+                ).astype(bf16)
+                pair_s[at, columns] = dot(score_back, qkv_ref[:, key_columns])
+                over = (((0,), (0,)), ((), ()))
+                pair_s[:, key_columns] += lax.dot_general(
+                    score_back, qkv_ref[at, columns], over, preferred_element_type=f32
+                )
+                value_s[:, columns] += lax.dot_general(
+                    probs_low, back, over, preferred_element_type=f32
+                )
+                return carry
+
+            chunks(scores)
+        passed[0].wait_recv()
+        out_core[1] = (out_core[1].astype(f32) + out_p[chip].astype(f32)).astype(bf16)
+        passed.append(passing(2, out_core.at[1], out_chip, chip))
+        passed[-1].start()
+        pair_sum[...] = jnp.zeros((8, pair), f32)
+
+        def unturn(j, carry):
+            at = pl.ds(pl.multiple_of(j * chunk, chunk), chunk)
+            held = jnp.zeros((chunk, LANES), f32)
+            for which in range(2):
+                total = jnp.zeros((chunk, 1), f32)
+                for head in range(heads):
+                    columns = pl.ds(which * cols + head * HEAD_DIM, HEAD_DIM)
+                    back = turn(pair_s[at, columns] * scale, cos_ref[at], -sin_ref[at])
+                    normed = raw_ref[at, columns] * inverse_ref[at, which : which + 1]
+                    pair_sum[0:1, columns] += jnp.sum(back * normed, axis=0, keepdims=True)
+                    back = back * pair_ref[0:1, columns]
+                    pair_s[at, columns] = back
+                    total = total + jnp.sum(back * normed, axis=-1, keepdims=True)
+                held = jnp.where(lanes == which, total, held)
+            sum_s[at] = held
+            return carry
+
+        chunks(unturn)
+        exchange_rows(ring, sum_s, flat, got, sum_send, sum_receive, steps)
+        loads[3].wait()
+
+        def finish(j, carry):
+            at = pl.ds(pl.multiple_of(j * chunk, chunk), chunk)
+            for which in range(2):
+                columns = pl.ds(which * cols, cols)
+                factor = inverse_ref[at, which : which + 1]
+                normed = raw_ref[at, columns] * factor
+                mean = sum_s[at, which : which + 1] / width
+                raw_back[at, columns] = (factor * (pair_s[at, columns] - normed * mean)).astype(bf16)
+            raw_back[at, pl.ds(pair, cols)] = value_s[at].astype(bf16)
+            for t in range(width // wide):
+                row_part[at, pl.ds(t * wide, wide)] = dot_across(
+                    raw_back[at], in_s[pl.ds(t * wide, wide), :]
+                ).astype(bf16)
+            return carry
+
+        chunks(finish)
+        passed[1].wait_recv()
+        passed[2].wait_recv()
+        out_sum[...] = (
+            out_core[0].astype(f32) + out_p[dp].astype(f32) + out_chip[...].astype(f32)
+        ).astype(bf16)
+        advance(steps, 64)
+        for copy in passed:
+            copy.wait_send()
+
+    return pl.pallas_call(
+        body,
+        out_shape=(
+            jax.ShapeDtypeStruct((rows, 3 * cols), bf16),
+            jax.ShapeDtypeStruct((rows, width), bf16),
+            jax.ShapeDtypeStruct((8, pair), f32),
+            jax.ShapeDtypeStruct((tok_rows, width), f32),
+            jax.ShapeDtypeStruct((weight_rows, width), bf16),
+        ),
+        in_specs=[VMEM] + [ANY] * 3 + [VMEM] * 7 + [ANY],
+        out_specs=(VMEM,) * 5,
+        scratch_shapes=[
+            pltpu.VMEM((cols, width), bf16),
+            pltpu.VMEM((width, pair + cols), bf16),
+            pltpu.VMEM((heads, rows, rows), bf16),
+            pltpu.VMEM((rows, width), bf16),
+            pltpu.VMEM((rows, cols), bf16),
+            pltpu.VMEM((rows, pair), f32),
+            pltpu.VMEM((rows, cols), f32),
+            pltpu.VMEM((rows, LANES), f32),
+            pltpu.VMEM((2, 2, n // 2, half_rows, width), bf16),
+            pltpu.VMEM((8, rows), f32),
+            pltpu.VMEM((n - 1, 8, rows), f32),
+            sems(n - 1),
+            sems(n - 1),
+            sems(2, 2, n // 2),
+            sems(2, 2, n // 2),
+            sems(4),
+            pltpu.VMEM((n_dp, weight_rows, width), bf16),
+            pltpu.VMEM((2, weight_rows, width), bf16),
+            pltpu.VMEM((weight_rows, width), bf16),
+            sems(3),
+            sems(3),
+        ],
+        name="attention_back",
+        cost_estimate=pl.CostEstimate(
+            flops=2 * rows * width * 4 * cols, bytes_accessed=160_000_000, transcendentals=0
+        ),
+        compiler_params=pltpu.CompilerParams(
+            collective_id=identity, has_side_effects=True, vmem_limit_bytes=BIG_VMEM
+        ),
+    )(
+        back_all,
+        out_all,
+        in_all,
+        probs,
+        attend_low,
+        qkv,
+        raw,
+        inverse,
+        pair_gains,
+        cosine,
+        sine,
+        partial,
+    )
 
 
 def heads_local(
@@ -1753,26 +2214,16 @@
         ],
         axis=2,
     )
-    token_all, named_all, in_all, out_all = gather_inputs(
-        tokens[0], named, in_blocks, project_out, n, n_dp, 1
-    )
+    token_all, named_all, in_all = gather_inputs(tokens[0], named, in_blocks, n, n_dp, 1)
     named_all = named_all.reshape(rows, LANES)
     in_all = in_all.reshape(width, 3 * cols + LANES)
-    in_own, small_all = in_all[:, : 3 * cols], in_all[:, 3 * cols :]
+    small_all = in_all[:, 3 * cols :]
     gains = small_all[:, :4].astype(f32)
     router_all = small_all[:, 4 : 4 + expert_count]
     router_wide = jnp.pad(router_all, ((0, 0), (0, LANES - expert_count)))
     first = lax.all_gather(expert_in, "dp", axis=1, tiled=True)
     second = lax.all_gather(expert_out, "dp", axis=1, tiled=True).reshape(local_experts * FF, width)
 
-    def sum_ctx(values):
-        shape = values.shape
-        block = values.reshape(-1, LANES)
-        got = direct_exchange(
-            jnp.broadcast_to(block[None], (n,) + block.shape), n, 2, "exchange"
-        )
-        return jnp.sum(got, axis=0).reshape(shape)
-
     half_rows = tok_rows // 2
 
     def dealt(row):
@@ -1781,34 +2232,30 @@
 
     places = dealt(jnp.arange(rows, dtype=jnp.int32))
     document_row = document_ids[0]
-    documents = dealt(document_row)
-    relative = places - dealt(document_starts(document_row))
+    starts = dealt(document_starts(document_row))
+    relative = places - starts
     cosine, sine = rotary_tables(relative, HEAD_DIM)
-    visible = (documents[None, :] == documents[:, None]) & (places[None, :] <= places[:, None])
-
-    inputs = token_all.astype(f32)
-    attend_inverse = inverse_rms(inputs)
-    attend_in = (inputs * attend_inverse * gains[:, 0]).astype(bf16)
-    projected = jnp.dot(attend_in, in_own, preferred_element_type=f32)
-    raw = projected[:, : 2 * cols].reshape(rows, 2, cols)
-    squares = sum_ctx(jnp.sum(raw * raw, axis=-1))
-    inverse = lax.rsqrt(squares / width + EPSILON)[..., None]
-    normed = raw * inverse
-    pair_gains = own(gains, cols)[:, 1:3].T
-    rotated = rotate((normed * pair_gains).reshape(rows, 2 * own_heads, HEAD_DIM), cosine, sine)
-    rotated = rotated.reshape(rows, 2, own_heads, HEAD_DIM).astype(bf16)
-    query, key = rotated[:, 0], rotated[:, 1]
-    value = projected[:, 2 * cols :].astype(bf16).reshape(rows, own_heads, HEAD_DIM)
-
-    scores = jnp.einsum("thd,khd->htk", query, key, preferred_element_type=f32) * score_scale
-    scores = jnp.where(visible[None], scores, MASKED)
-    peak = jnp.max(scores, axis=-1, keepdims=True)
-    powers = jnp.where(visible[None], jnp.exp(scores - peak), 0.0)
-    total = jnp.sum(powers, axis=-1, keepdims=True)
-    probs = (powers / total).astype(bf16)
-    attend_out = jnp.einsum("htk,khd->thd", probs, value, preferred_element_type=f32)
-    attend_low = attend_out.reshape(rows, cols).astype(bf16)
-    attend_all = ring_gather(attend_low, n, 3, "gather_attention", axis=1)
+    cosine = jnp.concatenate([cosine[:, 0], cosine[:, 0]], axis=-1)
+    sine = jnp.concatenate([-sine[:, 0], sine[:, 0]], axis=-1)
+    bounds = jnp.pad(jnp.stack([starts, places], axis=1), ((0, 0), (0, LANES - 2)))
+    place_row = jnp.broadcast_to(places[None], (8, rows))
+    pair_gains = jnp.broadcast_to(own(gains, cols)[:, 1:3].T.reshape(1, 2 * cols), (8, 2 * cols))
+
+    attend_gain = jnp.broadcast_to(gains[:, 0][None], (8, width))
+    attend_all, out_all, probs, attend_in, attend_low, qkv, raw, inverse = attention_in(
+        token_all,
+        in_all,
+        project_out,
+        attend_gain,
+        pair_gains,
+        cosine,
+        sine,
+        bounds,
+        place_row,
+        n,
+        n_dp,
+        10,
+    )
 
     upstream_all, mixed_all, gated_all, up_all, own_gates, gate_back, own_residual = experts_in(
         attend_all,
@@ -1827,13 +2274,18 @@
     second_back = jnp.einsum(
         "tf,td->fd", gated_all, upstream_all.reshape(rows, width), preferred_element_type=f32
     ).astype(bf16)
-    first_backs = [
-        jnp.einsum("td,tf->df", mixed_slots, up_all[x], preferred_element_type=f32).astype(bf16)
-        for x in range(local_experts)
-    ]
-    second_back, first_backs, up_all = lax.optimization_barrier(
-        (second_back, first_backs, up_all)
-    )
+    first_backs, last = [], second_back
+    for x in range(local_experts):
+        mixed_slots, last = lax.optimization_barrier((mixed_slots, last))
+        if x == 0:
+            second_back = last
+        else:
+            first_backs.append(last)
+        last = jnp.einsum(
+            "td,tf->df", mixed_slots, up_all[x], preferred_element_type=f32
+        ).astype(bf16)
+    up_all, last = lax.optimization_barrier((up_all, last))
+    first_backs.append(last)
     expert_out_gradient = lax.psum_scatter(
         second_back.reshape(local_experts, FF, width), "dp", scatter_dimension=1, tiled=True
     ).astype(f32)
@@ -1861,7 +2313,7 @@
         gate_back - jnp.sum(own_gates * gate_back, axis=-1, keepdims=True)
     )
     logit_back = chosen_back.astype(bf16)
-    router_part = jnp.einsum("td,te->de", own_mixed, logit_back, preferred_element_type=f32)
+    router_part = jnp.einsum("td,te->ed", own_mixed, logit_back, preferred_element_type=f32)
     mixed_back = mixed_back + jnp.einsum(
         "te,de->td", logit_back, router_all, preferred_element_type=f32
     )
@@ -1869,70 +2321,63 @@
     residual_back = cotangent[0].astype(f32) + normalize_back(
         mixed_back * gains[:, 3], own_mixed_normed, own_mixed_inverse
     )
-    back_all, mixture = gather_and_scatter(residual_back.astype(bf16), mixture, n, 5)
+    back_all = ring_gather(residual_back.astype(bf16), n, 5, "gather_back")
+
+    raw_back, row_part, pair_sum, mixture, out_part = attention_back(
+        back_all,
+        out_all,
+        in_all,
+        probs,
+        attend_low,
+        qkv,
+        raw,
+        inverse,
+        pair_gains,
+        cosine,
+        sine,
+        mixture,
+        n,
+        n_dp,
+        11,
+    )
     layer_output = (own_residual + mixture).astype(bf16)
-
-    out_part = jnp.einsum("td,te->de", attend_low, back_all, preferred_element_type=f32)
-    attend_back = jnp.einsum(
-        "td,ed->te", back_all, own(out_all, cols), preferred_element_type=f32
-    ).astype(bf16).reshape(rows, own_heads, HEAD_DIM)
-    delta = jnp.einsum("thd,thd->ht", attend_back.astype(f32), attend_out)[..., None]
-    prob_back = jnp.einsum("thd,khd->htk", attend_back, value, preferred_element_type=f32)
-    score_back = (probs.astype(f32) * (prob_back - delta)).astype(bf16)
-    query_back = jnp.einsum("htk,khd->thd", score_back, key, preferred_element_type=f32)
-    key_back = jnp.einsum("htk,thd->khd", score_back, query, preferred_element_type=f32)
-    value_back = jnp.einsum("htk,thd->khd", probs, attend_back, preferred_element_type=f32)
-    pair_back = jnp.concatenate([query_back, key_back], axis=1) * score_scale
-    pair_back = rotate(pair_back, cosine, -sine).reshape(rows, 2, cols)
-    pair_gain_back = jnp.sum(pair_back * normed, axis=0)
-    pair_back = pair_back * pair_gains
-    means = sum_ctx(jnp.sum(pair_back * normed, axis=-1))[..., None] / width
-    pair_back = inverse * (pair_back - normed * means)
-    raw_back = jnp.concatenate(
-        [pair_back.reshape(rows, 2 * cols), value_back.reshape(rows, cols)], axis=-1
-    ).astype(bf16)
-    row_part = jnp.einsum("tf,df->td", raw_back, in_own, preferred_element_type=f32).astype(bf16)
-    in_part = jnp.einsum("td,tf->df", attend_in, raw_back, preferred_element_type=f32).astype(bf16)
-    attend_in_back, in_part, out_part = scatter_end(
-        row_part,
-        in_part.reshape(n_dp, n, weight_rows, 3 * cols),
-        out_part.astype(bf16).reshape(n_dp, weight_rows, width),
-        n,
-        6,
-    )
     pairs = [(d * n + c, c * n_dp + d) for d in range(n_dp) for c in range(n)]
     project_out_gradient = lax.ppermute(out_part, ("dp", "ctx"), pairs).astype(f32)
-    in_part = in_part.reshape(n, weight_rows, 3, cols)
-    project_in_gradient = in_part.transpose(1, 2, 0, 3).reshape(weight_rows, 3 * width).astype(f32)
-
-    own_inverse = own(attend_inverse, tok_rows)
-    own_normed = tokens[0].astype(f32) * own_inverse
-    attend_gain_back = jnp.sum(attend_in_back * own_normed, axis=0)
-    tokens_back = residual_back + normalize_back(
-        attend_in_back * gains[:, 0], own_normed, own_inverse
-    )
-    pair_columns = lax.dynamic_update_slice_in_dim(
-        jnp.zeros((width, 2), f32), pair_gain_back.T, me * cols, 0
-    )
+
+    small_rows = -(-(4 + expert_count) // 8) * 8
     small_part = jnp.concatenate(
-        [attend_gain_back[:, None], pair_columns, mixed_gain_back[:, None], router_part], axis=1
-    )
-    small_width = small_part.shape[1]
-    small_rows = -(-weight_rows * small_width // (8 * LANES)) * 8
-    small_part = jnp.pad(
-        small_part.reshape(n_dp * n, weight_rows * small_width),
-        ((0, 0), (0, small_rows * LANES - weight_rows * small_width)),
-    )
-    small_gradient = small_scatter(small_part.reshape(n_dp, n, small_rows, LANES), n, n_dp, 7)
-    small_gradient = small_gradient.reshape(-1)[: weight_rows * small_width]
-    small_gradient = small_gradient.reshape(weight_rows, small_width)
+        [
+            jnp.zeros((3, width), f32),
+            mixed_gain_back[None],
+            router_part,
+            jnp.zeros((small_rows - 4 - expert_count, width), f32),
+        ],
+        axis=0,
+    )
+    tokens_back, project_in_gradient, small_gradient = scatter_end(
+        row_part,
+        attend_in,
+        raw_back,
+        tokens[0],
+        residual_back,
+        attend_gain,
+        small_part,
+        pair_sum,
+        n,
+        n_dp,
+        6,
+    )
+    per_tile = LANES // weight_rows
+    small_gradient = lax.dynamic_slice_in_dim(
+        small_gradient, me % per_tile * weight_rows, weight_rows, 1
+    ).T
     return (
         layer_output[None],
-        tokens_back.astype(bf16)[None],
+        tokens_back[None],
         small_gradient[:, :4],
         project_in_gradient,
         project_out_gradient,
-        small_gradient[:, 4:],
+        small_gradient[:, 4 : 4 + expert_count],
         expert_in_gradient,
         expert_out_gradient,
     )

time: 676 us -> 633 us (0.936)
  matrix products: 78.6 us -> 44 us
  local copies, waits for them, and re-layouts: 46 us -> 20.5 us
  other arithmetic: 36.4 us -> 18.3 us
  Pallas kernels: 485 us -> 503 us
  waiting for transfers between devices: 2.46 us -> 18.9 us
    pallas_call x5 -> x3, Pallas kernels: 191 us -> 267 us  [the longest x1 114 us: attention_in(): pl.pallas_call(body, out_shape=(jax.ShapeDtypeStruct((rows, width), bf16)...]
    pallas_call x1, Pallas kernels: 110 us -> 77.3 us  [gather_inputs(): kernel_call(body, (jax.ShapeDtypeStruct((tok_rows * n, width), tokens.dty...]
    dot_general x11 -> x1, matrix products: 28 us -> 1.26 us  [heads_local(): jnp.einsum('td,te->ed', own_mixed, logit_back, preferred_element_type=f32)]
    ppermute x1, waiting for transfers between devices: 0.01 us -> 16.9 us  [heads_local(): lax.ppermute(out_part, ('dp', 'ctx'), pairs).astype(f32)]
    pallas_call x1, Pallas kernels: 79.8 us -> 66.9 us  [experts_in(): pl.pallas_call(body, out_shape=(jax.ShapeDtypeStruct((n, tok_rows, width)...]
    pallas_call x1, Pallas kernels: 63.7 us -> 52.4 us  [experts_out(): pl.pallas_call(body, out_shape=(jax.ShapeDtypeStruct((tok_rows, width), f...]
    broadcast_in_dim x32, local copies, waits for them, and re-layouts: 10.5 us -> 2.13 us  [heads_local(): jnp.where((jnp.arange(n) == ring_device((place + offset + n) % n, n))[:,...]
    unnamed x107 -> x46, local copies, waits for them, and re-layouts: 13.9 us -> 8.3 us
  transfers between devices with their start and end apart: 6 -> 6, of which waited for: 0 -> 1; matrix products, arithmetic and copies ran while one was open for 16% -> 7% of each run, Pallas kernels for 61% -> 70%
where the time goes in v4:
time: 633 us; the launch traced here: 624 us
  Pallas kernels  503 us (79%)
  matrix products  44 us (7%)
  local copies, waits for them, and re-layouts  20.5 us (3%)
  waiting for transfers between devices  18.9 us (3%)
  other arithmetic  18.3 us (3%)
  between operations  15.1 us (2%)
    pallas_call x1, Pallas kernels, attention_in(): pl.pallas_call(body, out_shape=(jax.ShapeDtypeStruct((rows, width), bf16)...  114 us
    pallas_call x1, Pallas kernels, scatter_end(): kernel_call(body, (jax.ShapeDtypeStruct((rows, width), bf16), jax.ShapeDt...  91.3 us
    pallas_call x1, Pallas kernels, gather_inputs(): kernel_call(body, (jax.ShapeDtypeStruct((tok_rows * n, width), tokens.dty...  77.3 us
    pallas_call x1, Pallas kernels, experts_in(): pl.pallas_call(body, out_shape=(jax.ShapeDtypeStruct((n, tok_rows, width)...  66.9 us
    pallas_call x1, Pallas kernels, attention_back(): pl.pallas_call(body, out_shape=(jax.ShapeDtypeStruct((rows, 3 * cols), bf...  61 us
    pallas_call x1, Pallas kernels, experts_out(): pl.pallas_call(body, out_shape=(jax.ShapeDtypeStruct((tok_rows, width), f...  52.4 us
    pallas_call x1, Pallas kernels, ring_gather(): kernel_call(body, jax.ShapeDtypeStruct(shape, block.dtype), [ANY], ANY, [...  39.9 us
    dot_general x2, matrix products, heads_local(): jnp.einsum('td,tf->df', mixed_slots, up_all[x], preferred_element_type=f32)  26.3 us
  transfers between devices with their start and end apart: 6, of which 1 were waited for; matrix products, arithmetic and copies ran while one was open for 7% of the time, Pallas kernels for 70%

profile of v4, /device:TPU:1, one launch (start us, length us, event | category | flops | bytes accessed | tf_op | source)
XLA Modules:
  0.0 623.7 jit_solution(418362367136732000)
XLA Ops:
  10.9 0.8 pad.8.bound_ref
  12.4 0.9 reshape.167
  13.6 77.3 %gather_inputs.1 = (bf16[1024,2048]{1,0:T(8,128)(2,1)}, bf16[8,128,128]{2,1,0:T(8,128)(2,1)S(1)}, bf16[4,8,64,896]{3,2,1,0:T(8,128)(2,1)S(1)}) custom-call(bf16[128,2048]{1,0:T(8,128)(2,1)S(1)} %bitcast.92, bf16[128,128]{1,0:T(8,128)(2,1)S(1)} %convert_element_type.45.named_ref, bf16[8,64,896]{2,1,0:T(8,128)(2,1)S(1)} %pad_maximum_fusion.in_ref), custom_call_target="tpu_custom_call" | custom-call | bytes 200000000 | tf_op jit(solution)/shard_map/gather_inputs/pallas_call | solution.py:805
  91.0 1.8 copy-done.1
  93.0 0.9 pad.9.router_ref
  93.9 1.1 slice_convert_fusion
  95.2 1.9 fusion.9
  97.2 1.3 pad_maximum_fusion.1
  98.5 0.9 slice_reduce_fusion
  101.2 114.4 %attention_in.1 = (bf16[1024,2048]{1,0:T(8,128)(2,1)}, bf16[2048,2048]{1,0:T(8,128)(2,1)}, bf16[2,1024,1024]{2,1,0:T(8,128)(2,1)}, bf16[1024,2048]{1,0:T(8,128)(...) custom-call(bf16[1024,2048]{1,0:T(8,128)(2,1)} %get-tuple-element.43.to, ...), custom_call_target="tpu_custom_call" | custom-call | flops 3221225472 | bytes 200000000 | tf_op jit(solution)/shard_map/attention_in/pallas_call | solution.py:1856
  216.3 66.9 %experts_in.1 = (bf16[8,128,2048]{2,1,0:T(8,128)(2,1)}, bf16[8,128,2048]{2,1,0:T(8,128)(2,1)}, bf16[1024,2048]{1,0:T(8,128)(2,1)}, bf16[2,1024,2048]{2,1,0:T(8,1...) custom-call(bf16[1024,2048]{1,0:T(8,128)(2,1)} %get-tuple-element.45.attend_ref, ...), custom_call_target="tpu_custom_call" | custom-call | flops 34359738368 | bytes 60000000 | tf_op jit(solution)/shard_map/experts_in/pallas_call | solution.py:1334
  283.3 14.5 %convolution_convert_fusion.2 = bf16[2048,2048]{1,0:T(8,128)(2,1)} fusion(bf16[1024,2048]{1,0:T(8,128)(2,1)} %get-tuple-element.51.gated_ref, bf16[1024,2048]{1,0:T(8,128)(2,1)} %bitcast.123), kind=kOutput, calls=%fused_computation.2 | convolution fusion | flops 8594128896 | bytes 16777216 | tf_op jit(solution)/shard_map/tf,td->fd/dot_general | solution.py:2274
  297.7 11.4 %convolution_convert_fusion.1 = bf16[2048,2048]{1,0:T(8,128)(2,1)} fusion(bf16[1024,2048]{1,0:T(8,128)(2,1)S(1)} %bitcast.104, bf16[2,1024,2048]{2,1,0:T(8,128)(2,1)S(1)} %copy-done.19), kind=kOutput, calls=%fused_computation.1 | convolution fusion | flops 8594128896 | bytes 16777216 | tf_op jit(solution)/shard_map/td,tf->df/dot_general | solution.py:2284
  309.2 14.8 %convolution_convert_fusion = bf16[2048,2048]{1,0:T(8,128)(2,1)} fusion(bf16[1024,2048]{1,0:T(8,128)(2,1)} %bitcast.103, bf16[2,1024,2048]{2,1,0:T(8,128)(2,1)} %get-tuple-element.55.up_ref), kind=kOutput, calls=%fused_computation | convolution fusion | flops 8594128896 | bytes 16777216 | tf_op jit(solution)/shard_map/td,tf->df/dot_general | solution.py:2284
  326.6 52.4 %experts_out.1 = (f32[128,2048]{1,0:T(8,128)}, bf16[1024,2048]{1,0:T(8,128)(2,1)}, f32[8,8,128]{2,1,0:T(8,128)}) custom-call(bf16[2,1024,2048]{2,1,0:T(8,128)(2,1)} %get-tuple-element.55.up_ref, bf16[1024,2048]{1,0:T(8,128)(2,1)} %get-tuple-element.51.gated_ref, bf16[2,2048,2048]{2,1,0:T(8,128)(2,1)} %all-gather.3.cloned.1.call-done.first_ref, ...), custom_call_target="tpu_custom_call" | custom-call | flops 25769803776 | bytes 60000000 | tf_op jit(solution)/shard_map/experts_out/pallas_call | solution.py:1582
  379.0 0.8 slice_bitcast_fusion.7
  381.0 2.0 multiply_reduce_fusion
  383.4 39.9 %gather_back.1.back_ref = bf16[1024,2048]{1,0:T(8,128)(2,1)S(1)} custom-call(bf16[128,2048]{1,0:T(8,128)(2,1)S(1)} %get-tuple-element.82.block_ref), custom_call_target="tpu_custom_call" | custom-call | bytes 134217728 | tf_op jit(solution)/shard_map/gather_back/pallas_call | solution.py:644
  423.3 2.0 copy-done
  425.3 1.3 fusion.5
  426.6 61.0 %attention_back.1 = (bf16[1024,768]{1,0:T(8,128)(2,1)}, bf16[1024,2048]{1,0:T(8,128)(2,1)}, f32[8,512]{1,0:T(8,128)}, f32[128,2048]{1,0:T(8,128)}, bf16[64,2048]{1,0:T(8,128)(2,1)}) custom-call(bf16[1024,2048]{1,0:T(8,128)(2,1)} %copy-done, bf16[2048,2048]{1,0:T(8,128)(2,1)} %get-tuple-element.46.out_ref, bf16[2048,896]{1,0:T(8,128)(2,1)} %bitcast.91, ...), custom_call_target="tpu_custom_call" | custom-call | flops 4294967296 | bytes 160000000 | tf_op jit(solution)/shard_map/attention_back/pallas_call | solution.py:2120
  487.8 1.4 copy-done.3
  489.2 0.7 copy-done.5
  489.9 91.3 %scatter_end.1 = (bf16[128,2048]{1,0:T(8,128)(2,1)S(1)}, f32[64,6144]{1,0:T(8,128)S(1)}, f32[24,128]{1,0:T(8,128)S(1)}) custom-call(bf16[1024,2048]{1,0:T(8,128)(2,1)} %get-tuple-element.67.row_ref, bf16[1024,2048]{1,0:T(8,128)(2,1)} %get-tuple-element.68.attend_ref, bf16[1024,768]{1,0:T(8,128)(2,1)S(1)} %copy-done.3, bf16[128,2048]{1,0:T(8,128)(2,1)S(1)} %bitcast.93, ...), custom_call_target="tpu_custom_call" | custom-call | bytes 200000000 | tf_op jit(solution)/shard_map/scatter_end/pallas_call | solution.py:1028
  582.5 3.4 collective-permute-start
  585.9 0.9 fusion.4
  586.8 16.9 %collective-permute-done = bf16[64,2048]{1,0:T(8,128)(2,1)S(1)} collective-permute-done((bf16[64,2048]{1,0:T(8,128)(2,1)S(1)}, bf16[64,2048]{1,0:T(8,128)(2,1)S(1)}, u32[]{:S(2)}, u32[]{:S(2)}) %collective-permute-start) | collective-permute-done | bytes 262176 | tf_op jit(solution)/shard_map/ppermute | solution.py:2345
  603.7 0.8 convert_element_type.55
  604.6 6.2 maximum_convert_fusion
  610.7 4.1 convert_element_type.57
  614.9 0.8 copy.87
  615.6 1.1 copy.88
  (149 shorter events, 12.4 us)
Async XLA Ops:
  7.2 1.6 copy-start.14
  7.2 2.9 copy-start.17
  7.2 3.0 copy-start.15
  7.2 3.1 copy-start.16
  7.2 4.6 copy-start.10
  7.2 208.4 %all-gather.5.cloned.1.call-start = ((), (), s32[]{:S(2)}) async-start(), calls=%async_computation.4 | async-start | bytes 10485760 | tf_op jit(solution)/shard_map/all_gather | solution.py:2225
  8.0 207.7 %all-gather.3.cloned.1.call-start = ((), (), s32[]{:S(2)}) async-start(), calls=%async_computation.3 | async-start | bytes 20971520 | tf_op jit(solution)/shard_map/all_gather | solution.py:2224
  8.7 595.9 %reduce-scatter.4.cloned.1.call-start = ((), (), s32[]{:S(2)}) async-start(), calls=%async_computation.5 | async-start | bytes 10485760 | tf_op jit(solution)/shard_map/reduce_scatter | solution.py:2293
  10.9 2.7 copy-start.2
  91.0 1.8 copy-start.1
  91.0 8.4 %copy-start.6 = (bf16[8,128,128]{2,1,0:T(8,128)(2,1)}, bf16[8,128,128]{2,1,0:T(8,128)(2,1)S(1)}, u32[]{:S(2)}) copy-start(bf16[8,128,128]{2,1,0:T(8,128)(2,1)S(1)} %get-tuple-element.47) | copy-start | bytes 786436
  283.2 14.5 %copy-start.13 = (bf16[8,128,2048]{2,1,0:T(8,128)(2,1)S(1)}, bf16[8,128,2048]{2,1,0:T(8,128)(2,1)}, u32[]{:S(2)}) copy-start(bf16[8,128,2048]{2,1,0:T(8,128)(2,1)} %get-tuple-element.50) | copy-start | bytes 12582916
  283.2 14.5 %copy-start.19 = (bf16[2,1024,2048]{2,1,0:T(8,128)(2,1)S(1)}, bf16[2,1024,2048]{2,1,0:T(8,128)(2,1)}, u32[]{:S(2)}) copy-start(bf16[2,1024,2048]{2,1,0:T(8,128)(2,1)} %get-tuple-element.55.up_ref) | copy-start | bytes 25165828
  309.2 295.4 %reduce-scatter.6.cloned.1.call-start = ((), (), s32[]{:S(2)}) async-start(), calls=%async_computation.6 | async-start | bytes 10485760 | tf_op jit(solution)/shard_map/reduce_scatter | solution.py:2293
  324.1 286.6 %reduce-scatter.8.cloned.1.call-start = ((), (), s32[]{:S(2)}) async-start(), calls=%async_computation.7 | async-start | bytes 10485760 | tf_op jit(solution)/shard_map/reduce_scatter | solution.py:2289
  326.6 54.0 %copy-start.7 = (f32[128,2048]{1,0:T(8,128)S(1)}, f32[128,2048]{1,0:T(8,128)}, u32[]{:S(2)}) copy-start(f32[128,2048]{1,0:T(8,128)} %get-tuple-element.48) | copy-start | bytes 3145732
  326.6 54.2 %copy-start.12 = (f32[128,128]{1,0:T(8,128)S(1)}, f32[128,128]{1,0:T(8,128)}, u32[]{:S(2)}) copy-start(f32[128,128]{1,0:T(8,128)} %get-tuple-element.58) | copy-start | bytes 196612
  379.0 4.1 copy-start.11
  423.3 2.0 copy-start
  426.6 61.2 %copy-start.4 = (f32[8,2048]{1,0:T(8,128)S(1)}, f32[8,2048]{1,0:T(8,128)}, u32[]{:S(2)}) copy-start(f32[8,2048]{1,0:T(8,128)} %broadcast_in_dim.198.gain_ref) | copy-start | bytes 196612
  487.8 1.4 copy-start.3
  489.2 0.7 copy-start.5
  489.9 92.6 %copy-start.18 = (bf16[64,2048]{1,0:T(8,128)(2,1)S(1)}, bf16[64,2048]{1,0:T(8,128)(2,1)}, u32[]{:S(2)}) copy-start(bf16[64,2048]{1,0:T(8,128)(2,1)} %get-tuple-element.74) | copy-start | bytes 786436
  489.9 96.0 %copy-start.8 = (f32[128,2048]{1,0:T(8,128)S(1)}, f32[128,2048]{1,0:T(8,128)}, u32[]{:S(2)}) copy-start(f32[128,2048]{1,0:T(8,128)} %get-tuple-element.48) | copy-start | bytes 3145732
  489.9 96.0 %copy-start.9 = (f32[128,2048]{1,0:T(8,128)S(1)}, f32[128,2048]{1,0:T(8,128)}, u32[]{:S(2)}) copy-start(f32[128,2048]{1,0:T(8,128)} %get-tuple-element.66) | copy-start | bytes 3145732
  582.5 21.3 %collective-permute-start = (bf16[64,2048]{1,0:T(8,128)(2,1)S(1)}, bf16[64,2048]{1,0:T(8,128)(2,1)S(1)}, u32[]{:S(2)}, u32[]{:S(2)}) collective-permute-start(bf16[64,2048]{1,0:T(8,128)(2,1)S(1)} %copy-done.18), channel_id=1, source_target_pairs={{0,0},{1,4},{2,8},{3,12},{4,16},{5,20},{6,24},{7,28},{8,1},{9,5},{... | collective-permute-start | bytes 786440 | tf_op jit(solution)/shard_map/ppermute | solution.py:2345
Sparse Core Ops, SparseCore 0:
  9.6 80.4 all-gather.4
  91.7 111.5 all-gather.2
  309.3 74.6 reduce-scatter.3
  387.2 71.7 reduce-scatter.5
  461.4 88.5 reduce-scatter.7

commit v5 on v4

--- a/solution.py
+++ b/solution.py
@@ -14,6 +14,9 @@
 ROPE_BASE = 10000.0
 MASKED = -1e30
 LANES = 128
+PASS_A, PASS_B = 256, 256
+CUTS = 2
+WAITS = (4, 6, 6)
 TILE = 512
 WIDE = 1024
 
@@ -821,7 +824,7 @@
     )(tokens, named, in_blocks)
 
 
-def sum_small_steps(ring, small, core_s, chip_s, quarter, got, total, sem):
+def sum_small_steps(ring, small, near, quarter, got, total, sem):
     pass_send, pass_receive, send, receive = sem
     dp, core, chip, core_chip = partners()
     n, me = ring.n, ring.me
@@ -831,21 +834,19 @@
     def group(at):
         return small.at[:, pl.ds(pl.multiple_of(at * lanes, LANES), lanes)]
 
-    copies = [
-        remote(group(core_chip), core_s.at[1], pass_send.at[0], pass_receive.at[0], {"dp": core}),
-        remote(group(core), core_s.at[0], pass_send.at[1], pass_receive.at[1], {"dp": core}),
-    ]
-    for copy in copies:
-        copy.start()
-    copies[0].wait_recv()
-    core_s[1] = core_s[1] + group(chip)[...]
-    copies.append(
-        remote(core_s.at[1], chip_s, pass_send.at[2], pass_receive.at[2], {"dp": chip})
-    )
-    copies[-1].start()
-    copies[1].wait_recv()
-    copies[2].wait_recv()
-    quarter[...] = group(dp)[...] + core_s[0] + chip_s[...]
+    copies = []
+    for at, to in enumerate((core_chip, chip, core)):
+        copies.append(
+            remote(group(to), near.at[at], pass_send.at[at], pass_receive.at[at], {"dp": to})
+        )
+        copies[-1].start()
+    for _ in range(WAITS[1]):
+        yield
+    value = group(dp)[...]
+    for at in range(3):
+        copies[at].wait_recv()
+        value = value + near[at]
+    quarter[...] = value
 
     def tile(device):
         return quarter.at[:, pl.ds(pl.multiple_of(device // per_tile * LANES, LANES), LANES)]
@@ -856,6 +857,8 @@
             remote(tile(other), got.at[k - 1], send.at[k - 1], receive.at[k - 1], {"ctx": other})
         )
         copies[-1].start()
+    for _ in range(WAITS[2]):
+        yield
     value = tile(me)[...]
     for k in range(1, n):
         copies[2 + k].wait_recv()
@@ -866,7 +869,7 @@
 
 
 def scatter_end(
-    row_part, attend_in, raw_back, tokens, residual_back, gain, small, pair_sum, n, n_dp, identity
+    row_part, attend_in, raw_back, tokens, residual_back, gain, small, pair_sum, far, n, n_dp, identity
 ):
     rows, width = row_part.shape[0] // n, row_part.shape[1]
     half_rows = rows // 2
@@ -886,9 +889,11 @@
         gain_ref,
         small_ref,
         pair_ref,
+        far_ref,
         token_back,
         in_sum,
         small_sum,
+        far_got,
         slots,
         row_s,
         attend_s,
@@ -897,8 +902,7 @@
         in_chip,
         in_got,
         small_s,
-        small_core,
-        small_chip,
+        small_near,
         small_quarter,
         small_got,
         row_send,
@@ -912,6 +916,8 @@
         small_send,
         small_receive,
         load,
+        far_send,
+        far_receive,
     ):
         ring = Ring(n)
         me = ring.me
@@ -919,7 +925,9 @@
         others = [(me + k) % n for k in range(1, n)]
         loaded = pltpu.make_async_copy(attend_ref, attend_s, load)
         loaded.start()
-        ring.barrier([{"ctx": other} for other in others] + [{"dp": core}, {"dp": chip}])
+        ring.barrier(
+            [{"ctx": other} for other in others] + [{"dp": to} for to in (core, chip, core_chip)]
+        )
 
         def part(device, half):
             return row_ref.at[pl.ds(pl.multiple_of(device * rows + half * half_rows, 16), half_rows)]
@@ -927,8 +935,17 @@
         def store(half, total):
             row_s[pl.ds(half * half_rows, half_rows)] = total
 
-        def passing(at, source, target, to):
-            return remote(source, target, pass_send.at[at], pass_receive.at[at], {"dp": to})
+        half_slots = n // CUTS
+
+        def passing(at, k, source, target, to):
+            slots_k = pl.ds(k * half_slots, half_slots)
+            return remote(
+                source.at[slots_k],
+                target.at[slots_k],
+                pass_send.at[at, k],
+                pass_receive.at[at, k],
+                {"dp": to},
+            )
 
         def product(group):
             value = lax.dot_general(
@@ -936,63 +953,84 @@
                 raw_ref[...],
                 (((0,), (0,)), ((), ())),
                 preferred_element_type=f32,
-            )
-            in_part[group] = value.astype(bf16).reshape(n, weight_rows, in_cols)
+            ).astype(bf16)
+            for device in range(n):
+                in_part[group, (device - me + n) % n] = value[
+                    device * weight_rows : (device + 1) * weight_rows
+                ]
 
         def weight_steps():
             loaded.wait()
+            sent = []
             product(core_chip)
-            passed = [passing(0, in_part.at[core_chip], in_core.at[1], core)]
-            passed[-1].start()
+            far = [passing(0, k, in_part.at[core_chip], in_core.at[1], core) for k in range(CUTS)]
+            for copy in far:
+                copy.start()
             yield
             product(core)
-            passed.append(passing(1, in_part.at[core], in_core.at[0], core))
-            passed[-1].start()
+            near = [passing(1, k, in_part.at[core], in_core.at[0], core) for k in range(CUTS)]
+            for copy in near:
+                copy.start()
             yield
             product(chip)
-            passed[0].wait_recv()
-
-            def add_far(k, carry):
-                in_core[1, k] = (in_core[1, k].astype(f32) + in_part[chip, k].astype(f32)).astype(bf16)
-                return carry
-
-            lax.fori_loop(0, n, add_far, 0)
-            passed.append(passing(2, in_core.at[1], in_chip, chip))
-            passed[-1].start()
+            across = []
+            for k in range(CUTS):
+                far[k].wait_recv()
+
+                def add_far(at, carry):
+                    in_core[1, at] = (
+                        in_core[1, at].astype(f32) + in_part[chip, at].astype(f32)
+                    ).astype(bf16)
+                    return carry
+
+                lax.fori_loop(k * half_slots, (k + 1) * half_slots, add_far, 0)
+                across.append(passing(2, k, in_core.at[1], in_chip, chip))
+                across[-1].start()
+            beyond = remote(far_ref.at[1, pl.ds(PASS_B, far_got.shape[0])], far_got, far_send, far_receive, {"dp": chip})
             yield
             product(dp)
-            passed[1].wait_recv()
-            for _ in range(4):
+            for _ in range(2):
                 yield
-            passed[2].wait_recv()
-
-            def add_near(k, carry):
-                in_core[0, k] = (
-                    in_core[0, k].astype(f32) + in_part[dp, k].astype(f32) + in_chip[k].astype(f32)
-                ).astype(bf16)
-                return carry
-
-            lax.fori_loop(0, n, add_near, 0)
-            direct = []
-            for k, other in enumerate(others):
-                direct.append(
-                    remote(in_core.at[0, other], in_got.at[me], in_send.at[k], in_receive.at[k], {"ctx": other})
-                )
-                direct[-1].start()
-            in_got[me] = in_core[0, me]
-            for _ in range(8):
+            for k in range(CUTS):
+                near[k].wait_recv()
+                across[k].wait_recv()
+
+                def add_near(at, carry):
+                    in_core[0, at] = (
+                        in_core[0, at].astype(f32)
+                        + in_part[dp, at].astype(f32)
+                        + in_chip[at].astype(f32)
+                    ).astype(bf16)
+                    return carry
+
+                lax.fori_loop(k * half_slots, (k + 1) * half_slots, add_near, 0)
+                for at in range(max(1, k * half_slots), (k + 1) * half_slots):
+                    sent.append(
+                        remote(
+                            in_core.at[0, at],
+                            in_got.at[at],
+                            in_send.at[at - 1],
+                            in_receive.at[at - 1],
+                            {"ctx": others[at - 1]},
+                        )
+                    )
+                    sent[-1].start()
                 yield
-            for k in range(1, n):
-                spot = in_got.at[(me - k + n) % n]
-                remote(
-                    spot, spot, in_send.at[k - 1], in_receive.at[k - 1], {"ctx": others[k - 1]}
-                ).wait_recv()
-            for device in range(n):
+                yield
+            beyond.start()
+            in_got[0] = in_core[0, 0]
+            for _ in range(6):
+                yield
+            for at in range(n):
+                if at:
+                    sent[at - 1].wait_recv()
+                device = (me - at + n) % n
                 for which in range(3):
-                    in_sum[:, pl.ds(which * width + device * cols, cols)] = in_got[
-                        device, :, pl.ds(which * cols, cols)
-                    ].astype(f32)
-            for copy in passed + direct:
+                    in_sum[
+                        :, pl.ds(pl.multiple_of(which * width + device * cols, LANES), cols)
+                    ] = in_got[at, :, pl.ds(which * cols, cols)].astype(f32)
+            beyond.wait()
+            for copy in far + near + across + sent:
                 copy.wait_send()
 
         def row_steps():
@@ -1001,28 +1039,38 @@
             inverse = lax.rsqrt(jnp.mean(values * values, axis=-1, keepdims=True) + EPSILON)
             normed = values * inverse
             back = row_s[...]
-            small_s[...] = small_ref[...]
-            small_s[0:1, :] = jnp.sum(back * normed, axis=0, keepdims=True)
-            own = pl.ds(pl.multiple_of(me * cols, LANES), cols)
-            small_s[1:2, own] = pair_ref[0:1, :cols]
-            small_s[2:3, own] = pair_ref[0:1, cols:]
             back = back * gain_ref[0:1, :]
             token_back[...] = (
                 back_ref[...]
                 + inverse * (back - normed * jnp.mean(back * normed, axis=-1, keepdims=True))
             ).astype(bf16)
-            sum_small_steps(
+
+        def small_steps():
+            for _ in range(WAITS[0]):
+                yield
+
+            def column_sums(at, total):
+                part_rows = pl.ds(pl.multiple_of(at * rows, rows), rows)
+                terms = row_ref[part_rows].astype(f32) * attend_s[part_rows].astype(f32)
+                return total + jnp.sum(terms, axis=0, keepdims=True)
+
+            total = lax.fori_loop(0, n, column_sums, jnp.zeros((1, width), f32))
+            small_s[...] = small_ref[...]
+            small_s[0:1, :] = total / gain_ref[0:1, :]
+            own = pl.ds(pl.multiple_of(me * cols, LANES), cols)
+            small_s[1:2, own] = pair_ref[0:1, :cols]
+            small_s[2:3, own] = pair_ref[0:1, cols:]
+            yield from sum_small_steps(
                 ring,
                 small_s,
-                small_core,
-                small_chip,
+                small_near,
                 small_quarter,
                 small_got,
                 small_sum,
                 (small_pass_send, small_pass_receive, small_send, small_receive),
             )
 
-        run_steps(row_steps(), weight_steps())
+        run_steps(row_steps(), weight_steps(), small_steps())
 
     block = (n, weight_rows, in_cols)
     return kernel_call(
@@ -1031,9 +1079,10 @@
             jax.ShapeDtypeStruct((rows, width), bf16),
             jax.ShapeDtypeStruct((weight_rows, 3 * width), f32),
             jax.ShapeDtypeStruct((small_rows, LANES), f32),
+            jax.ShapeDtypeStruct((far.shape[1] - PASS_B, far.shape[2]), bf16),
         ),
-        [VMEM, ANY] + [VMEM] * 6,
-        (VMEM,) * 3,
+        [VMEM, ANY] + [VMEM] * 6 + [ANY],
+        (VMEM,) * 3 + (ANY,),
         [
             pltpu.VMEM((2, 2, n // 2, half_rows, width), row_part.dtype),
             pltpu.VMEM((rows, width), f32),
@@ -1043,14 +1092,13 @@
             pltpu.VMEM(block, bf16),
             pltpu.VMEM(block, bf16),
             pltpu.VMEM((small_rows, width), f32),
-            pltpu.VMEM((2, small_rows, span), f32),
-            pltpu.VMEM((small_rows, span), f32),
+            pltpu.VMEM((3, small_rows, span), f32),
             pltpu.VMEM((small_rows, span), f32),
             pltpu.VMEM((n - 1, small_rows, LANES), f32),
             sems(2, 2, n // 2),
             sems(2, 2, n // 2),
-            sems(3),
-            sems(3),
+            sems(3, CUTS),
+            sems(3, CUTS),
             sems(n - 1),
             sems(n - 1),
             sems(3),
@@ -1058,11 +1106,13 @@
             sems(n - 1),
             sems(n - 1),
             pltpu.SemaphoreType.DMA,
+            pltpu.SemaphoreType.DMA,
+            pltpu.SemaphoreType.DMA,
         ],
         identity,
         "scatter_end",
         200_000_000,
-    )(row_part, attend_in, raw_back, tokens, residual_back, gain, small, pair_sum)
+    )(row_part, attend_in, raw_back, tokens, residual_back, gain, small, pair_sum, far)
 
 
 def slot_offsets(n):
@@ -1763,7 +1813,7 @@
             total = rows // chunk
             for first in range(0, total, count):
                 lax.fori_loop(first, min(first + count, total), step, 0)
-                advance(steps, 2)
+                advance(steps, 1)
 
         def project(j, carry):
             at = pl.ds(pl.multiple_of(j * chunk, chunk), chunk)
@@ -1895,6 +1945,157 @@
     )(token_all, in_all, out_rows, gain, pair_gains, cosine, sine, bounds, place_row)
 
 
+def gather_with_gradients(block, mixed, up_all, n, n_dp, identity):
+    rows, width = block.shape
+    half_rows = rows // 2
+    count, inner = up_all.shape[0], up_all.shape[2]
+    span, tile, piece = width // n_dp, 256, 64
+    bf16, f32 = jnp.bfloat16, jnp.float32
+
+    def body(
+        block_ref,
+        mixed_ref,
+        up_ref,
+        all_ref,
+        near_ref,
+        far_ref,
+        far_got,
+        mixed_s,
+        up_s,
+        grad_s,
+        core_s,
+        send,
+        receive,
+        core_send,
+        core_receive,
+        local,
+        load,
+        save,
+        far_send,
+        far_receive,
+    ):
+        ring = Ring(n)
+        dp, core, chip, core_chip = partners()
+        loads = [pltpu.make_async_copy(mixed_ref, mixed_s, load.at[count])]
+        for x in range(count):
+            loads.append(pltpu.make_async_copy(up_ref.at[x], up_s.at[x], load.at[x]))
+        own = pltpu.make_async_copy(
+            block_ref, all_ref.at[pl.ds(pl.multiple_of(ring.me * rows, 16), rows)], local
+        )
+        own.start()
+        for copy in loads:
+            copy.start()
+        ring.barrier(ring.neighbours() + [{"dp": core}, {"dp": chip}])
+        steps = gather_steps(
+            ring,
+            lambda half: block_ref.at[pl.ds(half * half_rows, half_rows)],
+            lambda device, half: all_ref.at[
+                pl.ds(pl.multiple_of(device * rows + half * half_rows, 16), half_rows)
+            ],
+            send,
+            receive,
+        )
+        advance(steps, 2)
+        loads[0].wait()
+        saves, passed = [], []
+        for x in range(count):
+            loads[1 + x].wait()
+            for at, group in enumerate((core_chip, core, chip, dp)):
+
+                def product(j, carry, x=x, at=at, group=group):
+                    columns = pl.ds(pl.multiple_of(group * span + j * tile, tile), tile)
+                    grad_s[x, at, pl.ds(pl.multiple_of(j * tile, tile), tile)] = lax.dot_general(
+                        mixed_s[:, columns],
+                        up_s[x],
+                        (((0,), (0,)), ((), ())),
+                        preferred_element_type=f32,
+                    ).astype(bf16)
+                    return carry
+
+                lax.fori_loop(0, span // tile, product, 0)
+                which = 1 - at % 2
+                if at < 2:
+                    passed.append(
+                        remote(
+                            grad_s.at[x, at],
+                            core_s.at[x, which],
+                            core_send.at[x, which],
+                            core_receive.at[x, which],
+                            {"dp": core},
+                        )
+                    )
+                    passed[-1].start()
+                else:
+                    passed[2 * x + at - 2].wait_recv()
+
+                    def add(j, carry, x=x, at=at, which=which):
+                        part = pl.ds(pl.multiple_of(j * piece, piece), piece)
+                        core_s[x, which, part] = (
+                            core_s[x, which, part].astype(f32) + grad_s[x, at, part].astype(f32)
+                        ).astype(bf16)
+                        return carry
+
+                    lax.fori_loop(0, span // piece, add, 0)
+                    if x == 0 and which:
+                        across = remote(
+                            core_s.at[0, 1, pl.ds(0, PASS_A)], far_got, far_send, far_receive, {"dp": chip}
+                        )
+                        across.start()
+                    saves.append(
+                        pltpu.make_async_copy(
+                            core_s.at[x, which],
+                            (far_ref if which else near_ref).at[x],
+                            save.at[x, which],
+                        )
+                    )
+                    saves[-1].start()
+                advance(steps, 2)
+        advance(steps, 64)
+        for copy in passed:
+            copy.wait_send()
+        across.wait()
+        for copy in saves:
+            copy.wait()
+        own.wait()
+
+    sums = jax.ShapeDtypeStruct((count, span, inner), bf16)
+    return pl.pallas_call(
+        body,
+        out_shape=(
+            jax.ShapeDtypeStruct((rows * n, width), block.dtype),
+            sums,
+            sums,
+            jax.ShapeDtypeStruct((PASS_A, inner), bf16),
+        ),
+        in_specs=[ANY] * 3,
+        out_specs=(ANY,) * 4,
+        scratch_shapes=[
+            pltpu.VMEM(mixed.shape, bf16),
+            pltpu.VMEM(up_all.shape, bf16),
+            pltpu.VMEM((count, n_dp, span, inner), bf16),
+            pltpu.VMEM((count, 2, span, inner), bf16),
+            sems(2, 2, n // 2),
+            sems(2, 2, n // 2),
+            sems(count, 2),
+            sems(count, 2),
+            pltpu.SemaphoreType.DMA,
+            sems(count + 1),
+            sems(count, 2),
+            pltpu.SemaphoreType.DMA,
+            pltpu.SemaphoreType.DMA,
+        ],
+        name="gather_with_gradients",
+        cost_estimate=pl.CostEstimate(
+            flops=2 * count * width * inner * mixed.shape[0],
+            bytes_accessed=160_000_000,
+            transcendentals=0,
+        ),
+        compiler_params=pltpu.CompilerParams(
+            collective_id=identity, has_side_effects=True, vmem_limit_bytes=BIG_VMEM
+        ),
+    )(block, mixed, up_all)
+
+
 def attention_back(
     back_all,
     out_all,
@@ -1908,6 +2109,7 @@
     cosine,
     sine,
     partial,
+    far,
     n,
     n_dp,
     identity,
@@ -1936,11 +2138,14 @@
         cos_ref,
         sin_ref,
         part_ref,
+        far_ref,
         raw_back,
         row_part,
         pair_sum,
         part_sum,
         out_sum,
+        far_got,
+        next_got,
         out_s,
         in_s,
         probs_s,
@@ -1962,6 +2167,8 @@
         out_chip,
         pass_send,
         pass_receive,
+        far_send,
+        far_receive,
     ):
         ring = Ring(n)
         dp, core, chip, core_chip = partners()
@@ -1978,6 +2185,21 @@
         ring.barrier(
             [{"ctx": (ring.me + k) % n} for k in range(1, n)] + [{"dp": core}, {"dp": chip}]
         )
+
+        beyond = [
+            remote(
+                far_ref.at[0, pl.ds(PASS_A, far_got.shape[0])],
+                far_got,
+                far_send.at[0],
+                far_receive.at[0],
+                {"dp": chip},
+            ),
+            remote(
+                far_ref.at[1, pl.ds(0, PASS_B)], next_got, far_send.at[1], far_receive.at[1], {"dp": chip}
+            ),
+        ]
+        for copy in beyond:
+            copy.start()
 
         def store(half, total):
             part_sum[pl.ds(half * half_rows, half_rows)] = total
@@ -2114,6 +2336,8 @@
             out_core[0].astype(f32) + out_p[dp].astype(f32) + out_chip[...].astype(f32)
         ).astype(bf16)
         advance(steps, 64)
+        for copy in beyond:
+            copy.wait()
         for copy in passed:
             copy.wait_send()
 
@@ -2125,9 +2349,11 @@
             jax.ShapeDtypeStruct((8, pair), f32),
             jax.ShapeDtypeStruct((tok_rows, width), f32),
             jax.ShapeDtypeStruct((weight_rows, width), bf16),
+            jax.ShapeDtypeStruct((far.shape[1] - PASS_A, far.shape[2]), bf16),
+            jax.ShapeDtypeStruct((PASS_B, far.shape[2]), bf16),
         ),
-        in_specs=[VMEM] + [ANY] * 3 + [VMEM] * 7 + [ANY],
-        out_specs=(VMEM,) * 5,
+        in_specs=[VMEM] + [ANY] * 3 + [VMEM] * 7 + [ANY] * 2,
+        out_specs=(VMEM,) * 5 + (ANY,) * 2,
         scratch_shapes=[
             pltpu.VMEM((cols, width), bf16),
             pltpu.VMEM((width, pair + cols), bf16),
@@ -2150,6 +2376,8 @@
             pltpu.VMEM((weight_rows, width), bf16),
             sems(3),
             sems(3),
+            sems(2),
+            sems(2),
         ],
         name="attention_back",
         cost_estimate=pl.CostEstimate(
@@ -2171,6 +2399,7 @@
         cosine,
         sine,
         partial,
+        far,
     )
 
 
@@ -2274,23 +2503,9 @@
     second_back = jnp.einsum(
         "tf,td->fd", gated_all, upstream_all.reshape(rows, width), preferred_element_type=f32
     ).astype(bf16)
-    first_backs, last = [], second_back
-    for x in range(local_experts):
-        mixed_slots, last = lax.optimization_barrier((mixed_slots, last))
-        if x == 0:
-            second_back = last
-        else:
-            first_backs.append(last)
-        last = jnp.einsum(
-            "td,tf->df", mixed_slots, up_all[x], preferred_element_type=f32
-        ).astype(bf16)
-    up_all, last = lax.optimization_barrier((up_all, last))
-    first_backs.append(last)
+    second_back, up_all = lax.optimization_barrier((second_back, up_all))
     expert_out_gradient = lax.psum_scatter(
         second_back.reshape(local_experts, FF, width), "dp", scatter_dimension=1, tiled=True
-    ).astype(f32)
-    expert_in_gradient = jnp.stack(
-        [lax.psum_scatter(one, "dp", scatter_dimension=0, tiled=True) for one in first_backs]
     ).astype(f32)
     mixed_back, mixture, gate_back = experts_out(up_all, gated_all, first, second, gate_back, n, 9)
     gate_back = gate_back[:, :local_experts]
@@ -2321,9 +2536,11 @@
     residual_back = cotangent[0].astype(f32) + normalize_back(
         mixed_back * gains[:, 3], own_mixed_normed, own_mixed_inverse
     )
-    back_all = ring_gather(residual_back.astype(bf16), n, 5, "gather_back")
-
-    raw_back, row_part, pair_sum, mixture, out_part = attention_back(
+    back_all, near, far, got_a = gather_with_gradients(
+        residual_back.astype(bf16), mixed_slots, up_all, n, n_dp, 5
+    )
+
+    raw_back, row_part, pair_sum, mixture, out_part, got_b, got_c = attention_back(
         back_all,
         out_all,
         in_all,
@@ -2336,6 +2553,7 @@
         cosine,
         sine,
         mixture,
+        far,
         n,
         n_dp,
         11,
@@ -2354,7 +2572,7 @@
         ],
         axis=0,
     )
-    tokens_back, project_in_gradient, small_gradient = scatter_end(
+    tokens_back, project_in_gradient, small_gradient, got_d = scatter_end(
         row_part,
         attend_in,
         raw_back,
@@ -2363,9 +2581,13 @@
         attend_gain,
         small_part,
         pair_sum,
+        far,
         n,
         n_dp,
         6,
+    )
+    expert_in_gradient = near.astype(f32) + (
+        jnp.concatenate([got_a, got_b, got_c, got_d], axis=0).reshape(near.shape).astype(f32)
     )
     per_tile = LANES // weight_rows
     small_gradient = lax.dynamic_slice_in_dim(
@@ -2383,9 +2605,14 @@
     )
 
 
+def layer(*arrays):
+    n, tok_rows, experts = lax.axis_size("ctx"), arrays[0].shape[1], arrays[7].shape[0]
+    fits = HEADS % n == 0 and n % 4 == 0 and lax.axis_size("dp") == 4
+    fits = fits and tok_rows == LANES and experts == 2 and experts * n + 4 <= LANES
+    return (heads_local if fits else gathered_local)(*arrays)
+
+
 def solution(mesh):
-    n = mesh.shape["ctx"]
-    split_heads = HEADS % n == 0 and n % 4 == 0 and mesh.shape["dp"] == 4
     placed = (
         P("dp", "ctx", None),
         P("dp", None),
@@ -2399,7 +2626,7 @@
         P("dp", "ctx", None),
     )
     return jax.shard_map(
-        heads_local if split_heads else gathered_local,
+        layer,
         mesh=mesh,
         in_specs=placed,
         out_specs=(

time: 633 us -> 584 us (0.923)
  matrix products: 44 us -> 17.4 us
  waiting for transfers between devices: 18.9 us -> 9.64 us
    dot_general x2 -> x0, matrix products: 26.3 us -> none  [heads_local(): jnp.einsum('td,tf->df', mixed_slots, up_all[x], preferred_element_type=f32)]
    pallas_call x1, Pallas kernels: 91.3 us -> 68.2 us  [scatter_end(): kernel_call(body, (jax.ShapeDtypeStruct((rows, width), bf16), jax.ShapeDt...]
    pallas_call x1, Pallas kernels: 39.9 us -> 52.5 us  [gather_with_gradients(): pl.pallas_call(body, out_shape=(jax.ShapeDtypeStruct((rows * n, width), b...]
    ppermute x1, waiting for transfers between devices: 16.9 us -> 8.21 us  [heads_local(): lax.ppermute(out_part, ('dp', 'ctx'), pairs).astype(f32)]
  transfers between devices with their start and end apart: 6 -> 4, of which waited for: 1 -> 1; matrix products, arithmetic and copies ran while one was open for 7% -> 5% of each run, Pallas kernels for 70% -> 74%
where the time goes in v5:
time: 584 us; the launch traced here: 580 us
  Pallas kernels  497 us (85%)
  local copies, waits for them, and re-layouts  18.9 us (3%)
  other arithmetic  18.5 us (3%)
  matrix products  17.4 us (3%)
  between operations  14.7 us (3%)
  waiting for transfers between devices  9.64 us (2%)
    pallas_call x1, Pallas kernels, attention_in(): pl.pallas_call(body, out_shape=(jax.ShapeDtypeStruct((rows, width), bf16)...  117 us
    pallas_call x1, Pallas kernels, gather_inputs(): kernel_call(body, (jax.ShapeDtypeStruct((tok_rows * n, width), tokens.dty...  77.3 us
    pallas_call x1, Pallas kernels, scatter_end(): kernel_call(body, (jax.ShapeDtypeStruct((rows, width), bf16), jax.ShapeDt...  68.2 us
    pallas_call x1, Pallas kernels, experts_in(): pl.pallas_call(body, out_shape=(jax.ShapeDtypeStruct((n, tok_rows, width)...  66.7 us
    pallas_call x1, Pallas kernels, attention_back(): pl.pallas_call(body, out_shape=(jax.ShapeDtypeStruct((rows, 3 * cols), bf...  63.2 us
    pallas_call x1, Pallas kernels, gather_with_gradients(): pl.pallas_call(body, out_shape=(jax.ShapeDtypeStruct((rows * n, width), b...  52.5 us
    pallas_call x1, Pallas kernels, experts_out(): pl.pallas_call(body, out_shape=(jax.ShapeDtypeStruct((tok_rows, width), f...  51.9 us
    dot_general x1, matrix products, heads_local(): jnp.einsum('tf,td->fd', gated_all, upstream_all.reshape(rows, width), pre...  14.2 us
  transfers between devices with their start and end apart: 4, of which 1 were waited for; matrix products, arithmetic and copies ran while one was open for 5% of the time, Pallas kernels for 74%

profile of v5, /device:TPU:1, one launch (start us, length us, event | category | flops | bytes accessed | tf_op | source)
XLA Modules:
  0.0 579.7 jit_solution(17288860559470282937)
XLA Ops:
  7.3 0.7 all-gather.5.cloned.1.call-update
  8.0 0.7 all-gather.3.cloned.1.call-update
  11.3 0.9 reshape.170
  12.6 77.3 %gather_inputs.1 = (bf16[1024,2048]{1,0:T(8,128)(2,1)}, bf16[8,128,128]{2,1,0:T(8,128)(2,1)S(1)}, bf16[4,8,64,896]{3,2,1,0:T(8,128)(2,1)S(1)}) custom-call(bf16[128,2048]{1,0:T(8,128)(2,1)S(1)} %bitcast.84, bf16[128,128]{1,0:T(8,128)(2,1)S(1)} %convert_element_type.45.named_ref, bf16[8,64,896]{2,1,0:T(8,128)(2,1)S(1)} %pad_maximum_fusion.1.in_ref), custom_call_target="tpu_custom_call" | custom-call | bytes 200000000 | tf_op jit(solution)/shard_map/gather_inputs/pallas_call | solution.py:808
  89.9 1.8 copy-done
  92.0 1.1 slice_convert_fusion
  93.5 0.8 pad.8.bound_ref
  94.4 0.9 pad.9.router_ref
  95.3 1.9 fusion.5
  97.2 1.3 pad_maximum_fusion.2
  98.5 0.9 slice_reduce_fusion
  101.3 117.1 %attention_in.1 = (bf16[1024,2048]{1,0:T(8,128)(2,1)}, bf16[2048,2048]{1,0:T(8,128)(2,1)}, bf16[2,1024,1024]{2,1,0:T(8,128)(2,1)}, bf16[1024,2048]{1,0:T(8,128)(...) custom-call(bf16[1024,2048]{1,0:T(8,128)(2,1)} %get-tuple-element.46.to, ...), custom_call_target="tpu_custom_call" | custom-call | flops 3221225472 | bytes 200000000 | tf_op jit(solution)/shard_map/attention_in/pallas_call | solution.py:1906
  219.0 66.7 %experts_in.1 = (bf16[8,128,2048]{2,1,0:T(8,128)(2,1)}, bf16[8,128,2048]{2,1,0:T(8,128)(2,1)}, bf16[1024,2048]{1,0:T(8,128)(2,1)}, bf16[2,1024,2048]{2,1,0:T(8,1...) custom-call(bf16[1024,2048]{1,0:T(8,128)(2,1)} %get-tuple-element.48.attend_ref, ...), custom_call_target="tpu_custom_call" | custom-call | flops 34359738368 | bytes 60000000 | tf_op jit(solution)/shard_map/experts_in/pallas_call | solution.py:1384
  285.7 14.2 %convolution_convert_fusion = bf16[2048,2048]{1,0:T(8,128)(2,1)} fusion(bf16[1024,2048]{1,0:T(8,128)(2,1)} %get-tuple-element.52.gated_ref, bf16[1024,2048]{1,0:T(8,128)(2,1)} %bitcast.113), kind=kOutput, calls=%fused_computation.1 | convolution fusion | flops 8594128896 | bytes 16777216 | tf_op jit(solution)/shard_map/tf,td->fd/dot_general | solution.py:2503
  301.7 51.9 %experts_out.1 = (f32[128,2048]{1,0:T(8,128)}, bf16[1024,2048]{1,0:T(8,128)(2,1)}, f32[8,8,128]{2,1,0:T(8,128)}) custom-call(bf16[2,1024,2048]{2,1,0:T(8,128)(2,1)} %get-tuple-element.55.up_ref, bf16[1024,2048]{1,0:T(8,128)(2,1)} %get-tuple-element.52.gated_ref, bf16[2,2048,2048]{2,1,0:T(8,128)(2,1)} %all-gather.3.cloned.1.call-done.first_ref, ...), custom_call_target="tpu_custom_call" | custom-call | flops 25769803776 | bytes 60000000 | tf_op jit(solution)/shard_map/experts_out/pallas_call | solution.py:1632
  353.7 0.8 slice_bitcast_fusion.7
  355.7 2.0 multiply_reduce_fusion
  357.7 1.3 fusion.1
  359.0 1.2 fusion.10
  360.1 52.5 %gather_with_gradients.1 = (bf16[1024,2048]{1,0:T(8,128)(2,1)}, bf16[2,512,2048]{2,1,0:T(8,128)(2,1)}, bf16[2,512,2048]{2,1,0:T(8,128)(2,1)}, bf16[256,2048]{1,0:T(8,128)(2,1)}) custom-call(bf16[128,2048]{1,0:T(8,128)(2,1)} %get-tuple-element.88.block_ref, bf16[1024,2048]{1,0:T(8,128)(2,1)} %bitcast.94, bf16[2,1024,2048]{2,1,0:T(8,128)(2,1)} %get-tuple-element.55.up_ref), custom_call_target="tpu_custom_call" | custom-call | flops 17179869184 | bytes 160000000 | tf_op jit(solution)/shard_map/gather_with_gradients/pallas_call | solution.py:2062
  412.7 63.2 %attention_back.1 = (bf16[1024,768]{1,0:T(8,128)(2,1)}, bf16[1024,2048]{1,0:T(8,128)(2,1)}, f32[8,512]{1,0:T(8,128)}, f32[128,2048]{1,0:T(8,128)}, bf16[64,2048]...) custom-call(bf16[1024,2048]{1,0:T(8,128)(2,1)} %get-tuple-element.61.back_ref, ...), custom_call_target="tpu_custom_call" | custom-call | flops 4294967296 | bytes 160000000 | tf_op jit(solution)/shard_map/attention_back/pallas_call | solution.py:2344
  476.0 0.7 copy-done.3
  476.8 68.2 %scatter_end.1 = (bf16[128,2048]{1,0:T(8,128)(2,1)S(1)}, f32[64,6144]{1,0:T(8,128)S(1)}, f32[24,128]{1,0:T(8,128)S(1)}, bf16[256,2048]{1,0:T(8,128)(2,1)S(1)}) custom-call(bf16[1024,2048]{1,0:T(8,128)(2,1)} %get-tuple-element.70.row_ref, bf16[1024,2048]{1,0:T(8,128)(2,1)} %get-tuple-element.71.attend_ref, bf16[1024,768]{1,0:T(8,128)(2,1)} %get-tuple-element.72.raw_ref, ...), custom_call_target="tpu_custom_call" | custom-call | bytes 200000000 | tf_op jit(solution)/shard_map/scatter_end/pallas_call | solution.py:1076
  546.2 3.3 collective-permute-start
  550.0 1.8 copy-done.7
  551.7 5.2 convert_add_fusion
  556.9 0.9 fusion
  557.8 8.2 %collective-permute-done = bf16[64,2048]{1,0:T(8,128)(2,1)S(1)} collective-permute-done((bf16[64,2048]{1,0:T(8,128)(2,1)S(1)}, bf16[64,2048]{1,0:T(8,128)(2,1)S(1)}, u32[]{:S(2)}, u32[]{:S(2)}) %collective-permute-start) | collective-permute-done | bytes 262176 | tf_op jit(solution)/shard_map/ppermute | solution.py:2563
  566.0 0.8 convert_element_type.53
  566.9 4.1 convert_element_type.57
  571.0 0.8 copy.87
  571.8 1.1 copy.88
  (142 shorter events, 10.5 us)
Async XLA Ops:
  7.2 1.8 copy-start.15
  7.2 2.9 copy-start.16
  7.2 3.3 copy-start.17
  7.2 3.4 copy-start.18
  7.2 3.5 copy-start.12
  7.2 211.1 %all-gather.5.cloned.1.call-start = ((), (), s32[]{:S(2)}) async-start(), calls=%async_computation.2 | async-start | bytes 10485760 | tf_op jit(solution)/shard_map/all_gather | solution.py:2454
  8.0 210.4 %all-gather.3.cloned.1.call-start = ((), (), s32[]{:S(2)}) async-start(), calls=%async_computation.1 | async-start | bytes 20971520 | tf_op jit(solution)/shard_map/all_gather | solution.py:2453
  8.7 3.9 copy-start.1
  8.7 558.2 %reduce-scatter.2.cloned.1.call-start = ((), (), s32[]{:S(2)}) async-start(), calls=%async_computation.3 | async-start | bytes 10485760 | tf_op jit(solution)/shard_map/reduce_scatter | solution.py:2507
  89.9 1.8 copy-start
  89.9 8.6 %copy-start.4 = (bf16[8,128,128]{2,1,0:T(8,128)(2,1)}, bf16[8,128,128]{2,1,0:T(8,128)(2,1)S(1)}, u32[]{:S(2)}) copy-start(bf16[8,128,128]{2,1,0:T(8,128)(2,1)S(1)} %get-tuple-element.50) | copy-start | bytes 786436
  301.7 53.6 %copy-start.5 = (f32[128,2048]{1,0:T(8,128)S(1)}, f32[128,2048]{1,0:T(8,128)}, u32[]{:S(2)}) copy-start(f32[128,2048]{1,0:T(8,128)} %get-tuple-element.51) | copy-start | bytes 3145732
  301.7 53.8 %copy-start.14 = (f32[128,128]{1,0:T(8,128)S(1)}, f32[128,128]{1,0:T(8,128)}, u32[]{:S(2)}) copy-start(f32[128,128]{1,0:T(8,128)} %get-tuple-element.58) | copy-start | bytes 196612
  353.6 5.3 copy-start.13
  412.7 63.3 %copy-start.2 = (f32[8,2048]{1,0:T(8,128)S(1)}, f32[8,2048]{1,0:T(8,128)}, u32[]{:S(2)}) copy-start(f32[8,2048]{1,0:T(8,128)} %broadcast_in_dim.198.gain_ref) | copy-start | bytes 196612
  476.0 0.7 copy-start.3
  476.8 69.4 %copy-start.19 = (bf16[64,2048]{1,0:T(8,128)(2,1)S(1)}, bf16[64,2048]{1,0:T(8,128)(2,1)}, u32[]{:S(2)}) copy-start(bf16[64,2048]{1,0:T(8,128)(2,1)} %get-tuple-element.77) | copy-start | bytes 786436
  476.8 72.8 %copy-start.9 = (bf16[256,2048]{1,0:T(8,128)(2,1)S(1)}, bf16[256,2048]{1,0:T(8,128)(2,1)}, u32[]{:S(2)}) copy-start(bf16[256,2048]{1,0:T(8,128)(2,1)} %get-tuple-element.79) | copy-start | bytes 3145732
  476.8 72.8 %copy-start.10 = (bf16[256,2048]{1,0:T(8,128)(2,1)S(1)}, bf16[256,2048]{1,0:T(8,128)(2,1)}, u32[]{:S(2)}) copy-start(bf16[256,2048]{1,0:T(8,128)(2,1)} %get-tuple-element.80) | copy-start | bytes 3145732
  476.8 72.8 %copy-start.11 = (bf16[256,2048]{1,0:T(8,128)(2,1)S(1)}, bf16[256,2048]{1,0:T(8,128)(2,1)}, u32[]{:S(2)}) copy-start(bf16[256,2048]{1,0:T(8,128)(2,1)} %get-tuple-element.81) | copy-start | bytes 3145732
  546.2 19.8 %collective-permute-start = (bf16[64,2048]{1,0:T(8,128)(2,1)S(1)}, bf16[64,2048]{1,0:T(8,128)(2,1)S(1)}, u32[]{:S(2)}, u32[]{:S(2)}) collective-permute-start(bf16[64,2048]{1,0:T(8,128)(2,1)S(1)} %copy-done.19), channel_id=1, source_target_pairs={{0,0},{1,4},{2,8},{3,12},{4,16},{5,20},{6,24},{7,28},{8,1},{9,5},{... | collective-permute-start | bytes 786440 | tf_op jit(solution)/shard_map/ppermute | solution.py:2563
  549.6 2.2 copy-start.7
  551.7 5.2 copy-start.6
  551.7 5.2 copy-start.8
Sparse Core Ops, SparseCore 0:
  9.6 80.4 all-gather.4
  91.7 111.5 all-gather.2
  300.1 76.5 reduce-scatter.1

commit v6 on v5

--- a/solution.py
+++ b/solution.py
@@ -695,16 +695,18 @@
     return dp, core, chip, (core + 2) % 4
 
 
-def gather_inputs(tokens, named, in_blocks, n, n_dp, identity):
+def gather_inputs(tokens, named, in_blocks, out_rows, n, n_dp, identity):
     tok_rows, width = tokens.shape
 
     def body(
         token_ref,
         named_ref,
         in_ref,
+        out_ref,
         token_all,
         named_all,
         in_all,
+        out_chip,
         token_send,
         token_receive,
         named_send,
@@ -714,6 +716,8 @@
         pass_send,
         pass_receive,
         local,
+        out_send,
+        out_receive,
     ):
         ring = Ring(n)
         me = ring.me
@@ -739,7 +743,8 @@
         others = [(me + k) % n for k in range(1, n)]
         ring.barrier([{"ctx": other} for other in others] + [{"dp": core}, {"dp": chip}])
 
-        direct = []
+        direct = [remote(out_ref, out_chip, out_send, out_receive, {"dp": chip})]
+        direct[0].start()
         for k, other in enumerate(others):
             direct.append(
                 remote(in_ref.at[other], in_all.at[dp, me], in_send.at[k], in_receive.at[k], {"ctx": other})
@@ -747,41 +752,43 @@
             direct.append(
                 remote(named_ref, named_all.at[me], named_send.at[k], named_receive.at[k], {"ctx": other})
             )
-        for copy in direct:
+        for copy in direct[1:]:
             copy.start()
 
         def in_steps():
-            for _ in range(2):
-                yield
+            passed = []
+
+            def forward(at, k, source, spot, to):
+                passed.append(
+                    remote(source, spot, pass_send.at[at, k], pass_receive.at[at, k], {"dp": to})
+                )
+                passed[-1].start()
+
+            def landed(at, k, group, source):
+                spot = in_all.at[group, (me - k + n) % n]
+                remote(
+                    spot, spot, pass_send.at[at, k], pass_receive.at[at, k], {"dp": source}
+                ).wait_recv()
+                return spot
+
+            for at, to in ((0, chip), (1, core)):
+                forward(at, 0, in_ref.at[me], in_all.at[dp, me], to)
+            yield
             for k in range(1, n):
                 spot = in_all.at[dp, (me - k + n) % n]
                 remote(
                     spot, spot, in_send.at[k - 1], in_receive.at[k - 1], {"ctx": others[k - 1]}
                 ).wait_recv()
-            locals_[0].wait()
-            passed = []
-            for at, to in ((0, chip), (1, core)):
-                passed.append(
-                    remote(
-                        in_all.at[dp], in_all.at[dp], pass_send.at[at], pass_receive.at[at], {"dp": to}
-                    )
-                )
-                passed[-1].start()
-            for _ in range(8):
+                for at, to in ((0, chip), (1, core)):
+                    forward(at, k, spot, spot, to)
                 yield
-            spot = in_all.at[chip]
-            remote(spot, spot, pass_send.at[0], pass_receive.at[0], {"dp": chip}).wait_recv()
-            passed.append(
-                remote(spot, spot, pass_send.at[2], pass_receive.at[2], {"dp": core})
-            )
-            passed[-1].start()
-            for _ in range(4):
+            for k in range(n):
+                spot = landed(0, k, chip, chip)
+                forward(2, k, spot, spot, core)
                 yield
-            for at, source in ((1, core), (2, core_chip)):
-                spot = in_all.at[source]
-                remote(
-                    spot, spot, pass_send.at[at], pass_receive.at[at], {"dp": core}
-                ).wait_recv()
+            for at, group in ((1, core), (2, core_chip)):
+                for k in range(n):
+                    landed(at, k, group, core)
             for copy in passed:
                 copy.wait_send()
 
@@ -800,9 +807,10 @@
             remote(
                 spot, spot, named_send.at[k - 1], named_receive.at[k - 1], {"ctx": others[k - 1]}
             ).wait_recv()
+        direct[0].wait_recv()
         for copy in direct:
             copy.wait_send()
-        for copy in locals_[1:]:
+        for copy in locals_:
             copy.wait()
 
     return kernel_call(
@@ -811,17 +819,18 @@
             jax.ShapeDtypeStruct((tok_rows * n, width), tokens.dtype),
             jax.ShapeDtypeStruct((n,) + named.shape, named.dtype),
             jax.ShapeDtypeStruct((n_dp,) + in_blocks.shape, in_blocks.dtype),
+            jax.ShapeDtypeStruct(out_rows.shape, out_rows.dtype),
         ),
-        [ANY] * 3,
-        (ANY,) * 3,
+        [ANY] * 4,
+        (ANY,) * 4,
         [sems(2, 2, n // 2)] * 2
         + [sems(n - 1)] * 4
-        + [sems(3)] * 2
-        + [sems(3)],
+        + [sems(3, n)] * 2
+        + [sems(3), pltpu.SemaphoreType.DMA, pltpu.SemaphoreType.DMA],
         identity,
         "gather_inputs",
         200_000_000,
-    )(tokens, named, in_blocks)
+    )(tokens, named, in_blocks, out_rows)
 
 
 def sum_small_steps(ring, small, near, quarter, got, total, sem):
@@ -1701,7 +1710,7 @@
     return values * cosine + pltpu.roll(values, HEAD_DIM // 2, 1) * sine
 
 
-def out_gather_steps(ring, out_ref, out_all, sem):
+def out_gather_steps(ring, out_ref, chip_ref, out_all, sem):
     own_send, own_receive, ring_send, ring_receive, core_send, core_receive, local = sem
     dp, core, chip, core_chip = partners()
     weight_rows, n, me = out_ref.shape[0], ring.n, ring.me
@@ -1709,23 +1718,21 @@
     def place(group, device):
         return out_all.at[pl.ds(pl.multiple_of((group * n + device) * weight_rows, 16), weight_rows)]
 
-    own = pltpu.make_async_copy(out_ref, place(dp, me), local)
-    own.start()
+    own = [
+        pltpu.make_async_copy(out_ref, place(dp, me), local.at[0]),
+        pltpu.make_async_copy(chip_ref, place(chip, me), local.at[1]),
+    ]
     copies = [
-        remote(out_ref, place(dp, me), own_send.at[0], own_receive.at[0], {"dp": chip}),
-        remote(out_ref, place(dp, me), own_send.at[1], own_receive.at[1], {"dp": core}),
+        remote(out_ref, place(dp, me), own_send.at[0], own_receive.at[0], {"dp": core}),
+        remote(chip_ref, place(chip, me), own_send.at[1], own_receive.at[1], {"dp": core}),
     ]
-    for copy in copies:
+    for copy in own:
         copy.start()
 
-    def ready(half):
-        if half == 1:
-            spot = place(chip, me)
-            remote(spot, spot, own_send.at[0], own_receive.at[0], {"dp": chip}).wait_recv()
-            copies.append(remote(spot, spot, own_send.at[2], own_receive.at[2], {"dp": core}))
-            copies[-1].start()
-
     def arrived(way, half, hop, origin):
+        if len(copies) == 2:
+            for copy in copies:
+                copy.start()
         spot = place(chip if half else dp, origin)
         copies.append(
             remote(
@@ -1736,14 +1743,13 @@
 
     yield from gather_steps(
         ring,
-        lambda half: place(chip, me) if half else out_ref,
+        lambda half: chip_ref if half else out_ref,
         lambda device, half: place(chip if half else dp, device),
         ring_send,
         ring_receive,
         arrived,
-        ready,
-    )
-    for at, group in ((1, core), (2, core_chip)):
+    )
+    for at, group in ((0, core), (1, core_chip)):
         spot = place(group, me)
         remote(spot, spot, own_send.at[at], own_receive.at[at], {"dp": core}).wait_recv()
     for way, sign in ((0, 1), (1, -1)):
@@ -1759,11 +1765,12 @@
                 ).wait_recv()
     for copy in copies:
         copy.wait_send()
-    own.wait()
+    for copy in own:
+        copy.wait()
 
 
 def attention_in(
-    token_all, in_all, out_rows, gain, pair_gains, cosine, sine, bounds, place_row, n, n_dp, identity
+    token_all, in_all, out_rows, out_chip, gain, pair_gains, cosine, sine, bounds, place_row, n, n_dp, identity
 ):
     rows, width = token_all.shape
     pair = pair_gains.shape[1]
@@ -1778,6 +1785,7 @@
         token_ref,
         in_ref,
         out_ref,
+        chip_ref,
         gain_ref,
         pair_ref,
         cos_ref,
@@ -1802,10 +1810,8 @@
         sum_send, sum_receive, ring_send, ring_receive, save = sem
         ring = Ring(n)
         dp, core, chip, core_chip = partners()
-        ring.barrier(
-            [{"ctx": (ring.me + k) % n} for k in range(1, n)] + [{"dp": core}, {"dp": chip}]
-        )
-        steps = out_gather_steps(ring, out_ref, out_all, out_sem)
+        ring.barrier([{"ctx": (ring.me + k) % n} for k in range(1, n)] + [{"dp": core}])
+        steps = out_gather_steps(ring, out_ref, chip_ref, out_all, out_sem)
         advance(steps, 1)
         lanes = lax.broadcasted_iota(jnp.int32, (chunk, LANES), 1)
 
@@ -1915,20 +1921,20 @@
             jax.ShapeDtypeStruct((rows, pair), f32),
             jax.ShapeDtypeStruct((rows, LANES), f32),
         ),
-        in_specs=[VMEM, VMEM, ANY] + [VMEM] * 6,
+        in_specs=[VMEM, VMEM, ANY, ANY] + [VMEM] * 6,
         out_specs=(ANY,) * 4 + (VMEM,) * 4,
         scratch_shapes=[
             pltpu.VMEM((heads, rows, rows), bf16),
             pltpu.VMEM((rows, width), bf16),
             pltpu.VMEM((8, rows), f32),
             pltpu.VMEM((n - 1, 8, rows), f32),
-            sems(3),
-            sems(3),
+            sems(2),
+            sems(2),
             sems(2, 2, n // 2),
             sems(2, 2, n // 2),
             sems(2, 2, n // 2),
             sems(2, 2, n // 2),
-            pltpu.SemaphoreType.DMA,
+            sems(2),
             sems(n - 1),
             sems(n - 1),
             sems(2, 2, n // 2),
@@ -1942,7 +1948,7 @@
         compiler_params=pltpu.CompilerParams(
             collective_id=identity, has_side_effects=True, vmem_limit_bytes=BIG_VMEM
         ),
-    )(token_all, in_all, out_rows, gain, pair_gains, cosine, sine, bounds, place_row)
+    )(token_all, in_all, out_rows, out_chip, gain, pair_gains, cosine, sine, bounds, place_row)
 
 
 def gather_with_gradients(block, mixed, up_all, n, n_dp, identity):
@@ -2433,7 +2439,7 @@
 
     named = jnp.any(routes[0][..., None] == jnp.arange(LANES, dtype=jnp.int32), axis=1).astype(bf16)
     small = jnp.concatenate(
-        [norm_gains, router_weight, jnp.zeros((weight_rows, LANES - 4 - expert_count), bf16)], axis=1
+        [router_weight, norm_gains, jnp.zeros((weight_rows, LANES - 4 - expert_count), bf16)], axis=1
     )
     in_blocks = project_in.reshape(weight_rows, 3, n, cols).transpose(2, 0, 1, 3)
     in_blocks = jnp.concatenate(
@@ -2443,13 +2449,14 @@
         ],
         axis=2,
     )
-    token_all, named_all, in_all = gather_inputs(tokens[0], named, in_blocks, n, n_dp, 1)
+    token_all, named_all, in_all, out_chip = gather_inputs(
+        tokens[0], named, in_blocks, project_out, n, n_dp, 1
+    )
     named_all = named_all.reshape(rows, LANES)
     in_all = in_all.reshape(width, 3 * cols + LANES)
     small_all = in_all[:, 3 * cols :]
-    gains = small_all[:, :4].astype(f32)
-    router_all = small_all[:, 4 : 4 + expert_count]
-    router_wide = jnp.pad(router_all, ((0, 0), (0, LANES - expert_count)))
+    gains = small_all[:, expert_count : expert_count + 4].astype(f32)
+    router_all = small_all[:, :expert_count]
     first = lax.all_gather(expert_in, "dp", axis=1, tiled=True)
     second = lax.all_gather(expert_out, "dp", axis=1, tiled=True).reshape(local_experts * FF, width)
 
@@ -2466,15 +2473,16 @@
     cosine, sine = rotary_tables(relative, HEAD_DIM)
     cosine = jnp.concatenate([cosine[:, 0], cosine[:, 0]], axis=-1)
     sine = jnp.concatenate([-sine[:, 0], sine[:, 0]], axis=-1)
-    bounds = jnp.pad(jnp.stack([starts, places], axis=1), ((0, 0), (0, LANES - 2)))
-    place_row = jnp.broadcast_to(places[None], (8, rows))
-    pair_gains = jnp.broadcast_to(own(gains, cols)[:, 1:3].T.reshape(1, 2 * cols), (8, 2 * cols))
-
-    attend_gain = jnp.broadcast_to(gains[:, 0][None], (8, width))
+    bounds = jnp.stack([starts, places], axis=1)
+    place_row = places[None]
+    pair_gains = own(gains, cols)[:, 1:3].T.reshape(1, 2 * cols)
+
+    attend_gain = gains[:, 0][None]
     attend_all, out_all, probs, attend_in, attend_low, qkv, raw, inverse = attention_in(
         token_all,
         in_all,
         project_out,
+        out_chip,
         attend_gain,
         pair_gains,
         cosine,
@@ -2493,8 +2501,8 @@
         out_all,
         first,
         second,
-        jnp.broadcast_to(gains[:, 3][None], (8, width)),
-        router_wide,
+        gains[:, 3][None],
+        small_all,
         named_all,
         n,
         8,

time: 584 us -> 572 us (0.979)
  Pallas kernels: 497 us -> 481 us
    pallas_call x1, Pallas kernels: 117 us -> 106 us  [attention_in(): pl.pallas_call(body, out_shape=(jax.ShapeDtypeStruct((rows, width), bf16)...]
  transfers between devices with their start and end apart: 4 -> 4, of which waited for: 1 -> 1; matrix products, arithmetic and copies ran while one was open for 5% -> 5% of each run, Pallas kernels for 74% -> 73%
where the time goes in v6:
time: 572 us; the launch traced here: 566 us
  Pallas kernels  481 us (84%)
  local copies, waits for them, and re-layouts  19.3 us (3%)
  other arithmetic  18.7 us (3%)
  matrix products  17.4 us (3%)
  between operations  14.7 us (3%)
  waiting for transfers between devices  9.55 us (2%)
    pallas_call x1, Pallas kernels, attention_in(): pl.pallas_call(body, out_shape=(jax.ShapeDtypeStruct((rows, width), bf16)...  106 us
    pallas_call x1, Pallas kernels, gather_inputs(): kernel_call(body, (jax.ShapeDtypeStruct((tok_rows * n, width), tokens.dty...  75.7 us
    pallas_call x1, Pallas kernels, scatter_end(): kernel_call(body, (jax.ShapeDtypeStruct((rows, width), bf16), jax.ShapeDt...  66 us
    pallas_call x1, Pallas kernels, experts_in(): pl.pallas_call(body, out_shape=(jax.ShapeDtypeStruct((n, tok_rows, width)...  65.6 us
    pallas_call x1, Pallas kernels, attention_back(): pl.pallas_call(body, out_shape=(jax.ShapeDtypeStruct((rows, 3 * cols), bf...  63.1 us
    pallas_call x1, Pallas kernels, gather_with_gradients(): pl.pallas_call(body, out_shape=(jax.ShapeDtypeStruct((rows * n, width), b...  52.7 us
    pallas_call x1, Pallas kernels, experts_out(): pl.pallas_call(body, out_shape=(jax.ShapeDtypeStruct((tok_rows, width), f...  51.8 us
    dot_general x1, matrix products, heads_local(): jnp.einsum('tf,td->fd', gated_all, upstream_all.reshape(rows, width), pre...  14.2 us
  transfers between devices with their start and end apart: 4, of which 1 were waited for; matrix products, arithmetic and copies ran while one was open for 5% of the time, Pallas kernels for 73%

profile of v6, /device:TPU:1, one launch (start us, length us, event | category | flops | bytes accessed | tf_op | source)
XLA Modules:
  0.0 566.0 jit_solution(4297332180958739780)
XLA Ops:
  8.0 0.7 all-gather.3.cloned.1.call-update
  11.7 0.9 reshape.167
  13.0 75.7 %gather_inputs.1 = (bf16[1024,2048]{1,0:T(8,128)(2,1)}, bf16[8,128,128]{2,1,0:T(8,128)(2,1)S(1)}, bf16[4,8,64,896]{3,2,1,0:T(8,128)(2,1)S(1)}, bf16[64,2048]{1,0:T(8,128)(2,1)S(1)}) custom-call(bf16[128,2048]{1,0:T(8,128)(2,1)S(1)} %bitcast.87, bf16[128,128]{1,0:T(8,128)(2,1)S(1)} %convert_element_type.46.named_ref, ...), custom_call_target="tpu_custom_call" | custom-call | bytes 200000000 | tf_op jit(solution)/shard_map/gather_inputs/pallas_call | solution.py:816
  89.4 0.7 copy-done.6
  90.1 1.8 copy-done
  92.0 0.8 slice.130.router_ref
  92.8 1.2 slice_convert_fusion
  95.0 1.0 copy.73.bound_ref
  96.1 1.9 fusion.6
  98.0 1.3 pad_maximum_fusion.2
  99.3 1.5 slice_reduce_fusion
  100.8 106.4 %attention_in.1 = (bf16[1024,2048]{1,0:T(8,128)(2,1)}, bf16[2048,2048]{1,0:T(8,128)(2,1)}, bf16[2,1024,1024]{2,1,0:T(8,128)(2,1)}, bf16[1024,2048]{1,0:T(8,128)(...) custom-call(bf16[1024,2048]{1,0:T(8,128)(2,1)} %get-tuple-element.47.to, ...), custom_call_target="tpu_custom_call" | custom-call | flops 3221225472 | bytes 200000000 | tf_op jit(solution)/shard_map/attention_in/pallas_call | solution.py:1912
  207.2 65.6 %experts_in.1 = (bf16[8,128,2048]{2,1,0:T(8,128)(2,1)}, bf16[8,128,2048]{2,1,0:T(8,128)(2,1)}, bf16[1024,2048]{1,0:T(8,128)(2,1)}, bf16[2,1024,2048]{2,1,0:T(8,1...) custom-call(bf16[1024,2048]{1,0:T(8,128)(2,1)} %get-tuple-element.50.attend_ref, ...), custom_call_target="tpu_custom_call" | custom-call | flops 34359738368 | bytes 60000000 | tf_op jit(solution)/shard_map/experts_in/pallas_call | solution.py:1393
  272.8 14.2 %convolution_convert_fusion = bf16[2048,2048]{1,0:T(8,128)(2,1)} fusion(bf16[1024,2048]{1,0:T(8,128)(2,1)} %get-tuple-element.54.gated_ref, bf16[1024,2048]{1,0:T(8,128)(2,1)} %bitcast.120), kind=kOutput, calls=%fused_computation.1 | convolution fusion | flops 8594128896 | bytes 16777216 | tf_op jit(solution)/shard_map/tf,td->fd/dot_general | solution.py:2511
  288.8 51.8 %experts_out.1 = (f32[128,2048]{1,0:T(8,128)}, bf16[1024,2048]{1,0:T(8,128)(2,1)}, f32[8,8,128]{2,1,0:T(8,128)}) custom-call(bf16[2,1024,2048]{2,1,0:T(8,128)(2,1)} %get-tuple-element.57.up_ref, bf16[1024,2048]{1,0:T(8,128)(2,1)} %get-tuple-element.54.gated_ref, bf16[2,2048,2048]{2,1,0:T(8,128)(2,1)} %all-gather.3.cloned.1.call-done.first_ref, ...), custom_call_target="tpu_custom_call" | custom-call | flops 25769803776 | bytes 60000000 | tf_op jit(solution)/shard_map/experts_out/pallas_call | solution.py:1641
  340.6 0.8 slice_bitcast_fusion.7
  342.6 1.9 multiply_reduce_fusion
  344.6 1.3 fusion.2
  345.8 1.2 fusion.10
  347.0 52.7 %gather_with_gradients.1 = (bf16[1024,2048]{1,0:T(8,128)(2,1)}, bf16[2,512,2048]{2,1,0:T(8,128)(2,1)}, bf16[2,512,2048]{2,1,0:T(8,128)(2,1)}, bf16[256,2048]{1,0:T(8,128)(2,1)}) custom-call(bf16[128,2048]{1,0:T(8,128)(2,1)} %get-tuple-element.90.block_ref, bf16[1024,2048]{1,0:T(8,128)(2,1)} %bitcast.100, bf16[2,1024,2048]{2,1,0:T(8,128)(2,1)} %get-tuple-element.57.up_ref), custom_call_target="tpu_custom_call" | custom-call | flops 17179869184 | bytes 160000000 | tf_op jit(solution)/shard_map/gather_with_gradients/pallas_call | solution.py:2068
  399.8 63.1 %attention_back.1 = (bf16[1024,768]{1,0:T(8,128)(2,1)}, bf16[1024,2048]{1,0:T(8,128)(2,1)}, f32[8,512]{1,0:T(8,128)}, f32[128,2048]{1,0:T(8,128)}, bf16[64,2048]...) custom-call(bf16[1024,2048]{1,0:T(8,128)(2,1)} %get-tuple-element.63.back_ref, ...), custom_call_target="tpu_custom_call" | custom-call | flops 4294967296 | bytes 160000000 | tf_op jit(solution)/shard_map/attention_back/pallas_call | solution.py:2350
  462.9 0.7 copy-done.4
  463.7 66.0 %scatter_end.1 = (bf16[128,2048]{1,0:T(8,128)(2,1)S(1)}, f32[64,6144]{1,0:T(8,128)S(1)}, f32[24,128]{1,0:T(8,128)S(1)}, bf16[256,2048]{1,0:T(8,128)(2,1)S(1)}) custom-call(bf16[1024,2048]{1,0:T(8,128)(2,1)} %get-tuple-element.72.row_ref, bf16[1024,2048]{1,0:T(8,128)(2,1)} %get-tuple-element.73.attend_ref, bf16[1024,768]{1,0:T(8,128)(2,1)} %get-tuple-element.74.raw_ref, ...), custom_call_target="tpu_custom_call" | custom-call | bytes 200000000 | tf_op jit(solution)/shard_map/scatter_end/pallas_call | solution.py:1085
  530.9 5.0 collective-permute-start
  536.4 1.8 copy-done.9
  538.1 5.2 convert_add_fusion
  543.3 0.9 fusion
  544.2 8.1 %collective-permute-done = bf16[64,2048]{1,0:T(8,128)(2,1)S(1)} collective-permute-done((bf16[64,2048]{1,0:T(8,128)(2,1)S(1)}, bf16[64,2048]{1,0:T(8,128)(2,1)S(1)}, u32[]{:S(2)}, u32[]{:S(2)}) %collective-permute-start) | collective-permute-done | bytes 262176 | tf_op jit(solution)/shard_map/ppermute | solution.py:2571
  552.3 0.8 convert_element_type.55
  553.2 4.1 convert_element_type.59
  557.3 0.8 copy.88
  558.1 1.1 copy.89
  (140 shorter events, 10.2 us)
Async XLA Ops:
  7.2 1.6 copy-start.18
  7.2 3.4 copy-start.19
  7.2 3.7 copy-start.21
  7.2 3.8 copy-start.20
  7.2 3.9 copy-start.14
  7.2 199.9 %all-gather.5.cloned.1.call-start = ((), (), s32[]{:S(2)}) async-start(), calls=%async_computation.2 | async-start | bytes 10485760 | tf_op jit(solution)/shard_map/all_gather | solution.py:2461
  8.0 199.2 %all-gather.3.cloned.1.call-start = ((), (), s32[]{:S(2)}) async-start(), calls=%async_computation.1 | async-start | bytes 20971520 | tf_op jit(solution)/shard_map/all_gather | solution.py:2460
  8.7 4.3 copy-start.1
  8.7 4.3 copy-start.2
  8.7 544.5 %reduce-scatter.2.cloned.1.call-start = ((), (), s32[]{:S(2)}) async-start(), calls=%async_computation.3 | async-start | bytes 10485760 | tf_op jit(solution)/shard_map/reduce_scatter | solution.py:2515
  88.7 0.7 copy-start.5
  89.4 0.7 copy-start.6
  90.1 1.8 copy-start
  288.7 53.5 %copy-start.7 = (f32[128,2048]{1,0:T(8,128)S(1)}, f32[128,2048]{1,0:T(8,128)}, u32[]{:S(2)}) copy-start(f32[128,2048]{1,0:T(8,128)} %get-tuple-element.53) | copy-start | bytes 3145732
  288.7 53.7 %copy-start.16 = (f32[128,128]{1,0:T(8,128)S(1)}, f32[128,128]{1,0:T(8,128)}, u32[]{:S(2)}) copy-start(f32[128,128]{1,0:T(8,128)} %get-tuple-element.60) | copy-start | bytes 196612
  288.8 53.9 %copy-start.17 = (f32[2048]{0:T(1024)S(1)}, f32[2048]{0:T(1024)}, u32[]{:S(2)}) copy-start(f32[2048]{0:T(1024)} %get-tuple-element.88) | copy-start | bytes 24580
  340.6 5.3 copy-start.15
  399.7 63.2 %copy-start.3 = (f32[2048]{0:T(1024)S(1)}, f32[2048]{0:T(1024)}, u32[]{:S(2)}) copy-start(f32[2048]{0:T(1024)} %get-tuple-element.89) | copy-start | bytes 24580
  462.9 0.7 copy-start.4
  463.7 67.3 %copy-start.22 = (bf16[64,2048]{1,0:T(8,128)(2,1)S(1)}, bf16[64,2048]{1,0:T(8,128)(2,1)}, u32[]{:S(2)}) copy-start(bf16[64,2048]{1,0:T(8,128)(2,1)} %get-tuple-element.79) | copy-start | bytes 786436
  463.7 72.3 %copy-start.11 = (bf16[256,2048]{1,0:T(8,128)(2,1)S(1)}, bf16[256,2048]{1,0:T(8,128)(2,1)}, u32[]{:S(2)}) copy-start(bf16[256,2048]{1,0:T(8,128)(2,1)} %get-tuple-element.81) | copy-start | bytes 3145732
  463.7 72.3 %copy-start.12 = (bf16[256,2048]{1,0:T(8,128)(2,1)S(1)}, bf16[256,2048]{1,0:T(8,128)(2,1)}, u32[]{:S(2)}) copy-start(bf16[256,2048]{1,0:T(8,128)(2,1)} %get-tuple-element.82) | copy-start | bytes 3145732
  463.7 72.3 %copy-start.13 = (bf16[256,2048]{1,0:T(8,128)(2,1)S(1)}, bf16[256,2048]{1,0:T(8,128)(2,1)}, u32[]{:S(2)}) copy-start(bf16[256,2048]{1,0:T(8,128)(2,1)} %get-tuple-element.83) | copy-start | bytes 3145732
  530.9 21.4 %collective-permute-start = (bf16[64,2048]{1,0:T(8,128)(2,1)S(1)}, bf16[64,2048]{1,0:T(8,128)(2,1)S(1)}, u32[]{:S(2)}, u32[]{:S(2)}) collective-permute-start(bf16[64,2048]{1,0:T(8,128)(2,1)S(1)} %copy-done.22), channel_id=1, source_target_pairs={{0,0},{1,4},{2,8},{3,12},{4,16},{5,20},{6,24},{7,28},{8,1},{9,5},{... | collective-permute-start | bytes 786440 | tf_op jit(solution)/shard_map/ppermute | solution.py:2571
  535.9 2.2 copy-start.9
  538.1 5.2 copy-start.8
  538.1 5.2 copy-start.10
Sparse Core Ops, SparseCore 0:
  9.6 83.3 all-gather.4
  94.5 103.2 all-gather.2
  287.1 76.4 reduce-scatter.1

commit v7 on v6

--- a/solution.py
+++ b/solution.py
@@ -1190,8 +1190,8 @@
     tok_rows, width = cotangent.shape
     local_experts, ff = first.shape[0], second.shape[0] // first.shape[0]
     rows = tok_rows * n
-    pair = 2 * tok_rows
-    part = 4 * tok_rows
+    group = 4
+    pair = part = group * tok_rows
     tile, wide = TILE, WIDE
     bf16, f32 = jnp.bfloat16, jnp.float32
     offsets = slot_offsets(n)
@@ -1219,7 +1219,6 @@
         mixed_s,
         back_s,
         attend_s,
-        token_s,
         residual_s,
         gate_s,
         sum_s,
@@ -1232,7 +1231,6 @@
     ):
         ring = Ring(n)
         lanes = lax.broadcasted_iota(jnp.int32, (pair, LANES), 1)
-        part_lanes = lax.broadcasted_iota(jnp.int32, (part, LANES), 1)
         loads = [pltpu.make_async_copy(out_ref, out_s, weight_load.at[0])]
         for x in range(local_experts):
             loads.append(pltpu.make_async_copy(first_ref.at[x], first_s.at[x], weight_load.at[1 + x]))
@@ -1240,16 +1238,20 @@
 
         def row_loads(j):
             copies = []
-            for k in range(2):
-                device = ring.at(offsets[2 * j + k])
+            for k in range(group):
+                device = ring.at(offsets[group * j + k])
                 source = pl.ds(pl.multiple_of(device * tok_rows, 16), tok_rows)
                 target = pl.ds(k * tok_rows, tok_rows)
-                for at, (array, held) in enumerate(((attend_ref, attend_s), (token_ref, token_s))):
-                    copies.append(
-                        pltpu.make_async_copy(
-                            array.at[source], held.at[j % 2, target], load.at[j % 2, k, at]
-                        )
+                copies.append(
+                    pltpu.make_async_copy(
+                        attend_ref.at[source], attend_s.at[j % 2, target], load.at[j % 2, k, 0]
                     )
+                )
+                copies.append(
+                    pltpu.make_async_copy(
+                        token_ref.at[source], mixed_s.at[group * j + k], load.at[j % 2, k, 1]
+                    )
+                )
             return copies
 
         pending = row_loads(0)
@@ -1266,34 +1268,34 @@
             copy.start()
 
         saves = []
-        for j in range(n // 2):
+        for j in range(n // group):
             for copy in pending:
                 copy.wait()
-            if j + 1 < n // 2:
+            if j + 1 < n // group:
                 pending = row_loads(j + 1)
                 for copy in pending:
                     copy.start()
 
             def project(t, carry, j=j):
                 columns = pl.ds(pl.multiple_of(t * wide, wide), wide)
-                residual_s[:, columns] = token_s[j % 2, :, columns].astype(f32) + dot(
-                    attend_s[j % 2], out_s[:, columns]
-                )
+                values = mixed_s[pl.ds(group * j, group), :, columns].reshape(pair, wide)
+                residual_s[:, columns] = values.astype(f32) + dot(attend_s[j % 2], out_s[:, columns])
                 return carry
 
             lax.fori_loop(0, width // wide, project, 0)
+            advance(steps, 2)
             residual = residual_s[...]
             if j == 0:
                 own_residual[...] = residual[:tok_rows]
             inverse = lax.rsqrt(jnp.mean(residual * residual, axis=-1, keepdims=True) + EPSILON)
             mixed = (residual * inverse * gain_ref[0:1, :]).astype(bf16)
-            for k in range(2):
-                mixed_s[2 * j + k] = mixed[k * tok_rows : (k + 1) * tok_rows]
+            for k in range(group):
+                mixed_s[group * j + k] = mixed[k * tok_rows : (k + 1) * tok_rows]
             logits = dot(mixed, router_ref[...])
             marks = jnp.concatenate(
                 [
-                    named_ref[pl.ds(pl.multiple_of(ring.at(offsets[2 * j + k]) * tok_rows, 16), tok_rows)]
-                    for k in range(2)
+                    named_ref[pl.ds(pl.multiple_of(ring.at(offsets[group * j + k]) * tok_rows, 16), tok_rows)]
+                    for k in range(group)
                 ],
                 axis=0,
             ).astype(f32)
@@ -1313,7 +1315,7 @@
             gate_s[pl.ds(j * pair, pair)] = held
             saves.append(
                 pltpu.make_async_copy(
-                    mixed_s.at[pl.ds(2 * j, 2)], mixed_all.at[pl.ds(2 * j, 2)], save.at[j]
+                    mixed_s.at[pl.ds(group * j, group)], mixed_all.at[pl.ds(group * j, group)], save.at[j]
                 )
             )
             saves[-1].start()
@@ -1323,7 +1325,7 @@
         outgoing = []
         base = n // 2
         for s in range(counts):
-            slots = pl.ds(s * 4, 4)
+            slots = pl.ds(s * group, group)
             part_rows = pl.ds(s * part, part)
             advance(steps, 0 if s < counts - 1 else 64)
             if s == 0:
@@ -1355,7 +1357,7 @@
                         value * gate
                     ).astype(bf16)
                     sums = jnp.sum(value * hidden_back, axis=-1, keepdims=True)
-                    sum_s[part_rows] = sum_s[part_rows] + jnp.where(part_lanes == x, sums, 0.0)
+                    sum_s[part_rows] = sum_s[part_rows] + jnp.where(lanes == x, sums, 0.0)
                     hidden_back = hidden_back * gate
                     slope = sigmoid * (1.0 + gate_part * (1.0 - sigmoid))
                     up_rows = pl.ds((1 + x) * part, part)
@@ -1410,13 +1412,12 @@
             pltpu.VMEM((n, tok_rows, width), bf16),
             pltpu.VMEM((n, tok_rows, width), bf16),
             pltpu.VMEM((2, pair, width), bf16),
-            pltpu.VMEM((2, pair, width), bf16),
             pltpu.VMEM((pair, width), f32),
             pltpu.VMEM((rows, LANES), f32),
             pltpu.VMEM((rows, LANES), f32),
             sems(2, 2, n // 2),
             sems(2, 2, n // 2),
-            sems(2, 2, 2),
+            sems(2, group, 2),
             sems(2 + local_experts),
             sems(n // 2 + 1 + local_experts),
             pltpu.SemaphoreType.DMA,

time: 572 us -> 571 us (level)
  no operation moved by 1% of the time
where the time goes in v7:
time: 571 us; the launch traced here: 564 us
  Pallas kernels  479 us (84%)
  local copies, waits for them, and re-layouts  19.3 us (3%)
  other arithmetic  18.7 us (3%)
  matrix products  17.5 us (3%)
  between operations  14.7 us (3%)
  waiting for transfers between devices  9.13 us (2%)
  starting transfers between devices  5.83 us (1%)
    pallas_call x1, Pallas kernels, attention_in(): pl.pallas_call(body, out_shape=(jax.ShapeDtypeStruct((rows, width), bf16)...  106 us
    pallas_call x1, Pallas kernels, gather_inputs(): kernel_call(body, (jax.ShapeDtypeStruct((tok_rows * n, width), tokens.dty...  75.7 us
    pallas_call x1, Pallas kernels, scatter_end(): kernel_call(body, (jax.ShapeDtypeStruct((rows, width), bf16), jax.ShapeDt...  64.8 us
    pallas_call x1, Pallas kernels, experts_in(): pl.pallas_call(body, out_shape=(jax.ShapeDtypeStruct((n, tok_rows, width)...  64.6 us
    pallas_call x1, Pallas kernels, attention_back(): pl.pallas_call(body, out_shape=(jax.ShapeDtypeStruct((rows, 3 * cols), bf...  62.8 us
    pallas_call x1, Pallas kernels, gather_with_gradients(): pl.pallas_call(body, out_shape=(jax.ShapeDtypeStruct((rows * n, width), b...  54.7 us
    pallas_call x1, Pallas kernels, experts_out(): pl.pallas_call(body, out_shape=(jax.ShapeDtypeStruct((tok_rows, width), f...  50.8 us
    dot_general x1, matrix products, heads_local(): jnp.einsum('tf,td->fd', gated_all, upstream_all.reshape(rows, width), pre...  14.2 us
  transfers between devices with their start and end apart: 4, of which 1 were waited for; matrix products, arithmetic and copies ran while one was open for 5% of the time, Pallas kernels for 73%

profile of v7, /device:TPU:1, one launch (start us, length us, event | category | flops | bytes accessed | tf_op | source)
XLA Modules:
  0.0 564.0 jit_solution(13041020698578511558)
XLA Ops:
  8.0 0.7 all-gather.3.cloned.1.call-update
  11.7 0.9 reshape.167
  13.0 75.7 %gather_inputs.1 = (bf16[1024,2048]{1,0:T(8,128)(2,1)}, bf16[8,128,128]{2,1,0:T(8,128)(2,1)S(1)}, bf16[4,8,64,896]{3,2,1,0:T(8,128)(2,1)S(1)}, bf16[64,2048]{1,0:T(8,128)(2,1)S(1)}) custom-call(bf16[128,2048]{1,0:T(8,128)(2,1)S(1)} %bitcast.87, bf16[128,128]{1,0:T(8,128)(2,1)S(1)} %convert_element_type.46.named_ref, ...), custom_call_target="tpu_custom_call" | custom-call | bytes 200000000 | tf_op jit(solution)/shard_map/gather_inputs/pallas_call | solution.py:816
  89.4 0.7 copy-done.6
  90.1 1.8 copy-done
  92.0 0.8 slice.130.router_ref
  92.8 1.2 slice_convert_fusion
  95.0 1.0 copy.73.bound_ref
  96.1 1.9 fusion.6
  98.0 1.3 pad_maximum_fusion.2
  99.3 1.5 slice_reduce_fusion
  100.8 105.5 %attention_in.1 = (bf16[1024,2048]{1,0:T(8,128)(2,1)}, bf16[2048,2048]{1,0:T(8,128)(2,1)}, bf16[2,1024,1024]{2,1,0:T(8,128)(2,1)}, bf16[1024,2048]{1,0:T(8,128)(...) custom-call(bf16[1024,2048]{1,0:T(8,128)(2,1)} %get-tuple-element.47.to, ...), custom_call_target="tpu_custom_call" | custom-call | flops 3221225472 | bytes 200000000 | tf_op jit(solution)/shard_map/attention_in/pallas_call | solution.py:1913
  206.3 64.6 %experts_in.1 = (bf16[8,128,2048]{2,1,0:T(8,128)(2,1)}, bf16[8,128,2048]{2,1,0:T(8,128)(2,1)}, bf16[1024,2048]{1,0:T(8,128)(2,1)}, bf16[2,1024,2048]{2,1,0:T(8,1...) custom-call(bf16[1024,2048]{1,0:T(8,128)(2,1)} %get-tuple-element.50.attend_ref, ...), custom_call_target="tpu_custom_call" | custom-call | flops 34359738368 | bytes 60000000 | tf_op jit(solution)/shard_map/experts_in/pallas_call | solution.py:1395
  270.9 14.2 %convolution_convert_fusion = bf16[2048,2048]{1,0:T(8,128)(2,1)} fusion(bf16[1024,2048]{1,0:T(8,128)(2,1)} %get-tuple-element.54.gated_ref, bf16[1024,2048]{1,0:T(8,128)(2,1)} %bitcast.120), kind=kOutput, calls=%fused_computation.1 | convolution fusion | flops 8594128896 | bytes 16777216 | tf_op jit(solution)/shard_map/tf,td->fd/dot_general | solution.py:2512
  286.9 50.8 %experts_out.1 = (f32[128,2048]{1,0:T(8,128)}, bf16[1024,2048]{1,0:T(8,128)(2,1)}, f32[8,8,128]{2,1,0:T(8,128)}) custom-call(bf16[2,1024,2048]{2,1,0:T(8,128)(2,1)} %get-tuple-element.57.up_ref, bf16[1024,2048]{1,0:T(8,128)(2,1)} %get-tuple-element.54.gated_ref, bf16[2,2048,2048]{2,1,0:T(8,128)(2,1)} %all-gather.3.cloned.1.call-done.first_ref, ...), custom_call_target="tpu_custom_call" | custom-call | flops 25769803776 | bytes 60000000 | tf_op jit(solution)/shard_map/experts_out/pallas_call | solution.py:1642
  337.8 0.8 slice_bitcast_fusion.7
  339.8 2.1 multiply_reduce_fusion
  341.9 1.3 fusion.2
  343.2 1.2 fusion.10
  344.3 54.7 %gather_with_gradients.1 = (bf16[1024,2048]{1,0:T(8,128)(2,1)}, bf16[2,512,2048]{2,1,0:T(8,128)(2,1)}, bf16[2,512,2048]{2,1,0:T(8,128)(2,1)}, bf16[256,2048]{1,0:T(8,128)(2,1)}) custom-call(bf16[128,2048]{1,0:T(8,128)(2,1)} %get-tuple-element.90.block_ref, bf16[1024,2048]{1,0:T(8,128)(2,1)} %bitcast.100, bf16[2,1024,2048]{2,1,0:T(8,128)(2,1)} %get-tuple-element.57.up_ref), custom_call_target="tpu_custom_call" | custom-call | flops 17179869184 | bytes 160000000 | tf_op jit(solution)/shard_map/gather_with_gradients/pallas_call | solution.py:2069
  399.0 62.8 %attention_back.1 = (bf16[1024,768]{1,0:T(8,128)(2,1)}, bf16[1024,2048]{1,0:T(8,128)(2,1)}, f32[8,512]{1,0:T(8,128)}, f32[128,2048]{1,0:T(8,128)}, bf16[64,2048]...) custom-call(bf16[1024,2048]{1,0:T(8,128)(2,1)} %get-tuple-element.63.back_ref, ...), custom_call_target="tpu_custom_call" | custom-call | flops 4294967296 | bytes 160000000 | tf_op jit(solution)/shard_map/attention_back/pallas_call | solution.py:2351
  461.9 0.7 copy-done.4
  462.6 64.8 %scatter_end.1 = (bf16[128,2048]{1,0:T(8,128)(2,1)S(1)}, f32[64,6144]{1,0:T(8,128)S(1)}, f32[24,128]{1,0:T(8,128)S(1)}, bf16[256,2048]{1,0:T(8,128)(2,1)S(1)}) custom-call(bf16[1024,2048]{1,0:T(8,128)(2,1)} %get-tuple-element.72.row_ref, bf16[1024,2048]{1,0:T(8,128)(2,1)} %get-tuple-element.73.attend_ref, bf16[1024,768]{1,0:T(8,128)(2,1)} %get-tuple-element.74.raw_ref, ...), custom_call_target="tpu_custom_call" | custom-call | bytes 200000000 | tf_op jit(solution)/shard_map/scatter_end/pallas_call | solution.py:1085
  528.7 5.7 %collective-permute-start = (bf16[64,2048]{1,0:T(8,128)(2,1)S(1)}, bf16[64,2048]{1,0:T(8,128)(2,1)S(1)}, u32[]{:S(2)}, u32[]{:S(2)}) collective-permute-start(bf16[64,2048]{1,0:T(8,128)(2,1)S(1)} %copy-done.22), channel_id=1, source_target_pairs={{0,0},{1,4},{2,8},{3,12},{4,16},{5,20},{6,24},{7,28},{8,1},{9,5},{... | collective-permute-start | bytes 786440 | tf_op jit(solution)/shard_map/ppermute | solution.py:2572
  534.9 1.8 copy-done.9
  536.6 5.2 convert_add_fusion
  541.8 0.9 fusion
  542.7 7.7 %collective-permute-done = bf16[64,2048]{1,0:T(8,128)(2,1)S(1)} collective-permute-done((bf16[64,2048]{1,0:T(8,128)(2,1)S(1)}, bf16[64,2048]{1,0:T(8,128)(2,1)S(1)}, u32[]{:S(2)}, u32[]{:S(2)}) %collective-permute-start) | collective-permute-done | bytes 262176 | tf_op jit(solution)/shard_map/ppermute | solution.py:2572
  550.4 0.8 convert_element_type.55
  551.3 4.1 convert_element_type.59
  555.4 0.8 copy.88
  556.2 1.1 copy.89
  (140 shorter events, 10.2 us)
Async XLA Ops:
  7.2 1.6 copy-start.18
  7.2 3.4 copy-start.19
  7.2 3.7 copy-start.21
  7.2 3.8 copy-start.20
  7.2 3.9 copy-start.14
  7.2 199.1 %all-gather.5.cloned.1.call-start = ((), (), s32[]{:S(2)}) async-start(), calls=%async_computation.2 | async-start | bytes 10485760 | tf_op jit(solution)/shard_map/all_gather | solution.py:2462
  8.0 198.4 %all-gather.3.cloned.1.call-start = ((), (), s32[]{:S(2)}) async-start(), calls=%async_computation.1 | async-start | bytes 20971520 | tf_op jit(solution)/shard_map/all_gather | solution.py:2461
  8.7 4.3 copy-start.1
  8.7 4.3 copy-start.2
  8.7 542.5 %reduce-scatter.2.cloned.1.call-start = ((), (), s32[]{:S(2)}) async-start(), calls=%async_computation.3 | async-start | bytes 10485760 | tf_op jit(solution)/shard_map/reduce_scatter | solution.py:2516
  88.7 0.7 copy-start.5
  89.4 0.7 copy-start.6
  90.1 1.8 copy-start
  286.9 52.5 %copy-start.7 = (f32[128,2048]{1,0:T(8,128)S(1)}, f32[128,2048]{1,0:T(8,128)}, u32[]{:S(2)}) copy-start(f32[128,2048]{1,0:T(8,128)} %get-tuple-element.53) | copy-start | bytes 3145732
  286.9 52.7 %copy-start.16 = (f32[128,128]{1,0:T(8,128)S(1)}, f32[128,128]{1,0:T(8,128)}, u32[]{:S(2)}) copy-start(f32[128,128]{1,0:T(8,128)} %get-tuple-element.60) | copy-start | bytes 196612
  286.9 52.9 %copy-start.17 = (f32[2048]{0:T(1024)S(1)}, f32[2048]{0:T(1024)}, u32[]{:S(2)}) copy-start(f32[2048]{0:T(1024)} %get-tuple-element.88) | copy-start | bytes 24580
  337.8 5.4 copy-start.15
  399.0 62.9 %copy-start.3 = (f32[2048]{0:T(1024)S(1)}, f32[2048]{0:T(1024)}, u32[]{:S(2)}) copy-start(f32[2048]{0:T(1024)} %get-tuple-element.89) | copy-start | bytes 24580
  461.9 0.7 copy-start.4
  462.6 66.1 %copy-start.22 = (bf16[64,2048]{1,0:T(8,128)(2,1)S(1)}, bf16[64,2048]{1,0:T(8,128)(2,1)}, u32[]{:S(2)}) copy-start(bf16[64,2048]{1,0:T(8,128)(2,1)} %get-tuple-element.79) | copy-start | bytes 786436
  462.6 71.8 %copy-start.11 = (bf16[256,2048]{1,0:T(8,128)(2,1)S(1)}, bf16[256,2048]{1,0:T(8,128)(2,1)}, u32[]{:S(2)}) copy-start(bf16[256,2048]{1,0:T(8,128)(2,1)} %get-tuple-element.81) | copy-start | bytes 3145732
  462.6 71.8 %copy-start.12 = (bf16[256,2048]{1,0:T(8,128)(2,1)S(1)}, bf16[256,2048]{1,0:T(8,128)(2,1)}, u32[]{:S(2)}) copy-start(bf16[256,2048]{1,0:T(8,128)(2,1)} %get-tuple-element.82) | copy-start | bytes 3145732
  462.6 71.8 %copy-start.13 = (bf16[256,2048]{1,0:T(8,128)(2,1)S(1)}, bf16[256,2048]{1,0:T(8,128)(2,1)}, u32[]{:S(2)}) copy-start(bf16[256,2048]{1,0:T(8,128)(2,1)} %get-tuple-element.83) | copy-start | bytes 3145732
  528.7 21.7 %collective-permute-start = (bf16[64,2048]{1,0:T(8,128)(2,1)S(1)}, bf16[64,2048]{1,0:T(8,128)(2,1)S(1)}, u32[]{:S(2)}, u32[]{:S(2)}) collective-permute-start(bf16[64,2048]{1,0:T(8,128)(2,1)S(1)} %copy-done.22), channel_id=1, source_target_pairs={{0,0},{1,4},{2,8},{3,12},{4,16},{5,20},{6,24},{7,28},{8,1},{9,5},{... | collective-permute-start | bytes 786440 | tf_op jit(solution)/shard_map/ppermute | solution.py:2572
  534.5 2.2 copy-start.9
  536.6 5.2 copy-start.8
  536.6 5.2 copy-start.10
Sparse Core Ops, SparseCore 0:
  9.6 83.3 all-gather.4
  94.5 103.2 all-gather.2
  285.3 77.5 reduce-scatter.1

commit v8 on v7

--- a/solution.py
+++ b/solution.py
@@ -2225,11 +2225,11 @@
         advance(steps, 1)
         lanes = lax.broadcasted_iota(jnp.int32, (chunk, LANES), 1)
 
-        def chunks(step, count=2):
+        def chunks(step, count=1):
             total = rows // chunk
             for first in range(0, total, count):
                 lax.fori_loop(first, min(first + count, total), step, 0)
-                advance(steps, 2)
+                advance(steps, 1)
 
         loads[1].wait()
 

time: 571 us -> 565 us (0.989)
  Pallas kernels: 479 us -> 470 us
    pallas_call x1, Pallas kernels: 106 us -> 97 us  [attention_in(): pl.pallas_call(body, out_shape=(jax.ShapeDtypeStruct((rows, width), bf16)...]
where the time goes in v8:
time: 565 us; the launch traced here: 555 us
  Pallas kernels  470 us (83%)
  local copies, waits for them, and re-layouts  19.3 us (3%)
  other arithmetic  18.7 us (3%)
  matrix products  17.4 us (3%)
  between operations  14.7 us (3%)
  waiting for transfers between devices  9.11 us (2%)
    pallas_call x1, Pallas kernels, attention_in(): pl.pallas_call(body, out_shape=(jax.ShapeDtypeStruct((rows, width), bf16)...  97 us
    pallas_call x1, Pallas kernels, gather_inputs(): kernel_call(body, (jax.ShapeDtypeStruct((tok_rows * n, width), tokens.dty...  75.7 us
    pallas_call x1, Pallas kernels, experts_in(): pl.pallas_call(body, out_shape=(jax.ShapeDtypeStruct((n, tok_rows, width)...  66.1 us
    pallas_call x1, Pallas kernels, attention_back(): pl.pallas_call(body, out_shape=(jax.ShapeDtypeStruct((rows, 3 * cols), bf...  63.8 us
    pallas_call x1, Pallas kernels, scatter_end(): kernel_call(body, (jax.ShapeDtypeStruct((rows, width), bf16), jax.ShapeDt...  63.6 us
    pallas_call x1, Pallas kernels, gather_with_gradients(): pl.pallas_call(body, out_shape=(jax.ShapeDtypeStruct((rows * n, width), b...  52.7 us
    pallas_call x1, Pallas kernels, experts_out(): pl.pallas_call(body, out_shape=(jax.ShapeDtypeStruct((tok_rows, width), f...  51.3 us
    dot_general x1, matrix products, heads_local(): jnp.einsum('tf,td->fd', gated_all, upstream_all.reshape(rows, width), pre...  14.2 us
  transfers between devices with their start and end apart: 4, of which 1 were waited for; matrix products, arithmetic and copies ran while one was open for 5% of the time, Pallas kernels for 73%

profile of v8, /device:TPU:1, one launch (start us, length us, event | category | flops | bytes accessed | tf_op | source)
XLA Modules:
  0.0 555.0 jit_solution(15474201517195468309)
XLA Ops:
  8.0 0.7 all-gather.3.cloned.1.call-update
  11.7 0.9 reshape.167
  13.0 75.7 %gather_inputs.1 = (bf16[1024,2048]{1,0:T(8,128)(2,1)}, bf16[8,128,128]{2,1,0:T(8,128)(2,1)S(1)}, bf16[4,8,64,896]{3,2,1,0:T(8,128)(2,1)S(1)}, bf16[64,2048]{1,0:T(8,128)(2,1)S(1)}) custom-call(bf16[128,2048]{1,0:T(8,128)(2,1)S(1)} %bitcast.87, bf16[128,128]{1,0:T(8,128)(2,1)S(1)} %convert_element_type.46.named_ref, ...), custom_call_target="tpu_custom_call" | custom-call | bytes 200000000 | tf_op jit(solution)/shard_map/gather_inputs/pallas_call | solution.py:816
  89.4 0.7 copy-done.6
  90.1 1.8 copy-done
  92.0 0.8 slice.130.router_ref
  92.8 1.2 slice_convert_fusion
  95.0 1.0 copy.73.bound_ref
  96.1 1.9 fusion.6
  98.0 1.3 pad_maximum_fusion.2
  99.3 1.5 slice_reduce_fusion
  100.8 97.0 %attention_in.1 = (bf16[1024,2048]{1,0:T(8,128)(2,1)}, bf16[2048,2048]{1,0:T(8,128)(2,1)}, bf16[2,1024,1024]{2,1,0:T(8,128)(2,1)}, bf16[1024,2048]{1,0:T(8,128)(...) custom-call(bf16[1024,2048]{1,0:T(8,128)(2,1)} %get-tuple-element.47.to, ...), custom_call_target="tpu_custom_call" | custom-call | flops 3221225472 | bytes 200000000 | tf_op jit(solution)/shard_map/attention_in/pallas_call | solution.py:1913
  197.9 66.1 %experts_in.1 = (bf16[8,128,2048]{2,1,0:T(8,128)(2,1)}, bf16[8,128,2048]{2,1,0:T(8,128)(2,1)}, bf16[1024,2048]{1,0:T(8,128)(2,1)}, bf16[2,1024,2048]{2,1,0:T(8,1...) custom-call(bf16[1024,2048]{1,0:T(8,128)(2,1)} %get-tuple-element.50.attend_ref, ...), custom_call_target="tpu_custom_call" | custom-call | flops 34359738368 | bytes 60000000 | tf_op jit(solution)/shard_map/experts_in/pallas_call | solution.py:1395
  264.0 14.2 %convolution_convert_fusion = bf16[2048,2048]{1,0:T(8,128)(2,1)} fusion(bf16[1024,2048]{1,0:T(8,128)(2,1)} %get-tuple-element.54.gated_ref, bf16[1024,2048]{1,0:T(8,128)(2,1)} %bitcast.120), kind=kOutput, calls=%fused_computation.1 | convolution fusion | flops 8594128896 | bytes 16777216 | tf_op jit(solution)/shard_map/tf,td->fd/dot_general | solution.py:2512
  280.0 51.3 %experts_out.1 = (f32[128,2048]{1,0:T(8,128)}, bf16[1024,2048]{1,0:T(8,128)(2,1)}, f32[8,8,128]{2,1,0:T(8,128)}) custom-call(bf16[2,1024,2048]{2,1,0:T(8,128)(2,1)} %get-tuple-element.57.up_ref, bf16[1024,2048]{1,0:T(8,128)(2,1)} %get-tuple-element.54.gated_ref, bf16[2,2048,2048]{2,1,0:T(8,128)(2,1)} %all-gather.3.cloned.1.call-done.first_ref, ...), custom_call_target="tpu_custom_call" | custom-call | flops 25769803776 | bytes 60000000 | tf_op jit(solution)/shard_map/experts_out/pallas_call | solution.py:1642
  331.3 0.8 slice_bitcast_fusion.7
  333.3 1.9 multiply_reduce_fusion
  335.2 1.3 fusion.2
  336.5 1.2 fusion.10
  337.7 52.7 %gather_with_gradients.1 = (bf16[1024,2048]{1,0:T(8,128)(2,1)}, bf16[2,512,2048]{2,1,0:T(8,128)(2,1)}, bf16[2,512,2048]{2,1,0:T(8,128)(2,1)}, bf16[256,2048]{1,0:T(8,128)(2,1)}) custom-call(bf16[128,2048]{1,0:T(8,128)(2,1)} %get-tuple-element.90.block_ref, bf16[1024,2048]{1,0:T(8,128)(2,1)} %bitcast.100, bf16[2,1024,2048]{2,1,0:T(8,128)(2,1)} %get-tuple-element.57.up_ref), custom_call_target="tpu_custom_call" | custom-call | flops 17179869184 | bytes 160000000 | tf_op jit(solution)/shard_map/gather_with_gradients/pallas_call | solution.py:2069
  390.4 63.8 %attention_back.1 = (bf16[1024,768]{1,0:T(8,128)(2,1)}, bf16[1024,2048]{1,0:T(8,128)(2,1)}, f32[8,512]{1,0:T(8,128)}, f32[128,2048]{1,0:T(8,128)}, bf16[64,2048]...) custom-call(bf16[1024,2048]{1,0:T(8,128)(2,1)} %get-tuple-element.63.back_ref, ...), custom_call_target="tpu_custom_call" | custom-call | flops 4294967296 | bytes 160000000 | tf_op jit(solution)/shard_map/attention_back/pallas_call | solution.py:2351
  454.4 0.7 copy-done.4
  455.1 63.6 %scatter_end.1 = (bf16[128,2048]{1,0:T(8,128)(2,1)S(1)}, f32[64,6144]{1,0:T(8,128)S(1)}, f32[24,128]{1,0:T(8,128)S(1)}, bf16[256,2048]{1,0:T(8,128)(2,1)S(1)}) custom-call(bf16[1024,2048]{1,0:T(8,128)(2,1)} %get-tuple-element.72.row_ref, bf16[1024,2048]{1,0:T(8,128)(2,1)} %get-tuple-element.73.attend_ref, bf16[1024,768]{1,0:T(8,128)(2,1)} %get-tuple-element.74.raw_ref, ...), custom_call_target="tpu_custom_call" | custom-call | bytes 200000000 | tf_op jit(solution)/shard_map/scatter_end/pallas_call | solution.py:1085
  519.9 5.5 collective-permute-start
  525.8 1.8 copy-done.9
  527.6 5.2 convert_add_fusion
  532.8 0.9 fusion
  533.7 7.7 %collective-permute-done = bf16[64,2048]{1,0:T(8,128)(2,1)S(1)} collective-permute-done((bf16[64,2048]{1,0:T(8,128)(2,1)S(1)}, bf16[64,2048]{1,0:T(8,128)(2,1)S(1)}, u32[]{:S(2)}, u32[]{:S(2)}) %collective-permute-start) | collective-permute-done | bytes 262176 | tf_op jit(solution)/shard_map/ppermute | solution.py:2572
  541.4 0.8 convert_element_type.55
  542.2 4.1 convert_element_type.59
  546.3 0.8 copy.88
  547.1 1.1 copy.89
  (140 shorter events, 10.2 us)
Async XLA Ops:
  7.2 1.6 copy-start.18
  7.2 3.4 copy-start.19
  7.2 3.7 copy-start.21
  7.2 3.8 copy-start.20
  7.2 3.9 copy-start.14
  7.2 190.6 %all-gather.5.cloned.1.call-start = ((), (), s32[]{:S(2)}) async-start(), calls=%async_computation.2 | async-start | bytes 10485760 | tf_op jit(solution)/shard_map/all_gather | solution.py:2462
  8.0 189.9 %all-gather.3.cloned.1.call-start = ((), (), s32[]{:S(2)}) async-start(), calls=%async_computation.1 | async-start | bytes 20971520 | tf_op jit(solution)/shard_map/all_gather | solution.py:2461
  8.7 4.3 copy-start.1
  8.7 4.3 copy-start.2
  8.7 533.5 %reduce-scatter.2.cloned.1.call-start = ((), (), s32[]{:S(2)}) async-start(), calls=%async_computation.3 | async-start | bytes 10485760 | tf_op jit(solution)/shard_map/reduce_scatter | solution.py:2516
  88.7 0.7 copy-start.5
  89.4 0.7 copy-start.6
  90.1 1.8 copy-start
  279.9 53.0 %copy-start.7 = (f32[128,2048]{1,0:T(8,128)S(1)}, f32[128,2048]{1,0:T(8,128)}, u32[]{:S(2)}) copy-start(f32[128,2048]{1,0:T(8,128)} %get-tuple-element.53) | copy-start | bytes 3145732
  279.9 53.1 %copy-start.16 = (f32[128,128]{1,0:T(8,128)S(1)}, f32[128,128]{1,0:T(8,128)}, u32[]{:S(2)}) copy-start(f32[128,128]{1,0:T(8,128)} %get-tuple-element.60) | copy-start | bytes 196612
  280.0 53.4 %copy-start.17 = (f32[2048]{0:T(1024)S(1)}, f32[2048]{0:T(1024)}, u32[]{:S(2)}) copy-start(f32[2048]{0:T(1024)} %get-tuple-element.88) | copy-start | bytes 24580
  331.2 5.3 copy-start.15
  390.4 63.9 %copy-start.3 = (f32[2048]{0:T(1024)S(1)}, f32[2048]{0:T(1024)}, u32[]{:S(2)}) copy-start(f32[2048]{0:T(1024)} %get-tuple-element.89) | copy-start | bytes 24580
  454.3 0.7 copy-start.4
  455.1 64.8 %copy-start.22 = (bf16[64,2048]{1,0:T(8,128)(2,1)S(1)}, bf16[64,2048]{1,0:T(8,128)(2,1)}, u32[]{:S(2)}) copy-start(bf16[64,2048]{1,0:T(8,128)(2,1)} %get-tuple-element.79) | copy-start | bytes 786436
  455.1 70.3 %copy-start.11 = (bf16[256,2048]{1,0:T(8,128)(2,1)S(1)}, bf16[256,2048]{1,0:T(8,128)(2,1)}, u32[]{:S(2)}) copy-start(bf16[256,2048]{1,0:T(8,128)(2,1)} %get-tuple-element.81) | copy-start | bytes 3145732
  455.1 70.3 %copy-start.12 = (bf16[256,2048]{1,0:T(8,128)(2,1)S(1)}, bf16[256,2048]{1,0:T(8,128)(2,1)}, u32[]{:S(2)}) copy-start(bf16[256,2048]{1,0:T(8,128)(2,1)} %get-tuple-element.82) | copy-start | bytes 3145732
  455.1 70.3 %copy-start.13 = (bf16[256,2048]{1,0:T(8,128)(2,1)S(1)}, bf16[256,2048]{1,0:T(8,128)(2,1)}, u32[]{:S(2)}) copy-start(bf16[256,2048]{1,0:T(8,128)(2,1)} %get-tuple-element.83) | copy-start | bytes 3145732
  519.9 21.5 %collective-permute-start = (bf16[64,2048]{1,0:T(8,128)(2,1)S(1)}, bf16[64,2048]{1,0:T(8,128)(2,1)S(1)}, u32[]{:S(2)}, u32[]{:S(2)}) collective-permute-start(bf16[64,2048]{1,0:T(8,128)(2,1)S(1)} %copy-done.22), channel_id=1, source_target_pairs={{0,0},{1,4},{2,8},{3,12},{4,16},{5,20},{6,24},{7,28},{8,1},{9,5},{... | collective-permute-start | bytes 786440 | tf_op jit(solution)/shard_map/ppermute | solution.py:2572
  525.4 2.2 copy-start.9
  527.6 5.2 copy-start.8
  527.6 5.2 copy-start.10
Sparse Core Ops, SparseCore 0:
  9.6 83.3 all-gather.4
  94.5 103.2 all-gather.2
  278.3 75.5 reduce-scatter.1
